TPU v7x, 256 devices: a whole 4x4x8 slice. The times are simulated.
256 devices in a mesh: row: 8 (over x, core), col: 32 (over y, z).
Axes of the slice: x: 4, y: 4, z: 8, core: 2. Of those that a mesh axis runs over, the one named last changes fastest.
Arguments:
- covariance: float32 [8, 2048, 2, 8192], P(None, 'row', None, 'col'), may hold values from 0 to 5, as said below
Outputs:
- factored: float32 [8, 2048, 2, 8192], P(None, 'row', None, 'col')
Inputs may be any that keep to these rules, and one draw needn't show every extreme that they name: covariance is symmetric positive definite: s_a s_b m(d_ab) plus a positive nugget on the diagonal, where m is the Matern 3/2 kernel of the distance d_ab between two units' feature points.
All inputs are finite; a program needn't handle non-finite values.
Results may differ from a plain program's by a relative error of at most 0.0001.
Values sent between devices are 32-bit elements; how exact they have to be, the bound alone decides.
No kernel may reach another device: no remote copies, remote signals or barrier semaphores. Data moves between devices by JAX's collectives and lax.ppermute only.
A program may use at most 128 MiB of HBM per device.

v0:
```python
import jax
import jax.numpy as jnp
from jax import lax
from jax.sharding import PartitionSpec as P

STEPS = 3


def broadcast(x, axis, root):
    mine = lax.axis_index(axis) == root
    return lax.psum(jnp.where(mine, x, jnp.zeros_like(x)), axis)


def factorize(diag_block):
    factor = jnp.linalg.cholesky(diag_block)
    identity = jnp.eye(diag_block.shape[0], dtype=jnp.float32)
    inverted_factor = jax.scipy.linalg.solve_triangular(factor, identity, lower=True)
    return (factor, inverted_factor)


def solve_panel(block_grid, inverted_factor):
    return jnp.einsum("fsp,jp->fsj", block_grid, inverted_factor, precision=lax.Precision.HIGHEST)


def on_device(covariance):
    row_count = lax.axis_size("row")
    col_count = lax.axis_size("col")
    my_row = lax.axis_index("row")
    my_col = lax.axis_index("col")
    tile_rows = covariance.shape[0]
    width = covariance.shape[1]
    tile_cols = covariance.shape[2]
    global_rows = jnp.arange(tile_rows, dtype=jnp.int32) * row_count + my_row
    global_cols = jnp.arange(tile_cols, dtype=jnp.int32) * col_count + my_col
    covariance_matrix = covariance
    for step in range(STEPS):
        root_row = step % row_count
        slot_row = step // row_count
        root_col = step % col_count
        column_position = step // col_count
        owned = covariance_matrix[:, :, column_position, :]
        diag_block = broadcast(owned[slot_row], "row", root_row)
        factor, inverted_factor = factorize(diag_block)
        row_panel = broadcast(solve_panel(owned, inverted_factor), "col", root_col)
        grouped = row_panel.reshape(tile_cols, col_count // row_count, width, width)
        picked = lax.dynamic_index_in_dim(grouped, my_col // row_count, 1, keepdims=False)
        col_panel = broadcast(picked, "row", my_col % row_count)
        refreshed_block = covariance_matrix - jnp.einsum(
            "tab,ucb->tauc", row_panel, col_panel, precision=lax.Precision.HIGHEST
        )
        row_extent = global_rows[:, None, None, None]
        column_extent = global_cols[None, None, :, None]
        trail = (row_extent > step) & (column_extent > step) & (row_extent >= column_extent)
        result = jnp.where(trail, refreshed_block, covariance_matrix)
        result = jnp.where(
            (row_extent > step) & (column_extent == step), row_panel[:, :, None, :], result
        )
        result = jnp.where(
            (row_extent == step) & (column_extent == step), factor[None, :, None, :], result
        )
        covariance_matrix = result
    return covariance_matrix


def solution(mesh):
    in_specs = (P(None, "row", None, "col"),)
    out_specs = P(None, "row", None, "col")
    return jax.shard_map(
        on_device, mesh=mesh, in_specs=in_specs, out_specs=out_specs, check_vma=False
    )
```

profile of v0, /device:TPU:1, one launch (start us, length us, event | category | flops | bytes accessed | tf_op | source)
XLA Modules:
  0.0 1112.6 jit_solution(1199169605112612088)
XLA Ops:
  6.5 7.2 copy.47
  13.7 1.7 fusion.21
  15.5 66.7 %all-reduce.11.cloned.1.call-done = f32[256,256]{0,1:T(8,128)} async-done(((f32[256,256]{0,1:T(8,128)}), f32[256,256]{0,1:T(8,128)}) %all-reduce.11.cloned.1.call-update) | async-done | bytes 262160 | tf_op jit(solution)/shard_map/psum | solution.py:11
  82.2 1.1 copy.48
  83.2 1.0 fusion.30
  84.3 11.7 %cholesky.172 = f32[128,128]{1,0:T(8,128)S(1)} custom-call(f32[128,128]{1,0:T(8,128)S(1)} %cholesky.270), custom_call_target="Cholesky" | custom-call | tf_op jit(solution)/shard_map/jit(cholesky)/cholesky | solution.py:15
  96.0 9.8 custom-call.15
  106.3 11.7 %cholesky.189 = f32[128,128]{1,0:T(8,128)S(1)} custom-call(f32[128,128]{1,0:T(8,128)S(1)} %convolution_subtract_fusion.5), custom_call_target="Cholesky" | custom-call | tf_op jit(solution)/shard_map/jit(cholesky)/cholesky | solution.py:15
  118.1 0.7 compare_reduce_fusion.4
  120.1 0.7 fusion.33
  120.9 4.3 while.6
  121.1 0.7 fusion.89
  121.8 1.3 bitcast_dynamic-update-slice_fusion.6
  123.1 0.7 fusion.89
  123.8 1.3 bitcast_dynamic-update-slice_fusion.6
  125.2 19.7 %custom-call.16 = f32[2,128,128]{1,2,0:T(8,128)S(1)} custom-call(f32[2,128,128]{2,1,0:T(8,128)S(1)} %get-tuple-element.27), custom_call_target="InvertDiagBlocksLowerTriangular" | custom-call | tf_op jit(solution)/shard_map/jit(_solve_triangular)/triangular_solve | solution.py:17
  145.8 3.2 select_bitcast_fusion
  149.2 151.0 %all-reduce.13.cloned.1.call-done = f32[8,256,256]{1,2,0:T(8,128)} async-done(((f32[8,256,256]{1,2,0:T(8,128)}), f32[8,256,256]{1,2,0:T(8,128)}) %all-reduce.13.cloned.1.call-update) | async-done | bytes 2097168 | tf_op jit(solution)/shard_map/psum | solution.py:11
  300.2 1.2 constant_dynamic-slice_fusion.3
  301.7 0.8 select_bitcast_fusion.1
  303.0 1.1 copy.49
  304.1 63.7 %all-reduce.15.cloned.1.call-done = f32[2,256,256]{2,1,0:T(8,128)} async-done(((f32[2,256,256]{2,1,0:T(8,128)}), f32[2,256,256]{2,1,0:T(8,128)}) %all-reduce.15.cloned.1.call-update) | async-done | bytes 524304 | tf_op jit(solution)/shard_map/psum | solution.py:11
  367.8 6.2 fusion.1
  374.0 2.0 copy-done
  376.0 0.7 fusion.20
  377.2 63.8 %all-reduce.17.cloned.1.call-done = f32[256,256]{0,1:T(8,128)} async-done(((f32[256,256]{0,1:T(8,128)}), f32[256,256]{0,1:T(8,128)}) %all-reduce.17.cloned.1.call-update) | async-done | bytes 262160 | tf_op jit(solution)/shard_map/psum | solution.py:11
  441.0 1.1 copy.58
  442.1 1.0 fusion.29
  443.1 11.7 %cholesky.206 = f32[128,128]{1,0:T(8,128)S(1)} custom-call(f32[128,128]{1,0:T(8,128)S(1)} %cholesky.273), custom_call_target="Cholesky" | custom-call | tf_op jit(solution)/shard_map/jit(cholesky)/cholesky | solution.py:15
  454.8 0.7 compare_reduce_fusion.3
  455.6 9.8 custom-call.17
  465.9 11.7 %cholesky.223 = f32[128,128]{1,0:T(8,128)S(1)} custom-call(f32[128,128]{1,0:T(8,128)S(1)} %convolution_subtract_fusion.4), custom_call_target="Cholesky" | custom-call | tf_op jit(solution)/shard_map/jit(cholesky)/cholesky | solution.py:15
  479.6 4.2 while.7
  479.8 0.7 fusion.90
  480.4 1.3 bitcast_dynamic-update-slice_fusion.7
  482.5 1.3 bitcast_dynamic-update-slice_fusion.7
  483.8 19.7 %custom-call.18 = f32[2,128,128]{1,2,0:T(8,128)S(1)} custom-call(f32[2,128,128]{2,1,0:T(8,128)S(1)} %get-tuple-element.28), custom_call_target="InvertDiagBlocksLowerTriangular" | custom-call | tf_op jit(solution)/shard_map/jit(_solve_triangular)/triangular_solve | solution.py:17
  504.4 6.3 fusion.12
  510.8 151.2 %all-reduce.19.cloned.1.call-done = f32[8,256,256]{2,1,0:T(8,128)} async-done(((f32[8,256,256]{2,1,0:T(8,128)}), f32[8,256,256]{2,1,0:T(8,128)}) %all-reduce.19.cloned.1.call-update) | async-done | bytes 2097168 | tf_op jit(solution)/shard_map/psum | solution.py:11
  662.0 2.0 fusion.15
  664.5 1.9 copy.62
  666.4 62.9 %all-reduce.21.cloned.1.call-done = f32[2,256,256]{2,1,0:T(8,128)} async-done(((f32[2,256,256]{2,1,0:T(8,128)}), f32[2,256,256]{2,1,0:T(8,128)}) %all-reduce.21.cloned.1.call-update) | async-done | bytes 524304 | tf_op jit(solution)/shard_map/psum | solution.py:11
  729.3 6.2 fusion.3
  735.6 2.0 copy-done.1
  737.6 0.7 fusion.19
  738.6 63.9 %all-reduce.23.cloned.1.call-done = f32[256,256]{0,1:T(8,128)} async-done(((f32[256,256]{0,1:T(8,128)}), f32[256,256]{0,1:T(8,128)}) %all-reduce.23.cloned.1.call-update) | async-done | bytes 262160 | tf_op jit(solution)/shard_map/psum | solution.py:11
  802.5 1.1 copy.66
  803.6 1.0 fusion.28
  804.6 11.7 %cholesky.240 = f32[128,128]{1,0:T(8,128)S(1)} custom-call(f32[128,128]{1,0:T(8,128)S(1)} %cholesky.276), custom_call_target="Cholesky" | custom-call | tf_op jit(solution)/shard_map/jit(cholesky)/cholesky | solution.py:15
  816.4 0.7 compare_reduce_fusion.1
  817.1 9.8 custom-call.19
  827.4 11.7 %cholesky.257 = f32[128,128]{1,0:T(8,128)S(1)} custom-call(f32[128,128]{1,0:T(8,128)S(1)} %convolution_subtract_fusion.3), custom_call_target="Cholesky" | custom-call | tf_op jit(solution)/shard_map/jit(cholesky)/cholesky | solution.py:15
  841.1 4.3 while.8
  842.0 1.3 bitcast_dynamic-update-slice_fusion.8
  843.4 0.7 fusion.91
  844.1 1.3 bitcast_dynamic-update-slice_fusion.8
  845.4 19.7 %custom-call.20 = f32[2,128,128]{1,2,0:T(8,128)S(1)} custom-call(f32[2,128,128]{2,1,0:T(8,128)S(1)} %get-tuple-element.29), custom_call_target="InvertDiagBlocksLowerTriangular" | custom-call | tf_op jit(solution)/shard_map/jit(_solve_triangular)/triangular_solve | solution.py:17
  866.0 6.3 fusion.13
  872.4 151.2 %all-reduce.25.cloned.1.call-done = f32[8,256,256]{2,1,0:T(8,128)} async-done(((f32[8,256,256]{2,1,0:T(8,128)}), f32[8,256,256]{2,1,0:T(8,128)}) %all-reduce.25.cloned.1.call-update) | async-done | bytes 2097168 | tf_op jit(solution)/shard_map/psum | solution.py:11
  1023.6 2.0 fusion.14
  1026.1 1.9 copy.70
  1028.0 63.0 %all-reduce.27.cloned.1.call-done = f32[2,256,256]{2,1,0:T(8,128)} async-done(((f32[2,256,256]{2,1,0:T(8,128)}), f32[2,256,256]{2,1,0:T(8,128)}) %all-reduce.27.cloned.1.call-update) | async-done | bytes 524304 | tf_op jit(solution)/shard_map/psum | solution.py:11
  1091.0 7.5 fusion.5
  1098.5 7.2 copy.74
  (94 shorter events, 9.8 us)
Async XLA Ops:
  6.5 75.6 %all-reduce.11.cloned.1.call-start = ((), (), s32[]{:S(2)}) async-start(), calls=%async_computation | async-start | bytes 524288 | tf_op jit(solution)/shard_map/psum | solution.py:11
  15.4 284.8 %all-reduce.13.cloned.1.call-start = ((), (), s32[]{:S(2)}) async-start(), calls=%async_computation.1 | async-start | bytes 4194304 | tf_op jit(solution)/shard_map/psum | solution.py:11
  84.2 61.5 %slice-start = ((f32[8,256,2,256]{3,2,1,0:T(2,128)}), f32[8,256,1,256]{3,2,1,0:T(1,128)S(1)}, s32[]{:S(2)}) async-start(f32[8,256,2,256]{3,2,1,0:T(2,128)} %param.4), calls=%async_computation.9 | async-start | bytes 4194304 | tf_op jit(solution)/shard_map/slice | solution.py:41
  149.0 218.8 %all-reduce.15.cloned.1.call-start = ((), (), s32[]{:S(2)}) async-start(), calls=%async_computation.2 | async-start | bytes 1048576 | tf_op jit(solution)/shard_map/psum | solution.py:11
  300.2 67.6 %copy-start.4 = (f32[8,256,256]{1,2,0:T(8,128)S(1)}, f32[8,256,256]{1,2,0:T(8,128)}, u32[]{:S(2)}) copy-start(f32[8,256,256]{1,2,0:T(8,128)} %all-reduce.13.cloned.1.call-done) | copy-start | bytes 6291460
  302.6 138.5 %all-reduce.17.cloned.1.call-start = ((), (), s32[]{:S(2)}) async-start(), calls=%async_computation.3 | async-start | bytes 524288 | tf_op jit(solution)/shard_map/psum | solution.py:11
  374.0 2.0 copy-start
  376.8 285.2 %all-reduce.19.cloned.1.call-start = ((), (), s32[]{:S(2)}) async-start(), calls=%async_computation.4 | async-start | bytes 4194304 | tf_op jit(solution)/shard_map/psum | solution.py:11
  510.8 218.5 %all-reduce.21.cloned.1.call-start = ((), (), s32[]{:S(2)}) async-start(), calls=%async_computation.5 | async-start | bytes 1048576 | tf_op jit(solution)/shard_map/psum | solution.py:11
  662.0 2.5 copy-start.2
  664.0 138.5 %all-reduce.23.cloned.1.call-start = ((), (), s32[]{:S(2)}) async-start(), calls=%async_computation.6 | async-start | bytes 524288 | tf_op jit(solution)/shard_map/psum | solution.py:11
  735.6 2.0 copy-start.1
  738.3 285.3 %all-reduce.25.cloned.1.call-start = ((), (), s32[]{:S(2)}) async-start(), calls=%async_computation.7 | async-start | bytes 4194304 | tf_op jit(solution)/shard_map/psum | solution.py:11
  872.4 218.6 %all-reduce.27.cloned.1.call-start = ((), (), s32[]{:S(2)}) async-start(), calls=%async_computation.8 | async-start | bytes 1048576 | tf_op jit(solution)/shard_map/psum | solution.py:11
  1023.6 2.5 copy-start.3
Sparse Core Ops, SparseCore 0:
  15.5 66.5 all-reduce.10
  149.2 151.0 all-reduce.12
  302.7 65.0 all-reduce.14
  376.9 64.0 all-reduce.16
  510.9 151.0 all-reduce.18
  664.3 65.0 all-reduce.20
  738.4 64.0 all-reduce.22
  872.5 151.0 all-reduce.24
  1025.9 64.9 all-reduce.26
where the time goes:
time: 1120 us; the launch traced here: 1110 us
  waiting for transfers between devices  838 us (75%)
  other arithmetic  174 us (16%)
  local copies, waits for them, and re-layouts  41.2 us (4%)
  matrix products  39.9 us (4%)
  between operations  17.9 us (2%)
    psum x9, waiting for transfers between devices, broadcast(): return lax.psum(jnp.where(mine, x, jnp.zeros_like(x)), axis)  837 us
    another operation x20, other arithmetic, factorize(): factor = jnp.linalg.cholesky(diag_block)  103 us
    another operation x7, other arithmetic, factorize(): jax.scipy.linalg.solve_triangular(factor, identity, lower=True)  59.8 us
  transfers between devices with their start and end apart: 9, of which 9 were waited for; matrix products, arithmetic and copies ran while one was open for 1% of the time, Pallas kernels for 0%

commit v1 on v0

v1 whole, which is shorter than its diff:
```python
import functools

import jax
import jax.numpy as jnp
from jax import lax
from jax.experimental import pallas as pl
from jax.experimental.pallas import tpu as pltpu
from jax.sharding import PartitionSpec as P

B = 256
BAND = 32
PIV = 4
PAIRS = tuple((k, j) for k in range(3) for j in range(k, 3))
HIGHEST = lax.Precision.HIGHEST
F32 = jnp.float32
BF16 = jnp.bfloat16


def dot(a, b):
    return jnp.dot(a, b, precision=HIGHEST, preferred_element_type=F32)


def dot_tn(a, b):
    return lax.dot_general(
        a, b, (((0,), (0,)), ((), ())), precision=HIGHEST, preferred_element_type=F32
    )


def split(a):
    hi = a.astype(BF16)
    return hi, (a - hi.astype(F32)).astype(BF16)


def band_eliminate(rows, band):
    iota = lax.broadcasted_iota(jnp.int32, (8, 128), 0)
    chunks = list(rows[0].keys())
    groups = BAND // 8
    for g in range(0, BAND, PIV):
        mine, first = g // 8, g % 8
        col = band * BAND + g
        piv_chunk, lane = col // 128, col % 128
        v = [
            [
                jnp.broadcast_to(rows[s][piv_chunk][:, lane + a : lane + a + 1], (8, 128)) if s >= mine else None
                for s in range(groups)
            ]
            for a in range(PIV)
        ]
        row = [
            {c: jnp.broadcast_to(rows[mine][c][first + a : first + a + 1, :], (8, 128)) for c in chunks}
            for a in range(PIV)
        ]
        s = {
            (a, b): jnp.broadcast_to(v[b][mine][first + a : first + a + 1, :], (8, 128))
            for a in range(PIV)
            for b in range(a, PIV)
        }
        inv, root = [], []
        for a in range(PIV):
            inv.append(1.0 / s[a, a])
            root.append(lax.rsqrt(s[a, a]))
            for b in range(a + 1, PIV):
                ratio = s[a, b] * inv[a]
                for c in range(b, PIV):
                    s[b, c] = s[b, c] - ratio * s[a, c]
                for c in chunks:
                    row[b][c] = row[b][c] - ratio * row[a][c]
                for h in range(mine, groups):
                    v[b][h] = v[b][h] - ratio * v[a][h]
        for h in range(mine, groups):
            if h == mine and first + PIV == 8:
                continue
            scaled = [v[a][h] * inv[a] for a in range(PIV)]
            for c in chunks:
                total = scaled[0] * row[0][c]
                for a in range(1, PIV):
                    total = total + scaled[a] * row[a][c]
                new = rows[h][c] - total
                rows[h][c] = jnp.where(iota >= first + PIV, new, rows[h][c]) if h == mine else new
        for a in range(PIV):
            for c in chunks:
                rows[mine][c] = jnp.where(iota == first + a, row[a][c] * root[a], rows[mine][c])
    return rows


def factor_tile(g_ref):
    for band in range(B // BAND):
        lo = band * BAND
        chunks = (0, 1, 2) if band < 4 else (1, 2, 3)
        rows = [
            {c: g_ref[lo + 8 * s : lo + 8 * s + 8, 128 * c : 128 * c + 128] for c in chunks}
            for s in range(BAND // 8)
        ]
        rows = band_eliminate(rows, band)
        for s in range(BAND // 8):
            for c in chunks:
                g_ref[lo + 8 * s : lo + 8 * s + 8, 128 * c : 128 * c + 128] = rows[s][c]
        hi = lo + BAND
        if hi < B:
            left, right = 128 * chunks[0], 128 * chunks[-1] + 128
            done = g_ref[lo:hi, left:right]
            turned = g_ref[lo:hi, 0:B].T
            g_ref[hi : hi + BAND, left:right] -= dot(turned[hi : hi + BAND], done)
            if hi + BAND < B:
                g_ref[hi + BAND : B, left:right] -= dot(turned[hi + BAND : B], done)


def factor_kernel(place_ref, *refs):
    own, other = refs[0:4], refs[4:8]
    panel_ref, zhi_ref, zlo_ref, diag_ref, t_ref, g_ref, v_ref, lt_ref = refs[8:]
    my_row, my_col = place_ref[0], place_ref[1]
    x, core = my_row // 2, my_row % 2
    y = my_col // 8
    for shift in range(4):
        for side, bufs in ((core, own), (1 - core, other)):
            base = (((x - shift + 4) % 4) * 2 + side) * 32
            for step in range(4):
                at = pl.multiple_of(base + ((y - step + 4) % 4) * 8, 8)
                for n, (k, j) in enumerate(PAIRS):
                    t_ref[k, pl.ds(at, 8), j * B : (j + 1) * B] = bufs[shift][step, n]
    for p in range(8):
        for k in range(3):
            t_ref[k, p * 32 : p * 32 + 32, 3 * B :] = panel_ref[p, k]
    identity = jnp.where(
        lax.broadcasted_iota(jnp.int32, (B, B), 0) == lax.broadcasted_iota(jnp.int32, (B, B), 1), 1.0, 0.0
    ).astype(F32)
    upper = lax.broadcasted_iota(jnp.int32, (B, B), 0) <= lax.broadcasted_iota(jnp.int32, (B, B), 1)

    def step(k, carry):
        for j in range(3):

            @pl.when(k == j)
            def _():
                g_ref[:, 0:B] = t_ref[j, :, j * B : (j + 1) * B]

        g_ref[:, B:] = identity
        factor_tile(g_ref)
        lt_ref[k] = jnp.where(upper, g_ref[:, 0:B], 0.0)
        v_ref[k] = g_ref[:, B:]
        for j in range(3):

            @pl.when(k == j)
            def _():
                lo = (j + 1) * B
                solved = dot(v_ref[j], t_ref[j, :, lo:])
                t_ref[j, :, lo:] = solved
                for i in range(j + 1, 3):
                    t_ref[i, :, i * B :] -= dot_tn(
                        t_ref[j, :, i * B : (i + 1) * B], t_ref[j, :, i * B :]
                    )

        return carry

    lax.fori_loop(0, 3, step, 0)
    for k in range(3):
        t_ref[k, :, 3 * B : 4 * B] = jnp.where(
            my_col == k, -identity, jnp.where(my_col < 3, 0.0, t_ref[k, :, 3 * B : 4 * B])
        )
    for k in (2, 1, 0):
        rest = t_ref[k, :, 3 * B :]
        for i in range(k + 1, 3):
            rest -= dot(t_ref[k, :, i * B : (i + 1) * B], t_ref[i, :, 3 * B :])
        z = dot_tn(v_ref[k], rest)
        t_ref[k, :, 3 * B :] = z
        hi, lo = split(z)
        for p in range(8):
            zhi_ref[p * 96 + k * 32 : p * 96 + k * 32 + 32, :] = hi[p * 32 : p * 32 + 32]
            zlo_ref[p * 96 + k * 32 : p * 96 + k * 32 + 32, :] = lo[p * 32 : p * 32 + 32]
    diag_ref[...] = lt_ref[jnp.minimum(my_col, 2)].T


def factor(place, own, other, panel):
    vmem = pl.BlockSpec(memory_space=pltpu.VMEM)
    return pl.pallas_call(
        factor_kernel,
        out_shape=(
            jax.ShapeDtypeStruct((3 * B, 2 * B), BF16),
            jax.ShapeDtypeStruct((3 * B, 2 * B), BF16),
            jax.ShapeDtypeStruct((B, B), F32),
        ),
        in_specs=[pl.BlockSpec(memory_space=pltpu.SMEM)] + [vmem] * 9,
        out_specs=(vmem, vmem, vmem),
        scratch_shapes=[
            pltpu.VMEM((3, B, 5 * B), F32),
            pltpu.VMEM((B, 2 * B), F32),
            pltpu.VMEM((3, B, B), F32),
            pltpu.VMEM((3, B, B), F32),
        ],
        compiler_params=pltpu.CompilerParams(vmem_limit_bytes=40 * 2**20),
        name="factor_panel",
    )(place, *own, *other, panel)


def update_kernel(place_ref, a_ref, u_ref, zhi_ref, zlo_ref, diag_ref, o_ref):
    t = pl.program_id(0)
    i = t * 8 + place_ref[0]
    my_col = place_ref[1]
    o_ref[...] = a_ref[...]

    @pl.when(i >= my_col)
    def _():
        hi, lo = split(u_ref[...].reshape(3 * B, B).T)

        def product(z):
            zhi, zlo = zhi_ref[:, z], zlo_ref[:, z]
            d = functools.partial(jnp.dot, preferred_element_type=F32)
            return d(hi, zhi) + (d(hi, zlo) + d(lo, zhi))

        panel = my_col < 3
        base = jnp.where(panel, 0.0, a_ref[0, :, 0, :])
        o_ref[0, :, 0, :] = base - product(slice(0, B))

        @pl.when(i >= my_col + 32)
        def _():
            o_ref[0, :, 1, :] = a_ref[0, :, 1, :] - product(slice(B, 2 * B))

        @pl.when(jnp.logical_and(i == my_col, panel))
        def _():
            o_ref[0, :, 0, :] = diag_ref[...]


def update(place, a, u, zhi, zlo, diag):
    full = pl.BlockSpec(memory_space=pltpu.VMEM)
    return pl.pallas_call(
        update_kernel,
        grid=(8,),
        out_shape=jax.ShapeDtypeStruct(a.shape, F32),
        in_specs=[
            pl.BlockSpec(memory_space=pltpu.SMEM),
            pl.BlockSpec((1, B, 2, B), lambda t: (t, 0, 0, 0)),
            pl.BlockSpec((8, 3, 32, B), lambda t: (t % 4, 0, 0, t // 4)),
            full,
            full,
            full,
        ],
        out_specs=pl.BlockSpec((1, B, 2, B), lambda t: (t, 0, 0, 0)),
        compiler_params=pltpu.CompilerParams(vmem_limit_bytes=40 * 2**20),
        name="trailing_update",
    )(place, a, u, zhi, zlo, diag)


def spread_corner(mine, my_col):
    y, z = my_col // 8, my_col % 8
    quarter = mine.reshape(3, 4, 8, B)
    got = jnp.where(y == 0, quarter[:, 0], 0.0)
    for d in range(1, 4):
        got = got + lax.ppermute(quarter[:, d], "col", [(j, d * 8 + j) for j in range(3)])
    got = jnp.where(z < 3, got, 0.0)
    got = got + lax.ppermute(got, "col", [(h * 8 + j, h * 8 + j + 4) for h in range(4) for j in range(3)])
    stack = [got]
    for s in range(1, 4):
        pairs = [
            (h * 8 + q * 4 + j, h * 8 + q * 4 + (j + s) % 4) for h in range(4) for q in range(2) for j in range(3)
        ]
        stack.append(lax.ppermute(got, "col", pairs))
    column = []
    for j in range(3):
        at = (z - j) % 4
        pick = stack[3]
        for s in range(3):
            pick = jnp.where(at == s, stack[s], pick)
        column.append(pick)
    part = jnp.stack([column[j][k] for k, j in PAIRS])
    parts = [part]
    for s in range(1, 4):
        parts.append(lax.ppermute(part, "col", [(c, (c + 8 * s) % 32) for c in range(32)]))
    block = jnp.stack(parts)
    own = [block]
    for s in range(1, 4):
        own.append(lax.ppermute(block, "row", [(r, (r + 2 * s) % 8) for r in range(8)]))
    other = [lax.ppermute(b, "row", [(r, r ^ 1) for r in range(8)]) for b in own]
    return own, other


def on_device(covariance):
    my_row, my_col = lax.axis_index("row"), lax.axis_index("col")
    place = jnp.stack([my_row, my_col]).astype(jnp.int32)
    top = covariance[0].reshape(8, 32, 2 * B)
    mine = lax.all_to_all(top, "row", 0, 0, tiled=True)[:3]
    turned = lax.ppermute(
        mine,
        ("row", "col"),
        [(r * 32 + y * 8 + z, z * 32 + y * 8 + r) for r in range(8) for y in range(4) for z in range(8)],
    )
    rows = lax.all_gather(turned, "col")
    panel = lax.all_gather(mine, "row")
    own, other = spread_corner(mine[:, :, :B], my_col)
    zhi, zlo, diag = factor(place, own, other, panel)
    return update(place, covariance, rows, zhi, zlo, diag)


def solution(mesh):
    spec = (P(None, "row", None, "col"),)
    return jax.shard_map(on_device, mesh=mesh, in_specs=spec, out_specs=spec[0], check_vma=False)
```

time: 1120 us -> 167 us (0.15)
  waiting for transfers between devices: 838 us -> 16.7 us
  other arithmetic: 174 us -> 0.12 us
  Pallas kernels: 0 us -> 55.2 us
  starting transfers between devices: 0.95 us -> 56.1 us
  matrix products: 39.9 us -> 0 us
  local copies, waits for them, and re-layouts: 41.2 us -> 9.45 us
  blocking collectives: 0 us -> 15 us
    psum x9 -> x0, waiting for transfers between devices: 837 us -> none  [broadcast(): return lax.psum(jnp.where(mine, x, jnp.zeros_like(x)), axis)]
    another operation x27 -> x2, other arithmetic: 163 us -> 0.09 us  [the longest x1 0.07 us: on_device(): place = jnp.stack([my_row, my_col]).astype(jnp.int32)]
    ppermute x0 -> x18, starting transfers between devices: none -> 56 us  [the longest x4 13.7 us: spread_corner(): lax.ppermute(b, 'row', [(r, r ^ 1) for r in range(8)])]
    pallas_call x0 -> x2, Pallas kernels: none -> 55.2 us  [the longest x1 45.6 us: factor(): pl.pallas_call(factor_kernel, out_shape=(jax.ShapeDtypeStruct((3 * B, 2 *...]
    dot_general x6 -> x0, matrix products: 35.9 us -> none  [the longest x3 19.9 us: on_device(): jnp.einsum('tab,ucb->tauc', row_panel, col_panel, precision=lax.Precision...]
    all_to_all x0 -> x1, blocking collectives: none -> 15 us  [on_device(): mine = lax.all_to_all(top, 'row', 0, 0, tiled=True)[:3]]
    ppermute x0 -> x18, waiting for transfers between devices: none -> 12.2 us  [the longest x3 3.93 us: spread_corner(): lax.ppermute(part, 'col', [(c, (c + 8 * s) % 32) for c in range(32)])]
    another operation x28 -> x2, local copies, waits for them, and re-layouts: 12.2 us -> 0.42 us  [the longest x1 0.42 us: on_device(): top = covariance[0].reshape(8, 32, 2 * B)]
  transfers between devices with their start and end apart: 9 -> 20, of which waited for: 9 -> 9; matrix products, arithmetic and copies ran while one was open for 1% -> 0% of each run, Pallas kernels for 0% -> 27%
where the time goes in v1:
time: 167 us; the launch traced here: 166 us
  starting transfers between devices  56.1 us (34%)
  Pallas kernels  55.2 us (33%)
  waiting for transfers between devices  16.7 us (10%)
  blocking collectives  15 us (9%)
  between operations  13.7 us (8%)
  local copies, waits for them, and re-layouts  9.45 us (6%)
    pallas_call x1, Pallas kernels, factor(): pl.pallas_call(factor_kernel, out_shape=(jax.ShapeDtypeStruct((3 * B, 2 *...  45.6 us
    all_to_all x1, blocking collectives, on_device(): mine = lax.all_to_all(top, 'row', 0, 0, tiled=True)[:3]  15 us
    ppermute x4, starting transfers between devices, spread_corner(): lax.ppermute(b, 'row', [(r, r ^ 1) for r in range(8)])  13.7 us
    ppermute x1, starting transfers between devices, spread_corner(): lax.ppermute(got, 'col', [(h * 8 + j, h * 8 + j + 4) for h in range(4) fo...  10.6 us
    pallas_call x1, Pallas kernels, update(): pl.pallas_call(update_kernel, grid=(8,), out_shape=jax.ShapeDtypeStruct(a...  9.59 us
    ppermute x3, starting transfers between devices, spread_corner(): stack.append(lax.ppermute(got, 'col', pairs))  8.87 us
    ppermute x3, starting transfers between devices, spread_corner(): lax.ppermute(block, 'row', [(r, (r + 2 * s) % 8) for r in range(8)])  7.79 us
    unnamed x11, local copies, waits for them, and re-layouts  7.1 us
  transfers between devices with their start and end apart: 20, of which 9 were waited for; matrix products, arithmetic and copies ran while one was open for 0% of the time, Pallas kernels for 27%

profile of v1, /device:TPU:1, one launch (start us, length us, event | category | flops | bytes accessed | tf_op | source)
XLA Modules:
  0.0 166.2 jit_solution(7250654200562994420)
XLA Ops:
  6.5 0.0 all-gather.7.cloned.1.call-start
  6.5 1.2 slice.39
  7.8 0.4 reshape_squeeze.3
  8.2 15.0 %all_to_all.5 = f32[8,32,512]{2,1,0:T(8,128)S(1)} all-to-all(f32[8,32,512]{2,1,0:T(8,128)S(1)} %reshape_squeeze.3), channel_id=1, replica_groups=mesh['row'=8,'col'=32] {'row'}, dimensions={0} | all-to-all | bytes 1048576 | tf_op jit(solution)/shard_map/all_to_all | solution.py:279
  23.2 0.7 slice.51
  23.9 0.0 all-gather.7.cloned.1.call-update
  23.9 0.0 all-gather.5.cloned.1.call-start
  24.0 4.4 %collective-permute-start = (f32[3,32,512]{2,1,0:T(8,128)}, f32[3,32,512]{2,1,0:T(8,128)S(1)}, u32[]{:S(2)}, u32[]{:S(2)}) collective-permute-start(f32[3,32,512]{2,1,0:T(8,128)} %slice.51), channel_id=1, source_target_pairs={{0,0},{1,32},{2,64},{3,96},{4,128},{5,160},{6,192},{7,224},{8,8},{... | collective-permute-start | bytes 589832 | tf_op jit(solution)/shard_map/ppermute | solution.py:280
  28.4 3.7 %collective-permute-done = f32[3,32,512]{2,1,0:T(8,128)S(1)} collective-permute-done((f32[3,32,512]{2,1,0:T(8,128)}, f32[3,32,512]{2,1,0:T(8,128)S(1)}, u32[]{:S(2)}, u32[]{:S(2)}) %collective-permute-start) | collective-permute-done | bytes 196640 | tf_op jit(solution)/shard_map/ppermute | solution.py:280
  32.1 0.0 copy-start.3
  32.1 0.7 copy-done.3
  32.8 0.0 all-gather.5.cloned.1.call-update
  32.9 3.5 %collective-permute-start.1 = (f32[3,8,256]{2,1,0:T(8,128)S(1)}, f32[3,8,256]{2,1,0:T(8,128)S(1)}, u32[]{:S(2)}, u32[]{:S(2)}) collective-permute-start(f32[3,8,256]{2,1,0:T(8,128)S(1)} %get-tuple-element.13), channel_id=1, source_target_pairs={{0,8},{1,9},{2,10},{32,40},{33,41},{34,42},{64,72},{65,73},{66,74}... | collective-permute-start | bytes 73736 | tf_op jit(solution)/shard_map/ppermute | solution.py:247
  36.4 2.0 %collective-permute-start.2 = (f32[3,8,256]{2,1,0:T(8,128)S(1)}, f32[3,8,256]{2,1,0:T(8,128)S(1)}, u32[]{:S(2)}, u32[]{:S(2)}) collective-permute-start(f32[3,8,256]{2,1,0:T(8,128)S(1)} %get-tuple-element.14), channel_id=1, source_target_pairs={{0,16},{1,17},{2,18},{32,48},{33,49},{34,50},{64,80},{65,81},{66,8... | collective-permute-start | bytes 73736 | tf_op jit(solution)/shard_map/ppermute | solution.py:247
  38.4 1.3 collective-permute-start.3
  39.7 0.0 collective-permute-done.1
  39.7 0.0 collective-permute-done.2
  39.7 0.9 collective-permute-done.3
  40.6 10.6 %collective-permute-start.4 = (f32[3,8,256]{2,1,0:T(8,128)S(1)}, f32[3,8,256]{2,1,0:T(8,128)S(1)}, u32[]{:S(2)}, u32[]{:S(2)}) collective-permute-start(f32[3,8,256]{2,1,0:T(8,128)S(1)} %fusion.5), channel_id=1, source_target_pairs={{0,4},{1,5},{2,6},{8,12},{9,13},{10,14},{16,20},{17,21},{18,22},{2... | collective-permute-start | bytes 73736 | tf_op jit(solution)/shard_map/ppermute | solution.py:249
  51.2 0.9 collective-permute-done.4
  52.2 1.9 %collective-permute-start.7 = (f32[3,8,256]{2,1,0:T(8,128)S(1)}, f32[3,8,256]{2,1,0:T(8,128)S(1)}, u32[]{:S(2)}, u32[]{:S(2)}) collective-permute-start(f32[3,8,256]{2,1,0:T(8,128)S(1)} %add.33), channel_id=1, source_target_pairs={{0,3},{1,0},{2,1},{4,7},{5,4},{6,5},{8,11},{9,8},{10,9},{12,15},{1... | collective-permute-start | bytes 73736 | tf_op jit(solution)/shard_map/ppermute | solution.py:255
  54.1 3.4 %collective-permute-start.6 = (f32[3,8,256]{2,1,0:T(8,128)S(1)}, f32[3,8,256]{2,1,0:T(8,128)S(1)}, u32[]{:S(2)}, u32[]{:S(2)}) collective-permute-start(f32[3,8,256]{2,1,0:T(8,128)S(1)} %add.33), channel_id=1, source_target_pairs={{0,1},{1,2},{2,3},{4,5},{5,6},{6,7},{8,9},{9,10},{10,11},{12,13},{... | collective-permute-start | bytes 73736 | tf_op jit(solution)/shard_map/ppermute | solution.py:255
  57.5 3.6 %collective-permute-start.5 = (f32[3,8,256]{2,1,0:T(8,128)S(1)}, f32[3,8,256]{2,1,0:T(8,128)S(1)}, u32[]{:S(2)}, u32[]{:S(2)}) collective-permute-start(f32[3,8,256]{2,1,0:T(8,128)S(1)} %add.33), channel_id=1, source_target_pairs={{0,2},{1,3},{2,0},{4,6},{5,7},{6,4},{8,10},{9,11},{10,8},{12,14},{... | collective-permute-start | bytes 73736 | tf_op jit(solution)/shard_map/ppermute | solution.py:255
  61.1 0.0 collective-permute-done.7
  61.2 0.0 collective-permute-done.6
  61.2 1.8 %collective-permute-done.5 = f32[3,8,256]{2,1,0:T(8,128)S(1)} collective-permute-done((f32[3,8,256]{2,1,0:T(8,128)S(1)}, f32[3,8,256]{2,1,0:T(8,128)S(1)}, u32[]{:S(2)}, u32[]{:S(2)}) %collective-permute-start.5) | collective-permute-done | bytes 24608 | tf_op jit(solution)/shard_map/ppermute | solution.py:255
  63.0 2.8 %collective-permute-start.10 = (f32[6,8,256]{2,1,0:T(8,128)S(1)}, f32[6,8,256]{2,1,0:T(8,128)S(1)}, u32[]{:S(2)}, u32[]{:S(2)}) collective-permute-start(f32[6,8,256]{2,1,0:T(8,128)S(1)} %slice_dynamic-update-slice_fusion), channel_id=1, source_target_pairs={{0,24},{1,25},{2,26},{3,27},{4,28},{5,29},{6,30},{7,31},{8,0},{9,1... | collective-permute-start | bytes 147464 | tf_op jit(solution)/shard_map/ppermute | solution.py:266
  65.8 0.3 collective-permute-start.9
  66.2 0.7 collective-permute-start.8
  66.9 0.1 collective-permute-done.10
  67.0 3.3 %collective-permute-done.9 = f32[6,8,256]{2,1,0:T(8,128)S(1)} collective-permute-done((f32[6,8,256]{2,1,0:T(8,128)S(1)}, f32[6,8,256]{2,1,0:T(8,128)S(1)}, u32[]{:S(2)}, u32[]{:S(2)}) %collective-permute-start.9) | collective-permute-done | bytes 49184 | tf_op jit(solution)/shard_map/ppermute | solution.py:266
  70.3 0.5 collective-permute-done.8
  70.8 7.1 %collective-permute-start.13 = (f32[4,6,8,256]{3,2,1,0:T(8,128)S(1)}, f32[4,6,8,256]{3,2,1,0:T(8,128)S(1)}, u32[]{:S(2)}, u32[]{:S(2)}) collective-permute-start(f32[4,6,8,256]{3,2,1,0:T(8,128)S(1)} %pad_maximum_fusion.refs_0_), channel_id=1, source_target_pairs={{0,192},{32,224},{64,0},{96,32},{128,64},{160,96},{192,128},{224,1... | collective-permute-start | bytes 589832 | tf_op jit(solution)/shard_map/ppermute | solution.py:270
  77.9 0.6 collective-permute-start.12
  78.5 0.1 collective-permute-start.11
  78.6 5.7 %collective-permute-start.14 = (f32[4,6,8,256]{3,2,1,0:T(8,128)S(1)}, f32[4,6,8,256]{3,2,1,0:T(8,128)S(1)}, u32[]{:S(2)}, u32[]{:S(2)}) collective-permute-start(f32[4,6,8,256]{3,2,1,0:T(8,128)S(1)} %pad_maximum_fusion.refs_0_), channel_id=1, source_target_pairs={{0,32},{32,0},{64,96},{96,64},{128,160},{160,128},{192,224},{224,1... | collective-permute-start | bytes 589832 | tf_op jit(solution)/shard_map/ppermute | solution.py:271
  84.2 0.0 collective-permute-done.13.refs_3_
  84.3 4.3 %collective-permute-start.17 = (f32[4,6,8,256]{3,2,1,0:T(8,128)S(1)}, f32[4,6,8,256]{3,2,1,0:T(8,128)S(1)}, u32[]{:S(2)}, u32[]{:S(2)}) collective-permute-start(f32[4,6,8,256]{3,2,1,0:T(8,128)S(1)} %collective-permute-done.13.refs_3_), channel_id=1, source_target_pairs={{0,32},{32,0},{64,96},{96,64},{128,160},{160,128},{192,224},{224,1... | collective-permute-start | bytes 589832 | tf_op jit(solution)/shard_map/ppermute | solution.py:271
  88.6 0.0 collective-permute-done.12.refs_2_
  88.6 2.0 %collective-permute-start.16 = (f32[4,6,8,256]{3,2,1,0:T(8,128)S(1)}, f32[4,6,8,256]{3,2,1,0:T(8,128)S(1)}, u32[]{:S(2)}, u32[]{:S(2)}) collective-permute-start(f32[4,6,8,256]{3,2,1,0:T(8,128)S(1)} %collective-permute-done.12.refs_2_), channel_id=1, source_target_pairs={{0,32},{32,0},{64,96},{96,64},{128,160},{160,128},{192,224},{224,1... | collective-permute-start | bytes 589832 | tf_op jit(solution)/shard_map/ppermute | solution.py:271
  90.6 0.0 collective-permute-done.11.refs_1_
  90.6 1.7 %collective-permute-start.15 = (f32[4,6,8,256]{3,2,1,0:T(8,128)S(1)}, f32[4,6,8,256]{3,2,1,0:T(8,128)S(1)}, u32[]{:S(2)}, u32[]{:S(2)}) collective-permute-start(f32[4,6,8,256]{3,2,1,0:T(8,128)S(1)} %collective-permute-done.11.refs_1_), channel_id=1, source_target_pairs={{0,32},{32,0},{64,96},{96,64},{128,160},{160,128},{192,224},{224,1... | collective-permute-start | bytes 589832 | tf_op jit(solution)/shard_map/ppermute | solution.py:271
  92.3 0.1 pad_add_fusion.place_ref
  92.4 0.0 collective-permute-done.14.refs_4_
  92.4 0.0 collective-permute-done.17.refs_7_
  92.4 0.0 collective-permute-done.16.refs_6_
  92.4 1.0 collective-permute-done.15.refs_5_
  93.4 0.0 all-gather.7.cloned.1.call-done
  93.4 0.0 copy-start.2
  93.4 1.4 copy-done.2
  94.8 45.6 %factor_panel.1 = (bf16[768,512]{1,0:T(8,128)(2,1)S(1)}, bf16[768,512]{1,0:T(8,128)(2,1)S(1)}, f32[256,256]{1,0:T(8,128)S(1)}) custom-call(s32[2]{0:T(128)S(1)} %pad_add_fusion.place_ref, f32[4,6,8,256]{3,2,1,0:T(8,128)S(1)} %pad_maximum_fusion.refs_0_, f32[4,6,8,256]{3,2,1,0:T(8,128)S(1)} %collective-permute-done.11.refs_1_, ...), custom_call_target="tpu_custom_call" | custom-call | tf_op jit(solution)/shard_map/factor_panel/pallas_call | solution.py:174
  140.3 4.5 %all-gather.5.cloned.1.call-done = f32[96,32,512]{2,1,0:T(8,128)} async-done(((f32[3,32,512]{2,1,0:T(8,128)}), f32[96,32,512]{2,1,0:T(8,128)}) %all-gather.5.cloned.1.call-update) | async-done | bytes 6291472 | tf_op jit(solution)/shard_map/all_gather | solution.py:285
  144.8 0.0 copy-start
  144.8 2.8 %copy-done = f32[96,32,512]{2,1,0:T(8,128)S(1)} copy-done((f32[96,32,512]{2,1,0:T(8,128)S(1)}, f32[96,32,512]{2,1,0:T(8,128)}, u32[]{:S(2)}) %copy-start) | copy-done | bytes 6291480
  147.6 0.0 copy-start.1
  147.6 2.2 %copy-done.1 = f32[8,256,2,256]{3,2,1,0:T(2,128)S(1)} copy-done((f32[8,256,2,256]{3,2,1,0:T(2,128)S(1)}, f32[8,256,2,256]{3,2,1,0:T(2,128)}, u32[]{:S(2)}) %copy-start.1) | copy-done | bytes 4194328
  149.8 9.6 %trailing_update.1 = f32[8,256,2,256]{3,2,1,0:T(2,128)} custom-call(s32[2]{0:T(128)S(1)} %pad_add_fusion.place_ref, f32[8,256,2,256]{3,2,1,0:T(2,128)S(1)} %copy-done.1, f32[32,3,32,512]{3,2,1,0:T(8,128)S(1)} %bitcast.46, bf16[768,512]{1,0:T(8,128)(2,1)S(1)} %get-tuple-element.8.zhi_ref, bf16[768,512]{1,0:T(8,128)(2,1)S(1)} %get-tuple-element.9.zlo_ref, ...), custom_call_target="tpu_custom_call" | custom-call | tf_op jit(solution)/shard_map/trailing_update/pallas_call | solution.py:224
  (11 shorter events, 0.1 us)
Async XLA Ops:
  6.5 86.8 %all-gather.7.cloned.1.call-start = ((), (), s32[]{:S(2)}) async-start(), calls=%async_computation.2 | async-start | bytes 1769472 | tf_op jit(solution)/shard_map/all_gather | solution.py:286
  23.9 120.9 %all-gather.5.cloned.1.call-start = ((), (), s32[]{:S(2)}) async-start(), calls=%async_computation.1 | async-start | bytes 6488064 | tf_op jit(solution)/shard_map/all_gather | solution.py:285
  24.0 8.1 %collective-permute-start = (f32[3,32,512]{2,1,0:T(8,128)}, f32[3,32,512]{2,1,0:T(8,128)S(1)}, u32[]{:S(2)}, u32[]{:S(2)}) collective-permute-start(f32[3,32,512]{2,1,0:T(8,128)} %slice.51), channel_id=1, source_target_pairs={{0,0},{1,32},{2,64},{3,96},{4,128},{5,160},{6,192},{7,224},{8,8},{... | collective-permute-start | bytes 589832 | tf_op jit(solution)/shard_map/ppermute | solution.py:280
  32.1 0.7 copy-start.3
  32.9 6.8 %collective-permute-start.1 = (f32[3,8,256]{2,1,0:T(8,128)S(1)}, f32[3,8,256]{2,1,0:T(8,128)S(1)}, u32[]{:S(2)}, u32[]{:S(2)}) collective-permute-start(f32[3,8,256]{2,1,0:T(8,128)S(1)} %get-tuple-element.13), channel_id=1, source_target_pairs={{0,8},{1,9},{2,10},{32,40},{33,41},{34,42},{64,72},{65,73},{66,74}... | collective-permute-start | bytes 73736 | tf_op jit(solution)/shard_map/ppermute | solution.py:247
  36.4 3.3 %collective-permute-start.2 = (f32[3,8,256]{2,1,0:T(8,128)S(1)}, f32[3,8,256]{2,1,0:T(8,128)S(1)}, u32[]{:S(2)}, u32[]{:S(2)}) collective-permute-start(f32[3,8,256]{2,1,0:T(8,128)S(1)} %get-tuple-element.14), channel_id=1, source_target_pairs={{0,16},{1,17},{2,18},{32,48},{33,49},{34,50},{64,80},{65,81},{66,8... | collective-permute-start | bytes 73736 | tf_op jit(solution)/shard_map/ppermute | solution.py:247
  38.4 2.2 %collective-permute-start.3 = (f32[3,8,256]{2,1,0:T(8,128)S(1)}, f32[3,8,256]{2,1,0:T(8,128)S(1)}, u32[]{:S(2)}, u32[]{:S(2)}) collective-permute-start(f32[3,8,256]{2,1,0:T(8,128)S(1)} %get-tuple-element.15), channel_id=1, source_target_pairs={{0,24},{1,25},{2,26},{32,56},{33,57},{34,58},{64,88},{65,89},{66,9... | collective-permute-start | bytes 73736 | tf_op jit(solution)/shard_map/ppermute | solution.py:247
  40.6 11.6 %collective-permute-start.4 = (f32[3,8,256]{2,1,0:T(8,128)S(1)}, f32[3,8,256]{2,1,0:T(8,128)S(1)}, u32[]{:S(2)}, u32[]{:S(2)}) collective-permute-start(f32[3,8,256]{2,1,0:T(8,128)S(1)} %fusion.5), channel_id=1, source_target_pairs={{0,4},{1,5},{2,6},{8,12},{9,13},{10,14},{16,20},{17,21},{18,22},{2... | collective-permute-start | bytes 73736 | tf_op jit(solution)/shard_map/ppermute | solution.py:249
  52.2 9.0 %collective-permute-start.7 = (f32[3,8,256]{2,1,0:T(8,128)S(1)}, f32[3,8,256]{2,1,0:T(8,128)S(1)}, u32[]{:S(2)}, u32[]{:S(2)}) collective-permute-start(f32[3,8,256]{2,1,0:T(8,128)S(1)} %add.33), channel_id=1, source_target_pairs={{0,3},{1,0},{2,1},{4,7},{5,4},{6,5},{8,11},{9,8},{10,9},{12,15},{1... | collective-permute-start | bytes 73736 | tf_op jit(solution)/shard_map/ppermute | solution.py:255
  54.1 7.1 %collective-permute-start.6 = (f32[3,8,256]{2,1,0:T(8,128)S(1)}, f32[3,8,256]{2,1,0:T(8,128)S(1)}, u32[]{:S(2)}, u32[]{:S(2)}) collective-permute-start(f32[3,8,256]{2,1,0:T(8,128)S(1)} %add.33), channel_id=1, source_target_pairs={{0,1},{1,2},{2,3},{4,5},{5,6},{6,7},{8,9},{9,10},{10,11},{12,13},{... | collective-permute-start | bytes 73736 | tf_op jit(solution)/shard_map/ppermute | solution.py:255
  57.5 5.5 %collective-permute-start.5 = (f32[3,8,256]{2,1,0:T(8,128)S(1)}, f32[3,8,256]{2,1,0:T(8,128)S(1)}, u32[]{:S(2)}, u32[]{:S(2)}) collective-permute-start(f32[3,8,256]{2,1,0:T(8,128)S(1)} %add.33), channel_id=1, source_target_pairs={{0,2},{1,3},{2,0},{4,6},{5,7},{6,4},{8,10},{9,11},{10,8},{12,14},{... | collective-permute-start | bytes 73736 | tf_op jit(solution)/shard_map/ppermute | solution.py:255
  63.0 4.0 %collective-permute-start.10 = (f32[6,8,256]{2,1,0:T(8,128)S(1)}, f32[6,8,256]{2,1,0:T(8,128)S(1)}, u32[]{:S(2)}, u32[]{:S(2)}) collective-permute-start(f32[6,8,256]{2,1,0:T(8,128)S(1)} %slice_dynamic-update-slice_fusion), channel_id=1, source_target_pairs={{0,24},{1,25},{2,26},{3,27},{4,28},{5,29},{6,30},{7,31},{8,0},{9,1... | collective-permute-start | bytes 147464 | tf_op jit(solution)/shard_map/ppermute | solution.py:266
  65.8 4.5 %collective-permute-start.9 = (f32[6,8,256]{2,1,0:T(8,128)S(1)}, f32[6,8,256]{2,1,0:T(8,128)S(1)}, u32[]{:S(2)}, u32[]{:S(2)}) collective-permute-start(f32[6,8,256]{2,1,0:T(8,128)S(1)} %slice_dynamic-update-slice_fusion), channel_id=1, source_target_pairs={{0,16},{1,17},{2,18},{3,19},{4,20},{5,21},{6,22},{7,23},{8,24},{9,... | collective-permute-start | bytes 147464 | tf_op jit(solution)/shard_map/ppermute | solution.py:266
  66.2 4.6 %collective-permute-start.8 = (f32[6,8,256]{2,1,0:T(8,128)S(1)}, f32[6,8,256]{2,1,0:T(8,128)S(1)}, u32[]{:S(2)}, u32[]{:S(2)}) collective-permute-start(f32[6,8,256]{2,1,0:T(8,128)S(1)} %slice_dynamic-update-slice_fusion), channel_id=1, source_target_pairs={{0,8},{1,9},{2,10},{3,11},{4,12},{5,13},{6,14},{7,15},{8,16},{9,17... | collective-permute-start | bytes 147464 | tf_op jit(solution)/shard_map/ppermute | solution.py:266
  70.8 13.5 %collective-permute-start.13 = (f32[4,6,8,256]{3,2,1,0:T(8,128)S(1)}, f32[4,6,8,256]{3,2,1,0:T(8,128)S(1)}, u32[]{:S(2)}, u32[]{:S(2)}) collective-permute-start(f32[4,6,8,256]{3,2,1,0:T(8,128)S(1)} %pad_maximum_fusion.refs_0_), channel_id=1, source_target_pairs={{0,192},{32,224},{64,0},{96,32},{128,64},{160,96},{192,128},{224,1... | collective-permute-start | bytes 589832 | tf_op jit(solution)/shard_map/ppermute | solution.py:270
  77.9 10.7 %collective-permute-start.12 = (f32[4,6,8,256]{3,2,1,0:T(8,128)S(1)}, f32[4,6,8,256]{3,2,1,0:T(8,128)S(1)}, u32[]{:S(2)}, u32[]{:S(2)}) collective-permute-start(f32[4,6,8,256]{3,2,1,0:T(8,128)S(1)} %pad_maximum_fusion.refs_0_), channel_id=1, source_target_pairs={{0,128},{32,160},{64,192},{96,224},{128,0},{160,32},{192,64},{224,... | collective-permute-start | bytes 589832 | tf_op jit(solution)/shard_map/ppermute | solution.py:270
  78.5 12.1 %collective-permute-start.11 = (f32[4,6,8,256]{3,2,1,0:T(8,128)S(1)}, f32[4,6,8,256]{3,2,1,0:T(8,128)S(1)}, u32[]{:S(2)}, u32[]{:S(2)}) collective-permute-start(f32[4,6,8,256]{3,2,1,0:T(8,128)S(1)} %pad_maximum_fusion.refs_0_), channel_id=1, source_target_pairs={{0,64},{32,96},{64,128},{96,160},{128,192},{160,224},{192,0},{224,... | collective-permute-start | bytes 589832 | tf_op jit(solution)/shard_map/ppermute | solution.py:270
  78.6 13.8 %collective-permute-start.14 = (f32[4,6,8,256]{3,2,1,0:T(8,128)S(1)}, f32[4,6,8,256]{3,2,1,0:T(8,128)S(1)}, u32[]{:S(2)}, u32[]{:S(2)}) collective-permute-start(f32[4,6,8,256]{3,2,1,0:T(8,128)S(1)} %pad_maximum_fusion.refs_0_), channel_id=1, source_target_pairs={{0,32},{32,0},{64,96},{96,64},{128,160},{160,128},{192,224},{224,1... | collective-permute-start | bytes 589832 | tf_op jit(solution)/shard_map/ppermute | solution.py:271
  84.3 8.1 %collective-permute-start.17 = (f32[4,6,8,256]{3,2,1,0:T(8,128)S(1)}, f32[4,6,8,256]{3,2,1,0:T(8,128)S(1)}, u32[]{:S(2)}, u32[]{:S(2)}) collective-permute-start(f32[4,6,8,256]{3,2,1,0:T(8,128)S(1)} %collective-permute-done.13.refs_3_), channel_id=1, source_target_pairs={{0,32},{32,0},{64,96},{96,64},{128,160},{160,128},{192,224},{224,1... | collective-permute-start | bytes 589832 | tf_op jit(solution)/shard_map/ppermute | solution.py:271
  88.6 3.8 %collective-permute-start.16 = (f32[4,6,8,256]{3,2,1,0:T(8,128)S(1)}, f32[4,6,8,256]{3,2,1,0:T(8,128)S(1)}, u32[]{:S(2)}, u32[]{:S(2)}) collective-permute-start(f32[4,6,8,256]{3,2,1,0:T(8,128)S(1)} %collective-permute-done.12.refs_2_), channel_id=1, source_target_pairs={{0,32},{32,0},{64,96},{96,64},{128,160},{160,128},{192,224},{224,1... | collective-permute-start | bytes 589832 | tf_op jit(solution)/shard_map/ppermute | solution.py:271
  90.6 2.8 %collective-permute-start.15 = (f32[4,6,8,256]{3,2,1,0:T(8,128)S(1)}, f32[4,6,8,256]{3,2,1,0:T(8,128)S(1)}, u32[]{:S(2)}, u32[]{:S(2)}) collective-permute-start(f32[4,6,8,256]{3,2,1,0:T(8,128)S(1)} %collective-permute-done.11.refs_1_), channel_id=1, source_target_pairs={{0,32},{32,0},{64,96},{96,64},{128,160},{160,128},{192,224},{224,1... | collective-permute-start | bytes 589832 | tf_op jit(solution)/shard_map/ppermute | solution.py:271
  93.4 1.4 copy-start.2
  144.8 2.8 %copy-start = (f32[96,32,512]{2,1,0:T(8,128)S(1)}, f32[96,32,512]{2,1,0:T(8,128)}, u32[]{:S(2)}) copy-start(f32[96,32,512]{2,1,0:T(8,128)} %all-gather.5.cloned.1.call-done) | copy-start | bytes 18874372
  147.6 2.2 %copy-start.1 = (f32[8,256,2,256]{3,2,1,0:T(2,128)S(1)}, f32[8,256,2,256]{3,2,1,0:T(2,128)}, u32[]{:S(2)}) copy-start(f32[8,256,2,256]{3,2,1,0:T(2,128)} %a_ref.1) | copy-start | bytes 12582916
Sparse Core Ops, SparseCore 0:
  24.0 29.7 all-gather.6
  56.4 88.4 all-gather.4

commit v2 on v1

--- a/solution.py
+++ b/solution.py
@@ -9,7 +9,7 @@
 
 B = 256
 BAND = 32
-PIV = 4
+PIV = 8
 PAIRS = tuple((k, j) for k in range(3) for j in range(k, 3))
 HIGHEST = lax.Precision.HIGHEST
 F32 = jnp.float32
@@ -29,6 +29,11 @@
 def split(a):
     hi = a.astype(BF16)
     return hi, (a - hi.astype(F32)).astype(BF16)
+
+
+def product(a, b):
+    mul = functools.partial(jnp.dot, preferred_element_type=F32)
+    return mul(a[0], b[0]) + (mul(a[0], b[1]) + mul(a[1], b[0]))
 
 
 def band_eliminate(rows, band):
@@ -86,7 +91,7 @@
 def factor_tile(g_ref):
     for band in range(B // BAND):
         lo = band * BAND
-        chunks = (0, 1, 2) if band < 4 else (1, 2, 3)
+        chunks = (0, 1, 2) if lo < 128 else (1, 2, 3)
         rows = [
             {c: g_ref[lo + 8 * s : lo + 8 * s + 8, 128 * c : 128 * c + 128] for c in chunks}
             for s in range(BAND // 8)
@@ -105,9 +110,18 @@
                 g_ref[hi + BAND : B, left:right] -= dot(turned[hi + BAND : B], done)
 
 
+def upper_mask():
+    return lax.broadcasted_iota(jnp.int32, (B, B), 0) <= lax.broadcasted_iota(jnp.int32, (B, B), 1)
+
+
+def unit():
+    rows = lax.broadcasted_iota(jnp.int32, (B, B), 0)
+    return jnp.where(rows == lax.broadcasted_iota(jnp.int32, (B, B), 1), 1.0, 0.0).astype(F32)
+
+
 def factor_kernel(place_ref, *refs):
     own, other = refs[0:4], refs[4:8]
-    panel_ref, zhi_ref, zlo_ref, diag_ref, t_ref, g_ref, v_ref, lt_ref = refs[8:]
+    v_ref, x_ref, diag_ref, t_ref, g_ref, lt_ref = refs[8:]
     my_row, my_col = place_ref[0], place_ref[1]
     x, core = my_row // 2, my_row % 2
     y = my_col // 8
@@ -118,13 +132,6 @@
                 at = pl.multiple_of(base + ((y - step + 4) % 4) * 8, 8)
                 for n, (k, j) in enumerate(PAIRS):
                     t_ref[k, pl.ds(at, 8), j * B : (j + 1) * B] = bufs[shift][step, n]
-    for p in range(8):
-        for k in range(3):
-            t_ref[k, p * 32 : p * 32 + 32, 3 * B :] = panel_ref[p, k]
-    identity = jnp.where(
-        lax.broadcasted_iota(jnp.int32, (B, B), 0) == lax.broadcasted_iota(jnp.int32, (B, B), 1), 1.0, 0.0
-    ).astype(F32)
-    upper = lax.broadcasted_iota(jnp.int32, (B, B), 0) <= lax.broadcasted_iota(jnp.int32, (B, B), 1)
 
     def step(k, carry):
         for j in range(3):
@@ -133,11 +140,11 @@
             def _():
                 g_ref[:, 0:B] = t_ref[j, :, j * B : (j + 1) * B]
 
-        g_ref[:, B:] = identity
+        g_ref[:, B:] = unit()
         factor_tile(g_ref)
-        lt_ref[k] = jnp.where(upper, g_ref[:, 0:B], 0.0)
+        lt_ref[k] = jnp.where(upper_mask(), g_ref[:, 0:B], 0.0)
         v_ref[k] = g_ref[:, B:]
-        for j in range(3):
+        for j in range(2):
 
             @pl.when(k == j)
             def _():
@@ -152,91 +159,172 @@
         return carry
 
     lax.fori_loop(0, 3, step, 0)
-    for k in range(3):
-        t_ref[k, :, 3 * B : 4 * B] = jnp.where(
-            my_col == k, -identity, jnp.where(my_col < 3, 0.0, t_ref[k, :, 3 * B : 4 * B])
-        )
-    for k in (2, 1, 0):
-        rest = t_ref[k, :, 3 * B :]
-        for i in range(k + 1, 3):
-            rest -= dot(t_ref[k, :, i * B : (i + 1) * B], t_ref[i, :, 3 * B :])
-        z = dot_tn(v_ref[k], rest)
-        t_ref[k, :, 3 * B :] = z
-        hi, lo = split(z)
-        for p in range(8):
-            zhi_ref[p * 96 + k * 32 : p * 96 + k * 32 + 32, :] = hi[p * 32 : p * 32 + 32]
-            zlo_ref[p * 96 + k * 32 : p * 96 + k * 32 + 32, :] = lo[p * 32 : p * 32 + 32]
+    for n, (k, j) in enumerate(((0, 1), (0, 2), (1, 2))):
+        x_ref[n] = t_ref[k, :, j * B : (j + 1) * B]
     diag_ref[...] = lt_ref[jnp.minimum(my_col, 2)].T
 
 
-def factor(place, own, other, panel):
+def factor(place, own, other):
     vmem = pl.BlockSpec(memory_space=pltpu.VMEM)
     return pl.pallas_call(
         factor_kernel,
         out_shape=(
-            jax.ShapeDtypeStruct((3 * B, 2 * B), BF16),
-            jax.ShapeDtypeStruct((3 * B, 2 * B), BF16),
+            jax.ShapeDtypeStruct((3, B, B), F32),
+            jax.ShapeDtypeStruct((3, B, B), F32),
             jax.ShapeDtypeStruct((B, B), F32),
         ),
-        in_specs=[pl.BlockSpec(memory_space=pltpu.SMEM)] + [vmem] * 9,
+        in_specs=[pl.BlockSpec(memory_space=pltpu.SMEM)] + [vmem] * 8,
         out_specs=(vmem, vmem, vmem),
         scratch_shapes=[
-            pltpu.VMEM((3, B, 5 * B), F32),
+            pltpu.VMEM((3, B, 3 * B), F32),
             pltpu.VMEM((B, 2 * B), F32),
-            pltpu.VMEM((3, B, B), F32),
             pltpu.VMEM((3, B, B), F32),
         ],
         compiler_params=pltpu.CompilerParams(vmem_limit_bytes=40 * 2**20),
-        name="factor_panel",
-    )(place, *own, *other, panel)
-
-
-def update_kernel(place_ref, a_ref, u_ref, zhi_ref, zlo_ref, diag_ref, o_ref):
-    t = pl.program_id(0)
-    i = t * 8 + place_ref[0]
-    my_col = place_ref[1]
-    o_ref[...] = a_ref[...]
-
-    @pl.when(i >= my_col)
-    def _():
-        hi, lo = split(u_ref[...].reshape(3 * B, B).T)
-
-        def product(z):
-            zhi, zlo = zhi_ref[:, z], zlo_ref[:, z]
-            d = functools.partial(jnp.dot, preferred_element_type=F32)
-            return d(hi, zhi) + (d(hi, zlo) + d(lo, zhi))
-
-        panel = my_col < 3
-        base = jnp.where(panel, 0.0, a_ref[0, :, 0, :])
-        o_ref[0, :, 0, :] = base - product(slice(0, B))
-
-        @pl.when(i >= my_col + 32)
-        def _():
-            o_ref[0, :, 1, :] = a_ref[0, :, 1, :] - product(slice(B, 2 * B))
-
-        @pl.when(jnp.logical_and(i == my_col, panel))
-        def _():
-            o_ref[0, :, 0, :] = diag_ref[...]
+        cost_estimate=pl.CostEstimate(flops=30 * 10**9, bytes_accessed=10**7, transcendentals=0),
+        name="factor_corner",
+    )(place, *own, *other)
+
+
+def solve_kernel(place_ref, v_ref, x_ref, *refs):
+    pieces = refs[:8]
+    zhi_ref, zlo_ref, t_ref = refs[8:]
+    my_row, my_col = place_ref[0], place_ref[1]
+    x, core = my_row // 2, my_row % 2
+    for n in range(8):
+        source = ((x - n // 2 + 4) % 4) * 2 + (core if n % 2 == 0 else 1 - core)
+        at = pl.multiple_of(source * 32, 32)
+        for k in range(3):
+            t_ref[k, pl.ds(at, 32), :] = pieces[n][k]
+    above = {(0, 1): 0, (0, 2): 1, (1, 2): 2}
+    v = [split(v_ref[k]) for k in range(3)]
+    vt = [split(v_ref[k].T) for k in range(3)]
+    up = {key: split(x_ref[n]) for key, n in above.items()}
+    down = {key: split(x_ref[n].T) for key, n in above.items()}
+    sums = [t_ref[k] for k in range(3)]
+    for k in range(3):
+        sums[k] = product(v[k], split(sums[k]))
+        for i in range(k + 1, 3):
+            sums[i] = sums[i] - product(down[k, i], split(sums[k]))
+    for k in range(3):
+        left = jnp.where(my_col == k, -unit(), jnp.where(my_col < 3, 0.0, sums[k][:, :B]))
+        sums[k] = jnp.concatenate([left, sums[k][:, B:]], axis=1)
+    done = [None] * 3
+    for k in (2, 1, 0):
+        rest = sums[k]
+        for i in range(k + 1, 3):
+            rest = rest - product(up[k, i], done[i])
+        done[k] = split(product(vt[k], split(rest)))
+        for ref, part in ((zhi_ref, done[k][0]), (zlo_ref, done[k][1])):
+            for p in range(8):
+                ref[p * 96 + k * 32 : p * 96 + k * 32 + 32, :] = part[p * 32 : p * 32 + 32]
+
+
+def solve(place, v, x, pieces):
+    vmem = pl.BlockSpec(memory_space=pltpu.VMEM)
+    return pl.pallas_call(
+        solve_kernel,
+        out_shape=(
+            jax.ShapeDtypeStruct((3 * B, 2 * B), BF16),
+            jax.ShapeDtypeStruct((3 * B, 2 * B), BF16),
+        ),
+        in_specs=[pl.BlockSpec(memory_space=pltpu.SMEM)] + [vmem] * 10,
+        out_specs=(vmem, vmem),
+        scratch_shapes=[pltpu.VMEM((3, B, 2 * B), F32)],
+        compiler_params=pltpu.CompilerParams(vmem_limit_bytes=40 * 2**20),
+        cost_estimate=pl.CostEstimate(flops=3 * 10**9, bytes_accessed=10**7, transcendentals=0),
+        name="solve_columns",
+    )(place, v, x, *pieces)
+
+
+def update_kernel(place_ref, *refs):
+    zhi_hbm, zlo_hbm, diag_hbm, a_hbm, u_hbm, o_hbm, zhi_ref, zlo_ref, diag_ref, a_ref, u_ref, z_sem, a_sem, u_sem, o_sem = refs
+    my_row, my_col = place_ref[0], place_ref[1]
+    panel = my_col < 3
+    u_copies = [pltpu.make_async_copy(u_hbm.at[y], u_ref.at[y], u_sem.at[y]) for y in range(4)]
+    a_copies = [pltpu.make_async_copy(a_hbm.at[t], a_ref.at[t], a_sem.at[t]) for t in range(8)]
+    o_copies = [pltpu.make_async_copy(a_ref.at[t], o_hbm.at[t], o_sem.at[t]) for t in range(8)]
+    z_copies = [
+        pltpu.make_async_copy(zhi_hbm, zhi_ref, z_sem.at[0]),
+        pltpu.make_async_copy(zlo_hbm, zlo_ref, z_sem.at[1]),
+        pltpu.make_async_copy(diag_hbm, diag_ref, z_sem.at[2]),
+    ]
+    for copy in z_copies:
+        copy.start()
+    for y in range(4):
+        u_copies[y].start()
+        a_copies[y].start()
+        a_copies[y + 4].start()
+
+    for copy in z_copies:
+        copy.wait()
+    for y in range(4):
+        u_copies[y].wait()
+        for t in (y, y + 4):
+            i = t * 8 + my_row
+            a_copies[t].wait()
+
+            def write(u, change):
+                for half in range(2):
+                    at = pl.ds(2 * half + u, B, stride=4)
+                    base = a_ref[t, at, :]
+                    if u == 0:
+                        base = jnp.where(panel, 0.0, base)
+                    a_ref[t, at, :] = base - change[:, half * 128 : half * 128 + 128]
+
+            def turned():
+                return split(u_ref[y, :, t // 4 * B : t // 4 * B + B].T)
+
+            def left():
+                write(0, product(turned(), (zhi_ref[:, :B], zlo_ref[:, :B])))
+
+            if t < 4:
+                pl.when(i >= my_col)(left)
+
+                @pl.when(jnp.logical_and(i == my_col, panel))
+                def _():
+                    for half in range(2):
+                        a_ref[t, pl.ds(2 * half, B, stride=4), :] = diag_ref[:, half * 128 : half * 128 + 128]
+            else:
+                both = i >= my_col + 32
+
+                @pl.when(both)
+                def _():
+                    change = product(turned(), (zhi_ref[...], zlo_ref[...]))
+                    write(0, change[:, :B])
+                    write(1, change[:, B:])
+
+                pl.when(jnp.logical_not(both))(left)
+            o_copies[t].start()
+    for t in range(8):
+        o_copies[t].wait()
 
 
 def update(place, a, u, zhi, zlo, diag):
-    full = pl.BlockSpec(memory_space=pltpu.VMEM)
-    return pl.pallas_call(
+    hbm = pl.BlockSpec(memory_space=pltpu.HBM)
+    tiles, cols = a.shape[0], a.shape[2]
+    flat = a.reshape(tiles, B, cols, 2, 128).transpose(0, 1, 3, 2, 4).reshape(tiles, 4 * B, 128)
+    out = pl.pallas_call(
         update_kernel,
-        grid=(8,),
-        out_shape=jax.ShapeDtypeStruct(a.shape, F32),
-        in_specs=[
-            pl.BlockSpec(memory_space=pltpu.SMEM),
-            pl.BlockSpec((1, B, 2, B), lambda t: (t, 0, 0, 0)),
-            pl.BlockSpec((8, 3, 32, B), lambda t: (t % 4, 0, 0, t // 4)),
-            full,
-            full,
-            full,
+        out_shape=jax.ShapeDtypeStruct(flat.shape, F32),
+        in_specs=[pl.BlockSpec(memory_space=pltpu.SMEM)] + [hbm] * 5,
+        out_specs=hbm,
+        scratch_shapes=[
+            pltpu.VMEM((3 * B, 2 * B), BF16),
+            pltpu.VMEM((3 * B, 2 * B), BF16),
+            pltpu.VMEM((B, B), F32),
+            pltpu.VMEM((8, 4 * B, 128), F32),
+            pltpu.VMEM((4, 3 * B, 2 * B), F32),
+            pltpu.SemaphoreType.DMA((3,)),
+            pltpu.SemaphoreType.DMA((8,)),
+            pltpu.SemaphoreType.DMA((4,)),
+            pltpu.SemaphoreType.DMA((8,)),
         ],
-        out_specs=pl.BlockSpec((1, B, 2, B), lambda t: (t, 0, 0, 0)),
-        compiler_params=pltpu.CompilerParams(vmem_limit_bytes=40 * 2**20),
+        compiler_params=pltpu.CompilerParams(vmem_limit_bytes=58 * 2**20),
+        cost_estimate=pl.CostEstimate(flops=5 * 10**9, bytes_accessed=14 * 10**6, transcendentals=0),
         name="trailing_update",
-    )(place, a, u, zhi, zlo, diag)
+    )(place, zhi, zlo, diag, flat, u.reshape(4, 3 * B, 2 * B))
+    return out.reshape(tiles, B, 2, cols, 128).transpose(0, 1, 3, 2, 4).reshape(a.shape)
 
 
 def spread_corner(mine, my_col):
@@ -272,6 +360,15 @@
     return own, other
 
 
+def spread_columns(mine, after):
+    mine, _ = lax.optimization_barrier((mine, after))
+    pieces = []
+    for n in range(8):
+        pairs = [(r, (r // 2 + n // 2) % 4 * 2 + (r % 2) ^ (n % 2)) for r in range(8)]
+        pieces.append(mine if n == 0 else lax.ppermute(mine, "row", pairs))
+    return pieces
+
+
 def on_device(covariance):
     my_row, my_col = lax.axis_index("row"), lax.axis_index("col")
     place = jnp.stack([my_row, my_col]).astype(jnp.int32)
@@ -283,9 +380,10 @@
         [(r * 32 + y * 8 + z, z * 32 + y * 8 + r) for r in range(8) for y in range(4) for z in range(8)],
     )
     rows = lax.all_gather(turned, "col")
-    panel = lax.all_gather(mine, "row")
     own, other = spread_corner(mine[:, :, :B], my_col)
-    zhi, zlo, diag = factor(place, own, other, panel)
+    pieces = spread_columns(mine, own)
+    v, x, diag = factor(place, own, other)
+    zhi, zlo = solve(place, v, x, pieces)
     return update(place, covariance, rows, zhi, zlo, diag)
 
 

time: 167 us -> 158 us (0.946)
  Pallas kernels: 55.2 us -> 45.7 us
  local copies, waits for them, and re-layouts: 9.45 us -> 4.87 us
  starting transfers between devices: 56.1 us -> 59.9 us
  waiting for transfers between devices: 16.7 us -> 18.8 us
    pallas_call x2 -> x3, Pallas kernels: 55.2 us -> 45.7 us  [the longest x1 30 us: factor(): pl.pallas_call(factor_kernel, out_shape=(jax.ShapeDtypeStruct((3, B, B),...]
    ppermute x0 -> x7, waiting for transfers between devices: none -> 6.34 us  [spread_columns(): pieces.append(mine if n == 0 else lax.ppermute(mine, 'row', pairs))]
    ppermute x0 -> x7, starting transfers between devices: none -> 5.29 us  [spread_columns(): pieces.append(mine if n == 0 else lax.ppermute(mine, 'row', pairs))]
    all_gather x1, waiting for transfers between devices: 4.48 us -> 0.01 us  [on_device(): rows = lax.all_gather(turned, 'col')]
    unnamed x11 -> x13, local copies, waits for them, and re-layouts: 7.1 us -> 3.2 us
  transfers between devices with their start and end apart: 20 -> 26, of which waited for: 9 -> 9; matrix products, arithmetic and copies ran while one was open for 0% -> 0% of each run, Pallas kernels for 27% -> 22%
where the time goes in v2:
time: 158 us
  starting transfers between devices  59.9 us (38%)
  Pallas kernels  45.7 us (29%)
  waiting for transfers between devices  18.8 us (12%)
  blocking collectives  15 us (9%)
  between operations  13.7 us (9%)
  local copies, waits for them, and re-layouts  4.87 us (3%)
    pallas_call x1, Pallas kernels, factor(): pl.pallas_call(factor_kernel, out_shape=(jax.ShapeDtypeStruct((3, B, B),...  30 us
    all_to_all x1, blocking collectives, on_device(): mine = lax.all_to_all(top, 'row', 0, 0, tiled=True)[:3]  15 us
    ppermute x4, starting transfers between devices, spread_corner(): lax.ppermute(b, 'row', [(r, r ^ 1) for r in range(8)])  13.9 us
    pallas_call x1, Pallas kernels, update(): pl.pallas_call(update_kernel, out_shape=jax.ShapeDtypeStruct(flat.shape,...  11.1 us
    ppermute x1, starting transfers between devices, spread_corner(): lax.ppermute(got, 'col', [(h * 8 + j, h * 8 + j + 4) for h in range(4) fo...  10.6 us
    ppermute x3, starting transfers between devices, spread_corner(): stack.append(lax.ppermute(got, 'col', pairs))  8.46 us
    ppermute x3, starting transfers between devices, spread_corner(): lax.ppermute(block, 'row', [(r, (r + 2 * s) % 8) for r in range(8)])  7.11 us
    ppermute x3, starting transfers between devices, spread_corner(): lax.ppermute(quarter[:, d], 'col', [(j, d * 8 + j) for j in range(3)])  6.77 us
  transfers between devices with their start and end apart: 26, of which 9 were waited for; matrix products, arithmetic and copies ran while one was open for 0% of the time, Pallas kernels for 22%

profile of v2, /device:TPU:1, one launch (start us, length us, event | category | flops | bytes accessed | tf_op | source)
XLA Modules:
  0.0 158.2 jit_solution(11935148769998103878)
XLA Ops:
  6.5 0.0 all-gather.3.cloned.1.call-start
  6.5 1.2 slice.39
  7.8 0.4 reshape_squeeze.3
  8.2 15.0 %all_to_all.5 = f32[8,32,512]{2,1,0:T(8,128)S(1)} all-to-all(f32[8,32,512]{2,1,0:T(8,128)S(1)} %reshape_squeeze.3), channel_id=1, replica_groups=mesh['row'=8,'col'=32] {'row'}, dimensions={0} | all-to-all | bytes 1048576 | tf_op jit(solution)/shard_map/all_to_all | solution.py:376
  23.2 4.4 %collective-permute-start.24 = (f32[3,32,512]{2,1,0:T(8,128)S(1)}, f32[3,32,512]{2,1,0:T(8,128)S(1)}, u32[]{:S(2)}, u32[]{:S(2)}) collective-permute-start(f32[3,32,512]{2,1,0:T(8,128)S(1)} %slice.64.refs_0_), channel_id=1, source_target_pairs={{0,0},{1,32},{2,64},{3,96},{4,128},{5,160},{6,192},{7,224},{8,8},{... | collective-permute-start | bytes 589832 | tf_op jit(solution)/shard_map/ppermute | solution.py:377
  27.6 3.5 %collective-permute-done.24 = f32[3,32,512]{2,1,0:T(8,128)S(1)} collective-permute-done((f32[3,32,512]{2,1,0:T(8,128)S(1)}, f32[3,32,512]{2,1,0:T(8,128)S(1)}, u32[]{:S(2)}, u32[]{:S(2)}) %collective-permute-start.24) | collective-permute-done | bytes 196640 | tf_op jit(solution)/shard_map/ppermute | solution.py:377
  31.1 0.7 copy-done.4
  31.8 0.0 all-gather.3.cloned.1.call-update
  31.9 3.2 %collective-permute-start = (f32[3,8,256]{2,1,0:T(8,128)S(1)}, f32[3,8,256]{2,1,0:T(8,128)S(1)}, u32[]{:S(2)}, u32[]{:S(2)}) collective-permute-start(f32[3,8,256]{2,1,0:T(8,128)S(1)} %get-tuple-element.19), channel_id=1, source_target_pairs={{0,8},{1,9},{2,10},{32,40},{33,41},{34,42},{64,72},{65,73},{66,74}... | collective-permute-start | bytes 73736 | tf_op jit(solution)/shard_map/ppermute | solution.py:335
  35.1 2.3 %collective-permute-start.1 = (f32[3,8,256]{2,1,0:T(8,128)S(1)}, f32[3,8,256]{2,1,0:T(8,128)S(1)}, u32[]{:S(2)}, u32[]{:S(2)}) collective-permute-start(f32[3,8,256]{2,1,0:T(8,128)S(1)} %get-tuple-element.20), channel_id=1, source_target_pairs={{0,16},{1,17},{2,18},{32,48},{33,49},{34,50},{64,80},{65,81},{66,8... | collective-permute-start | bytes 73736 | tf_op jit(solution)/shard_map/ppermute | solution.py:335
  37.4 1.3 collective-permute-start.2
  38.7 0.0 collective-permute-done
  38.7 0.0 collective-permute-done.1
  38.7 0.9 collective-permute-done.2
  39.6 10.6 %collective-permute-start.3 = (f32[3,8,256]{2,1,0:T(8,128)S(1)}, f32[3,8,256]{2,1,0:T(8,128)S(1)}, u32[]{:S(2)}, u32[]{:S(2)}) collective-permute-start(f32[3,8,256]{2,1,0:T(8,128)S(1)} %fusion.5), channel_id=1, source_target_pairs={{0,4},{1,5},{2,6},{8,12},{9,13},{10,14},{16,20},{17,21},{18,22},{2... | collective-permute-start | bytes 73736 | tf_op jit(solution)/shard_map/ppermute | solution.py:337
  50.3 0.9 collective-permute-done.3
  51.2 1.9 %collective-permute-start.6 = (f32[3,8,256]{2,1,0:T(8,128)S(1)}, f32[3,8,256]{2,1,0:T(8,128)S(1)}, u32[]{:S(2)}, u32[]{:S(2)}) collective-permute-start(f32[3,8,256]{2,1,0:T(8,128)S(1)} %add.33), channel_id=1, source_target_pairs={{0,3},{1,0},{2,1},{4,7},{5,4},{6,5},{8,11},{9,8},{10,9},{12,15},{1... | collective-permute-start | bytes 73736 | tf_op jit(solution)/shard_map/ppermute | solution.py:343
  53.1 3.4 %collective-permute-start.5 = (f32[3,8,256]{2,1,0:T(8,128)S(1)}, f32[3,8,256]{2,1,0:T(8,128)S(1)}, u32[]{:S(2)}, u32[]{:S(2)}) collective-permute-start(f32[3,8,256]{2,1,0:T(8,128)S(1)} %add.33), channel_id=1, source_target_pairs={{0,1},{1,2},{2,3},{4,5},{5,6},{6,7},{8,9},{9,10},{10,11},{12,13},{... | collective-permute-start | bytes 73736 | tf_op jit(solution)/shard_map/ppermute | solution.py:343
  56.5 3.2 %collective-permute-start.4 = (f32[3,8,256]{2,1,0:T(8,128)S(1)}, f32[3,8,256]{2,1,0:T(8,128)S(1)}, u32[]{:S(2)}, u32[]{:S(2)}) collective-permute-start(f32[3,8,256]{2,1,0:T(8,128)S(1)} %add.33), channel_id=1, source_target_pairs={{0,2},{1,3},{2,0},{4,6},{5,7},{6,4},{8,10},{9,11},{10,8},{12,14},{... | collective-permute-start | bytes 73736 | tf_op jit(solution)/shard_map/ppermute | solution.py:343
  59.7 0.0 collective-permute-done.6
  59.7 0.0 collective-permute-done.5
  59.8 3.0 %collective-permute-done.4 = f32[3,8,256]{2,1,0:T(8,128)S(1)} collective-permute-done((f32[3,8,256]{2,1,0:T(8,128)S(1)}, f32[3,8,256]{2,1,0:T(8,128)S(1)}, u32[]{:S(2)}, u32[]{:S(2)}) %collective-permute-start.4) | collective-permute-done | bytes 24608 | tf_op jit(solution)/shard_map/ppermute | solution.py:343
  62.9 2.3 %collective-permute-start.9 = (f32[6,8,256]{2,1,0:T(8,128)S(1)}, f32[6,8,256]{2,1,0:T(8,128)S(1)}, u32[]{:S(2)}, u32[]{:S(2)}) collective-permute-start(f32[6,8,256]{2,1,0:T(8,128)S(1)} %slice_dynamic-update-slice_fusion), channel_id=1, source_target_pairs={{0,24},{1,25},{2,26},{3,27},{4,28},{5,29},{6,30},{7,31},{8,0},{9,1... | collective-permute-start | bytes 147464 | tf_op jit(solution)/shard_map/ppermute | solution.py:354
  65.1 0.4 collective-permute-start.8
  65.5 0.6 collective-permute-start.7
  66.2 0.2 collective-permute-done.9
  66.4 3.2 %collective-permute-done.8 = f32[6,8,256]{2,1,0:T(8,128)S(1)} collective-permute-done((f32[6,8,256]{2,1,0:T(8,128)S(1)}, f32[6,8,256]{2,1,0:T(8,128)S(1)}, u32[]{:S(2)}, u32[]{:S(2)}) %collective-permute-start.8) | collective-permute-done | bytes 49184 | tf_op jit(solution)/shard_map/ppermute | solution.py:354
  69.6 0.6 collective-permute-done.7
  70.3 6.4 %collective-permute-start.12 = (f32[4,6,8,256]{3,2,1,0:T(8,128)S(1)}, f32[4,6,8,256]{3,2,1,0:T(8,128)S(1)}, u32[]{:S(2)}, u32[]{:S(2)}) collective-permute-start(f32[4,6,8,256]{3,2,1,0:T(8,128)S(1)} %pad_maximum_fusion.refs_0_), channel_id=1, source_target_pairs={{0,192},{32,224},{64,0},{96,32},{128,64},{160,96},{192,128},{224,1... | collective-permute-start | bytes 589832 | tf_op jit(solution)/shard_map/ppermute | solution.py:358
  76.7 0.0 collective-permute-start.11
  76.7 0.7 collective-permute-start.10
  77.4 5.5 %collective-permute-start.13 = (f32[4,6,8,256]{3,2,1,0:T(8,128)S(1)}, f32[4,6,8,256]{3,2,1,0:T(8,128)S(1)}, u32[]{:S(2)}, u32[]{:S(2)}) collective-permute-start(f32[4,6,8,256]{3,2,1,0:T(8,128)S(1)} %pad_maximum_fusion.refs_0_), channel_id=1, source_target_pairs={{0,32},{32,0},{64,96},{96,64},{128,160},{160,128},{192,224},{224,1... | collective-permute-start | bytes 589832 | tf_op jit(solution)/shard_map/ppermute | solution.py:359
  82.9 0.0 collective-permute-done.12.refs_3_
  82.9 4.3 %collective-permute-start.16 = (f32[4,6,8,256]{3,2,1,0:T(8,128)S(1)}, f32[4,6,8,256]{3,2,1,0:T(8,128)S(1)}, u32[]{:S(2)}, u32[]{:S(2)}) collective-permute-start(f32[4,6,8,256]{3,2,1,0:T(8,128)S(1)} %collective-permute-done.12.refs_3_), channel_id=1, source_target_pairs={{0,32},{32,0},{64,96},{96,64},{128,160},{160,128},{192,224},{224,1... | collective-permute-start | bytes 589832 | tf_op jit(solution)/shard_map/ppermute | solution.py:359
  87.2 0.0 collective-permute-done.11.refs_2_
  87.2 0.0 collective-permute-done.10.refs_1_
  87.2 3.7 %collective-permute-start.15 = (f32[4,6,8,256]{3,2,1,0:T(8,128)S(1)}, f32[4,6,8,256]{3,2,1,0:T(8,128)S(1)}, u32[]{:S(2)}, u32[]{:S(2)}) collective-permute-start(f32[4,6,8,256]{3,2,1,0:T(8,128)S(1)} %collective-permute-done.11.refs_2_), channel_id=1, source_target_pairs={{0,32},{32,0},{64,96},{96,64},{128,160},{160,128},{192,224},{224,1... | collective-permute-start | bytes 589832 | tf_op jit(solution)/shard_map/ppermute | solution.py:359
  90.9 0.5 collective-permute-start.23
  91.4 0.1 collective-permute-start.22
  91.6 0.0 collective-permute-done.13.refs_4_
  91.6 0.4 collective-permute-start.14
  92.0 0.1 pad_add_fusion.place_ref
  92.0 0.0 collective-permute-done.16.refs_7_
  92.0 2.8 %collective-permute-start.21 = (f32[3,32,512]{2,1,0:T(8,128)S(1)}, f32[3,32,512]{2,1,0:T(8,128)S(1)}, u32[]{:S(2)}, u32[]{:S(2)}) collective-permute-start(f32[3,32,512]{2,1,0:T(8,128)S(1)} %slice.64.refs_0_), channel_id=1, source_target_pairs={{0,160},{32,128},{64,224},{96,192},{128,32},{160,0},{192,96},{224,... | collective-permute-start | bytes 589832 | tf_op jit(solution)/shard_map/ppermute | solution.py:368
  94.9 0.0 collective-permute-done.15.refs_6_
  94.9 0.2 collective-permute-start.20
  95.1 3.4 %collective-permute-done.23.refs_7_ = f32[3,32,512]{2,1,0:T(8,128)S(1)} collective-permute-done((f32[3,32,512]{2,1,0:T(8,128)S(1)}, f32[3,32,512]{2,1,0:T(8,128)S(1)}, u32[]{:S(2)}, u32[]{:S(2)}) %collective-permute-start.23) | collective-permute-done | bytes 196640 | tf_op jit(solution)/shard_map/ppermute | solution.py:368
  98.5 0.0 collective-permute-start.19
  98.5 2.9 %collective-permute-done.22.refs_6_ = f32[3,32,512]{2,1,0:T(8,128)S(1)} collective-permute-done((f32[3,32,512]{2,1,0:T(8,128)S(1)}, f32[3,32,512]{2,1,0:T(8,128)S(1)}, u32[]{:S(2)}, u32[]{:S(2)}) %collective-permute-start.22) | collective-permute-done | bytes 196640 | tf_op jit(solution)/shard_map/ppermute | solution.py:368
  101.4 0.0 collective-permute-start.18
  101.4 0.0 collective-permute-done.14.refs_5_
  101.4 1.6 collective-permute-start.17
  103.0 30.0 %factor_corner.1 = (f32[3,256,256]{2,1,0:T(8,128)S(1)}, f32[3,256,256]{2,1,0:T(8,128)S(1)}, f32[256,256]{1,0:T(8,128)S(1)}) custom-call(s32[2]{0:T(128)S(1)} %pad_add_fusion.place_ref, f32[4,6,8,256]{3,2,1,0:T(8,128)S(1)} %pad_maximum_fusion.refs_0_, f32[4,6,8,256]{3,2,1,0:T(8,128)S(1)} %collective-permute-done.10.refs_1_, ...), custom_call_target="tpu_custom_call" | custom-call | flops 30000001024 | bytes 10000000 | tf_op jit(solution)/shard_map/factor_corner/pallas_call | solution.py:169
  133.0 0.7 copy-done.3
  133.8 0.0 collective-permute-done.21.refs_5_
  133.8 0.0 collective-permute-done.20.refs_4_
  133.8 0.0 collective-permute-done.19.refs_3_
  133.8 0.0 collective-permute-done.18.refs_2_
  133.8 0.0 collective-permute-done.17.refs_1_
  133.8 4.5 %solve_columns.1 = (bf16[768,512]{1,0:T(8,128)(2,1)S(1)}, bf16[768,512]{1,0:T(8,128)(2,1)S(1)}) custom-call(s32[2]{0:T(128)S(1)} %pad_add_fusion.place_ref, f32[3,256,256]{2,1,0:T(8,128)S(1)} %get-tuple-element.11.v_ref, f32[3,256,256]{2,1,0:T(8,128)S(1)} %get-tuple-element.12.x_ref, f32[3,32,512]{2,1,0:T(8,128)S(1)} %slice.64.refs_0_, ...), custom_call_target="tpu_custom_call" | custom-call | flops 3000000000 | bytes 10000000 | tf_op jit(solution)/shard_map/solve_columns/pallas_call | solution.py:225
  138.3 0.0 copy-start.1
  138.4 0.9 copy-done.1
  139.2 0.9 copy-done.2
  140.1 11.1 %trailing_update.1 = f32[8,1024,128]{2,1,0:T(8,128)} custom-call(s32[2]{0:T(128)} %copy-done, bf16[768,512]{1,0:T(8,128)(2,1)} %copy-done.1, bf16[768,512]{1,0:T(8,128)(2,1)} %copy-done.2, f32[256,256]{1,0:T(8,128)} %copy-done.3, f32[8,1024,128]{2,1,0:T(8,128)} %bitcast.56, f32[4,768,512]{2,1,0:T(8,128)} %bitcast.60), custom_call_target="tpu_custom_call" | custom-call | flops 5000000000 | bytes 14000000 | tf_op jit(solution)/shard_map/trailing_update/pallas_call | solution.py:307
  (18 shorter events, 0.1 us)
Async XLA Ops:
  6.5 133.6 %all-gather.3.cloned.1.call-start = ((), (), s32[]{:S(2)}) async-start(), calls=%async_computation.1 | async-start | bytes 6488064 | tf_op jit(solution)/shard_map/all_gather | solution.py:382
  23.2 7.9 %collective-permute-start.24 = (f32[3,32,512]{2,1,0:T(8,128)S(1)}, f32[3,32,512]{2,1,0:T(8,128)S(1)}, u32[]{:S(2)}, u32[]{:S(2)}) collective-permute-start(f32[3,32,512]{2,1,0:T(8,128)S(1)} %slice.64.refs_0_), channel_id=1, source_target_pairs={{0,0},{1,32},{2,64},{3,96},{4,128},{5,160},{6,192},{7,224},{8,8},{... | collective-permute-start | bytes 589832 | tf_op jit(solution)/shard_map/ppermute | solution.py:377
  31.1 0.7 copy-start.4
  31.9 6.8 %collective-permute-start = (f32[3,8,256]{2,1,0:T(8,128)S(1)}, f32[3,8,256]{2,1,0:T(8,128)S(1)}, u32[]{:S(2)}, u32[]{:S(2)}) collective-permute-start(f32[3,8,256]{2,1,0:T(8,128)S(1)} %get-tuple-element.19), channel_id=1, source_target_pairs={{0,8},{1,9},{2,10},{32,40},{33,41},{34,42},{64,72},{65,73},{66,74}... | collective-permute-start | bytes 73736 | tf_op jit(solution)/shard_map/ppermute | solution.py:335
  35.1 3.6 %collective-permute-start.1 = (f32[3,8,256]{2,1,0:T(8,128)S(1)}, f32[3,8,256]{2,1,0:T(8,128)S(1)}, u32[]{:S(2)}, u32[]{:S(2)}) collective-permute-start(f32[3,8,256]{2,1,0:T(8,128)S(1)} %get-tuple-element.20), channel_id=1, source_target_pairs={{0,16},{1,17},{2,18},{32,48},{33,49},{34,50},{64,80},{65,81},{66,8... | collective-permute-start | bytes 73736 | tf_op jit(solution)/shard_map/ppermute | solution.py:335
  37.4 2.2 %collective-permute-start.2 = (f32[3,8,256]{2,1,0:T(8,128)S(1)}, f32[3,8,256]{2,1,0:T(8,128)S(1)}, u32[]{:S(2)}, u32[]{:S(2)}) collective-permute-start(f32[3,8,256]{2,1,0:T(8,128)S(1)} %get-tuple-element.21), channel_id=1, source_target_pairs={{0,24},{1,25},{2,26},{32,56},{33,57},{34,58},{64,88},{65,89},{66,9... | collective-permute-start | bytes 73736 | tf_op jit(solution)/shard_map/ppermute | solution.py:335
  39.6 11.6 %collective-permute-start.3 = (f32[3,8,256]{2,1,0:T(8,128)S(1)}, f32[3,8,256]{2,1,0:T(8,128)S(1)}, u32[]{:S(2)}, u32[]{:S(2)}) collective-permute-start(f32[3,8,256]{2,1,0:T(8,128)S(1)} %fusion.5), channel_id=1, source_target_pairs={{0,4},{1,5},{2,6},{8,12},{9,13},{10,14},{16,20},{17,21},{18,22},{2... | collective-permute-start | bytes 73736 | tf_op jit(solution)/shard_map/ppermute | solution.py:337
  51.2 8.5 %collective-permute-start.6 = (f32[3,8,256]{2,1,0:T(8,128)S(1)}, f32[3,8,256]{2,1,0:T(8,128)S(1)}, u32[]{:S(2)}, u32[]{:S(2)}) collective-permute-start(f32[3,8,256]{2,1,0:T(8,128)S(1)} %add.33), channel_id=1, source_target_pairs={{0,3},{1,0},{2,1},{4,7},{5,4},{6,5},{8,11},{9,8},{10,9},{12,15},{1... | collective-permute-start | bytes 73736 | tf_op jit(solution)/shard_map/ppermute | solution.py:343
  53.1 6.6 %collective-permute-start.5 = (f32[3,8,256]{2,1,0:T(8,128)S(1)}, f32[3,8,256]{2,1,0:T(8,128)S(1)}, u32[]{:S(2)}, u32[]{:S(2)}) collective-permute-start(f32[3,8,256]{2,1,0:T(8,128)S(1)} %add.33), channel_id=1, source_target_pairs={{0,1},{1,2},{2,3},{4,5},{5,6},{6,7},{8,9},{9,10},{10,11},{12,13},{... | collective-permute-start | bytes 73736 | tf_op jit(solution)/shard_map/ppermute | solution.py:343
  56.5 6.3 %collective-permute-start.4 = (f32[3,8,256]{2,1,0:T(8,128)S(1)}, f32[3,8,256]{2,1,0:T(8,128)S(1)}, u32[]{:S(2)}, u32[]{:S(2)}) collective-permute-start(f32[3,8,256]{2,1,0:T(8,128)S(1)} %add.33), channel_id=1, source_target_pairs={{0,2},{1,3},{2,0},{4,6},{5,7},{6,4},{8,10},{9,11},{10,8},{12,14},{... | collective-permute-start | bytes 73736 | tf_op jit(solution)/shard_map/ppermute | solution.py:343
  62.9 3.5 %collective-permute-start.9 = (f32[6,8,256]{2,1,0:T(8,128)S(1)}, f32[6,8,256]{2,1,0:T(8,128)S(1)}, u32[]{:S(2)}, u32[]{:S(2)}) collective-permute-start(f32[6,8,256]{2,1,0:T(8,128)S(1)} %slice_dynamic-update-slice_fusion), channel_id=1, source_target_pairs={{0,24},{1,25},{2,26},{3,27},{4,28},{5,29},{6,30},{7,31},{8,0},{9,1... | collective-permute-start | bytes 147464 | tf_op jit(solution)/shard_map/ppermute | solution.py:354
  65.1 4.5 %collective-permute-start.8 = (f32[6,8,256]{2,1,0:T(8,128)S(1)}, f32[6,8,256]{2,1,0:T(8,128)S(1)}, u32[]{:S(2)}, u32[]{:S(2)}) collective-permute-start(f32[6,8,256]{2,1,0:T(8,128)S(1)} %slice_dynamic-update-slice_fusion), channel_id=1, source_target_pairs={{0,16},{1,17},{2,18},{3,19},{4,20},{5,21},{6,22},{7,23},{8,24},{9,... | collective-permute-start | bytes 147464 | tf_op jit(solution)/shard_map/ppermute | solution.py:354
  65.5 4.7 %collective-permute-start.7 = (f32[6,8,256]{2,1,0:T(8,128)S(1)}, f32[6,8,256]{2,1,0:T(8,128)S(1)}, u32[]{:S(2)}, u32[]{:S(2)}) collective-permute-start(f32[6,8,256]{2,1,0:T(8,128)S(1)} %slice_dynamic-update-slice_fusion), channel_id=1, source_target_pairs={{0,8},{1,9},{2,10},{3,11},{4,12},{5,13},{6,14},{7,15},{8,16},{9,17... | collective-permute-start | bytes 147464 | tf_op jit(solution)/shard_map/ppermute | solution.py:354
  70.3 12.6 %collective-permute-start.12 = (f32[4,6,8,256]{3,2,1,0:T(8,128)S(1)}, f32[4,6,8,256]{3,2,1,0:T(8,128)S(1)}, u32[]{:S(2)}, u32[]{:S(2)}) collective-permute-start(f32[4,6,8,256]{3,2,1,0:T(8,128)S(1)} %pad_maximum_fusion.refs_0_), channel_id=1, source_target_pairs={{0,192},{32,224},{64,0},{96,32},{128,64},{160,96},{192,128},{224,1... | collective-permute-start | bytes 589832 | tf_op jit(solution)/shard_map/ppermute | solution.py:358
  76.7 10.5 %collective-permute-start.11 = (f32[4,6,8,256]{3,2,1,0:T(8,128)S(1)}, f32[4,6,8,256]{3,2,1,0:T(8,128)S(1)}, u32[]{:S(2)}, u32[]{:S(2)}) collective-permute-start(f32[4,6,8,256]{3,2,1,0:T(8,128)S(1)} %pad_maximum_fusion.refs_0_), channel_id=1, source_target_pairs={{0,128},{32,160},{64,192},{96,224},{128,0},{160,32},{192,64},{224,... | collective-permute-start | bytes 589832 | tf_op jit(solution)/shard_map/ppermute | solution.py:358
  76.7 10.5 %collective-permute-start.10 = (f32[4,6,8,256]{3,2,1,0:T(8,128)S(1)}, f32[4,6,8,256]{3,2,1,0:T(8,128)S(1)}, u32[]{:S(2)}, u32[]{:S(2)}) collective-permute-start(f32[4,6,8,256]{3,2,1,0:T(8,128)S(1)} %pad_maximum_fusion.refs_0_), channel_id=1, source_target_pairs={{0,64},{32,96},{64,128},{96,160},{128,192},{160,224},{192,0},{224,... | collective-permute-start | bytes 589832 | tf_op jit(solution)/shard_map/ppermute | solution.py:358
  77.4 14.2 %collective-permute-start.13 = (f32[4,6,8,256]{3,2,1,0:T(8,128)S(1)}, f32[4,6,8,256]{3,2,1,0:T(8,128)S(1)}, u32[]{:S(2)}, u32[]{:S(2)}) collective-permute-start(f32[4,6,8,256]{3,2,1,0:T(8,128)S(1)} %pad_maximum_fusion.refs_0_), channel_id=1, source_target_pairs={{0,32},{32,0},{64,96},{96,64},{128,160},{160,128},{192,224},{224,1... | collective-permute-start | bytes 589832 | tf_op jit(solution)/shard_map/ppermute | solution.py:359
  82.9 9.1 %collective-permute-start.16 = (f32[4,6,8,256]{3,2,1,0:T(8,128)S(1)}, f32[4,6,8,256]{3,2,1,0:T(8,128)S(1)}, u32[]{:S(2)}, u32[]{:S(2)}) collective-permute-start(f32[4,6,8,256]{3,2,1,0:T(8,128)S(1)} %collective-permute-done.12.refs_3_), channel_id=1, source_target_pairs={{0,32},{32,0},{64,96},{96,64},{128,160},{160,128},{192,224},{224,1... | collective-permute-start | bytes 589832 | tf_op jit(solution)/shard_map/ppermute | solution.py:359
  87.2 7.6 %collective-permute-start.15 = (f32[4,6,8,256]{3,2,1,0:T(8,128)S(1)}, f32[4,6,8,256]{3,2,1,0:T(8,128)S(1)}, u32[]{:S(2)}, u32[]{:S(2)}) collective-permute-start(f32[4,6,8,256]{3,2,1,0:T(8,128)S(1)} %collective-permute-done.11.refs_2_), channel_id=1, source_target_pairs={{0,32},{32,0},{64,96},{96,64},{128,160},{160,128},{192,224},{224,1... | collective-permute-start | bytes 589832 | tf_op jit(solution)/shard_map/ppermute | solution.py:359
  90.9 7.6 %collective-permute-start.23 = (f32[3,32,512]{2,1,0:T(8,128)S(1)}, f32[3,32,512]{2,1,0:T(8,128)S(1)}, u32[]{:S(2)}, u32[]{:S(2)}) collective-permute-start(f32[3,32,512]{2,1,0:T(8,128)S(1)} %slice.64.refs_0_), channel_id=1, source_target_pairs={{0,224},{32,192},{64,32},{96,0},{128,96},{160,64},{192,160},{224,1... | collective-permute-start | bytes 589832 | tf_op jit(solution)/shard_map/ppermute | solution.py:368
  91.4 10.0 %collective-permute-start.22 = (f32[3,32,512]{2,1,0:T(8,128)S(1)}, f32[3,32,512]{2,1,0:T(8,128)S(1)}, u32[]{:S(2)}, u32[]{:S(2)}) collective-permute-start(f32[3,32,512]{2,1,0:T(8,128)S(1)} %slice.64.refs_0_), channel_id=1, source_target_pairs={{0,192},{32,224},{64,0},{96,32},{128,64},{160,96},{192,128},{224,1... | collective-permute-start | bytes 589832 | tf_op jit(solution)/shard_map/ppermute | solution.py:368
  91.6 9.8 %collective-permute-start.14 = (f32[4,6,8,256]{3,2,1,0:T(8,128)S(1)}, f32[4,6,8,256]{3,2,1,0:T(8,128)S(1)}, u32[]{:S(2)}, u32[]{:S(2)}) collective-permute-start(f32[4,6,8,256]{3,2,1,0:T(8,128)S(1)} %collective-permute-done.10.refs_1_), channel_id=1, source_target_pairs={{0,32},{32,0},{64,96},{96,64},{128,160},{160,128},{192,224},{224,1... | collective-permute-start | bytes 589832 | tf_op jit(solution)/shard_map/ppermute | solution.py:359
  92.0 41.8 %copy-start = (s32[2]{0:T(128)}, s32[2]{0:T(128)S(1)}, u32[]{:S(2)}) copy-start(s32[2]{0:T(128)S(1)} %pad_add_fusion.place_ref) | copy-start | bytes 28
  92.0 41.7 %collective-permute-start.21 = (f32[3,32,512]{2,1,0:T(8,128)S(1)}, f32[3,32,512]{2,1,0:T(8,128)S(1)}, u32[]{:S(2)}, u32[]{:S(2)}) collective-permute-start(f32[3,32,512]{2,1,0:T(8,128)S(1)} %slice.64.refs_0_), channel_id=1, source_target_pairs={{0,160},{32,128},{64,224},{96,192},{128,32},{160,0},{192,96},{224,... | collective-permute-start | bytes 589832 | tf_op jit(solution)/shard_map/ppermute | solution.py:368
  94.9 38.9 %collective-permute-start.20 = (f32[3,32,512]{2,1,0:T(8,128)S(1)}, f32[3,32,512]{2,1,0:T(8,128)S(1)}, u32[]{:S(2)}, u32[]{:S(2)}) collective-permute-start(f32[3,32,512]{2,1,0:T(8,128)S(1)} %slice.64.refs_0_), channel_id=1, source_target_pairs={{0,128},{32,160},{64,192},{96,224},{128,0},{160,32},{192,64},{224,... | collective-permute-start | bytes 589832 | tf_op jit(solution)/shard_map/ppermute | solution.py:368
  98.5 35.3 %collective-permute-start.19 = (f32[3,32,512]{2,1,0:T(8,128)S(1)}, f32[3,32,512]{2,1,0:T(8,128)S(1)}, u32[]{:S(2)}, u32[]{:S(2)}) collective-permute-start(f32[3,32,512]{2,1,0:T(8,128)S(1)} %slice.64.refs_0_), channel_id=1, source_target_pairs={{0,96},{32,64},{64,160},{96,128},{128,224},{160,192},{192,32},{224... | collective-permute-start | bytes 589832 | tf_op jit(solution)/shard_map/ppermute | solution.py:368
  101.4 32.4 %collective-permute-start.18 = (f32[3,32,512]{2,1,0:T(8,128)S(1)}, f32[3,32,512]{2,1,0:T(8,128)S(1)}, u32[]{:S(2)}, u32[]{:S(2)}) collective-permute-start(f32[3,32,512]{2,1,0:T(8,128)S(1)} %slice.64.refs_0_), channel_id=1, source_target_pairs={{0,64},{32,96},{64,128},{96,160},{128,192},{160,224},{192,0},{224,... | collective-permute-start | bytes 589832 | tf_op jit(solution)/shard_map/ppermute | solution.py:368
  101.4 32.4 %collective-permute-start.17 = (f32[3,32,512]{2,1,0:T(8,128)S(1)}, f32[3,32,512]{2,1,0:T(8,128)S(1)}, u32[]{:S(2)}, u32[]{:S(2)}) collective-permute-start(f32[3,32,512]{2,1,0:T(8,128)S(1)} %slice.64.refs_0_), channel_id=1, source_target_pairs={{0,32},{32,0},{64,96},{96,64},{128,160},{160,128},{192,224},{224,1... | collective-permute-start | bytes 589832 | tf_op jit(solution)/shard_map/ppermute | solution.py:368
  133.0 0.7 copy-start.3
  138.3 0.9 copy-start.1
  139.2 0.9 copy-start.2
Sparse Core Ops, SparseCore 0:
  32.0 101.5 all-gather.2

commit v3 on v2

--- a/solution.py
+++ b/solution.py
@@ -238,28 +238,24 @@
 
 
 def update_kernel(place_ref, *refs):
-    zhi_hbm, zlo_hbm, diag_hbm, a_hbm, u_hbm, o_hbm, zhi_ref, zlo_ref, diag_ref, a_ref, u_ref, z_sem, a_sem, u_sem, o_sem = refs
+    zhi_ref, zlo_ref, diag_ref, a_hbm, u_hbm, o_hbm, a_ref, u_ref, a_sem, u_sem, o_sem = refs
     my_row, my_col = place_ref[0], place_ref[1]
     panel = my_col < 3
     u_copies = [pltpu.make_async_copy(u_hbm.at[y], u_ref.at[y], u_sem.at[y]) for y in range(4)]
     a_copies = [pltpu.make_async_copy(a_hbm.at[t], a_ref.at[t], a_sem.at[t]) for t in range(8)]
     o_copies = [pltpu.make_async_copy(a_ref.at[t], o_hbm.at[t], o_sem.at[t]) for t in range(8)]
-    z_copies = [
-        pltpu.make_async_copy(zhi_hbm, zhi_ref, z_sem.at[0]),
-        pltpu.make_async_copy(zlo_hbm, zlo_ref, z_sem.at[1]),
-        pltpu.make_async_copy(diag_hbm, diag_ref, z_sem.at[2]),
-    ]
-    for copy in z_copies:
-        copy.start()
-    for y in range(4):
+
+    def fetch(y):
         u_copies[y].start()
         a_copies[y].start()
         a_copies[y + 4].start()
 
-    for copy in z_copies:
-        copy.wait()
+    fetch(0)
+    fetch(1)
     for y in range(4):
         u_copies[y].wait()
+        if y < 2:
+            fetch(y + 2)
         for t in (y, y + 4):
             i = t * 8 + my_row
             a_copies[t].wait()
@@ -301,26 +297,23 @@
 
 
 def update(place, a, u, zhi, zlo, diag):
+    vmem = pl.BlockSpec(memory_space=pltpu.VMEM)
     hbm = pl.BlockSpec(memory_space=pltpu.HBM)
     tiles, cols = a.shape[0], a.shape[2]
     flat = a.reshape(tiles, B, cols, 2, 128).transpose(0, 1, 3, 2, 4).reshape(tiles, 4 * B, 128)
     out = pl.pallas_call(
         update_kernel,
         out_shape=jax.ShapeDtypeStruct(flat.shape, F32),
-        in_specs=[pl.BlockSpec(memory_space=pltpu.SMEM)] + [hbm] * 5,
+        in_specs=[pl.BlockSpec(memory_space=pltpu.SMEM), vmem, vmem, vmem, hbm, hbm],
         out_specs=hbm,
         scratch_shapes=[
-            pltpu.VMEM((3 * B, 2 * B), BF16),
-            pltpu.VMEM((3 * B, 2 * B), BF16),
-            pltpu.VMEM((B, B), F32),
             pltpu.VMEM((8, 4 * B, 128), F32),
             pltpu.VMEM((4, 3 * B, 2 * B), F32),
-            pltpu.SemaphoreType.DMA((3,)),
             pltpu.SemaphoreType.DMA((8,)),
             pltpu.SemaphoreType.DMA((4,)),
             pltpu.SemaphoreType.DMA((8,)),
         ],
-        compiler_params=pltpu.CompilerParams(vmem_limit_bytes=58 * 2**20),
+        compiler_params=pltpu.CompilerParams(vmem_limit_bytes=49 * 2**20),
         cost_estimate=pl.CostEstimate(flops=5 * 10**9, bytes_accessed=14 * 10**6, transcendentals=0),
         name="trailing_update",
     )(place, zhi, zlo, diag, flat, u.reshape(4, 3 * B, 2 * B))
@@ -334,6 +327,7 @@
     for d in range(1, 4):
         got = got + lax.ppermute(quarter[:, d], "col", [(j, d * 8 + j) for j in range(3)])
     got = jnp.where(z < 3, got, 0.0)
+    first = got
     got = got + lax.ppermute(got, "col", [(h * 8 + j, h * 8 + j + 4) for h in range(4) for j in range(3)])
     stack = [got]
     for s in range(1, 4):
@@ -357,7 +351,7 @@
     for s in range(1, 4):
         own.append(lax.ppermute(block, "row", [(r, (r + 2 * s) % 8) for r in range(8)]))
     other = [lax.ppermute(b, "row", [(r, r ^ 1) for r in range(8)]) for b in own]
-    return own, other
+    return own, other, first
 
 
 def spread_columns(mine, after):
@@ -380,8 +374,8 @@
         [(r * 32 + y * 8 + z, z * 32 + y * 8 + r) for r in range(8) for y in range(4) for z in range(8)],
     )
     rows = lax.all_gather(turned, "col")
-    own, other = spread_corner(mine[:, :, :B], my_col)
-    pieces = spread_columns(mine, own)
+    own, other, first = spread_corner(mine[:, :, :B], my_col)
+    pieces = spread_columns(mine, first)
     v, x, diag = factor(place, own, other)
     zhi, zlo = solve(place, v, x, pieces)
     return update(place, covariance, rows, zhi, zlo, diag)

time: 158 us -> 150 us (0.949)
  waiting for transfers between devices: 18.8 us -> 10.3 us
  starting transfers between devices: 59.9 us -> 64.4 us
  local copies, waits for them, and re-layouts: 4.87 us -> 2.36 us
  Pallas kernels: 45.7 us -> 43.4 us
    ppermute x7, starting transfers between devices: 5.29 us -> 18.9 us  [spread_columns(): pieces.append(mine if n == 0 else lax.ppermute(mine, 'row', pairs))]
    ppermute x7, waiting for transfers between devices: 6.34 us -> 0.47 us  [spread_columns(): pieces.append(mine if n == 0 else lax.ppermute(mine, 'row', pairs))]
    ppermute x3, starting transfers between devices: 7.11 us -> 1.53 us  [spread_corner(): lax.ppermute(block, 'row', [(r, (r + 2 * s) % 8) for r in range(8)])]
    ppermute x3, waiting for transfers between devices: 4.09 us -> 0.01 us  [spread_corner(): lax.ppermute(part, 'col', [(c, (c + 8 * s) % 32) for c in range(32)])]
    ppermute x4, starting transfers between devices: 13.9 us -> 10.4 us  [spread_corner(): lax.ppermute(b, 'row', [(r, r ^ 1) for r in range(8)])]
    unnamed x13 -> x5, local copies, waits for them, and re-layouts: 3.2 us -> 0.69 us
    pallas_call x1, Pallas kernels: 11.1 us -> 8.92 us  [update(): pl.pallas_call(update_kernel, out_shape=jax.ShapeDtypeStruct(flat.shape,...]
  transfers between devices with their start and end apart: 26 -> 26, of which waited for: 9 -> 6; matrix products, arithmetic and copies ran while one was open for 0% -> 0% of each run, Pallas kernels for 22% -> 23%
where the time goes in v3:
time: 150 us; the launch traced here: 149 us
  starting transfers between devices  64.4 us (43%)
  Pallas kernels  43.4 us (29%)
  blocking collectives  15 us (10%)
  between operations  13.8 us (9%)
  waiting for transfers between devices  10.3 us (7%)
  local copies, waits for them, and re-layouts  2.36 us (2%)
    pallas_call x1, Pallas kernels, factor(): pl.pallas_call(factor_kernel, out_shape=(jax.ShapeDtypeStruct((3, B, B),...  30 us
    ppermute x7, starting transfers between devices, spread_columns(): pieces.append(mine if n == 0 else lax.ppermute(mine, 'row', pairs))  18.9 us
    all_to_all x1, blocking collectives, on_device(): mine = lax.all_to_all(top, 'row', 0, 0, tiled=True)[:3]  15 us
    ppermute x1, starting transfers between devices, spread_corner(): lax.ppermute(got, 'col', [(h * 8 + j, h * 8 + j + 4) for h in range(4) fo...  10.6 us
    ppermute x4, starting transfers between devices, spread_corner(): lax.ppermute(b, 'row', [(r, r ^ 1) for r in range(8)])  10.4 us
    pallas_call x1, Pallas kernels, update(): pl.pallas_call(update_kernel, out_shape=jax.ShapeDtypeStruct(flat.shape,...  8.92 us
    ppermute x3, starting transfers between devices, spread_corner(): stack.append(lax.ppermute(got, 'col', pairs))  8.46 us
    ppermute x3, starting transfers between devices, spread_corner(): lax.ppermute(quarter[:, d], 'col', [(j, d * 8 + j) for j in range(3)])  6.77 us
  transfers between devices with their start and end apart: 26, of which 6 were waited for; matrix products, arithmetic and copies ran while one was open for 0% of the time, Pallas kernels for 23%

profile of v3, /device:TPU:1, one launch (start us, length us, event | category | flops | bytes accessed | tf_op | source)
XLA Modules:
  0.0 149.3 jit_solution(649887965250951571)
XLA Ops:
  6.5 0.0 all-gather.3.cloned.1.call-start
  6.5 1.2 slice.39
  7.8 0.4 reshape_squeeze.3
  8.2 15.0 %all_to_all.5 = f32[8,32,512]{2,1,0:T(8,128)S(1)} all-to-all(f32[8,32,512]{2,1,0:T(8,128)S(1)} %reshape_squeeze.3), channel_id=1, replica_groups=mesh['row'=8,'col'=32] {'row'}, dimensions={0} | all-to-all | bytes 1048576 | tf_op jit(solution)/shard_map/all_to_all | solution.py:370
  23.2 4.4 %collective-permute-start.24 = (f32[3,32,512]{2,1,0:T(8,128)S(1)}, f32[3,32,512]{2,1,0:T(8,128)S(1)}, u32[]{:S(2)}, u32[]{:S(2)}) collective-permute-start(f32[3,32,512]{2,1,0:T(8,128)S(1)} %slice.64.refs_0_), channel_id=1, source_target_pairs={{0,0},{1,32},{2,64},{3,96},{4,128},{5,160},{6,192},{7,224},{8,8},{... | collective-permute-start | bytes 589832 | tf_op jit(solution)/shard_map/ppermute | solution.py:371
  27.6 3.5 %collective-permute-done.24 = f32[3,32,512]{2,1,0:T(8,128)S(1)} collective-permute-done((f32[3,32,512]{2,1,0:T(8,128)S(1)}, f32[3,32,512]{2,1,0:T(8,128)S(1)}, u32[]{:S(2)}, u32[]{:S(2)}) %collective-permute-start.24) | collective-permute-done | bytes 196640 | tf_op jit(solution)/shard_map/ppermute | solution.py:371
  31.1 0.0 copy-start
  31.1 0.7 copy-done
  31.8 0.0 all-gather.3.cloned.1.call-update
  31.9 3.2 %collective-permute-start = (f32[3,8,256]{2,1,0:T(8,128)S(1)}, f32[3,8,256]{2,1,0:T(8,128)S(1)}, u32[]{:S(2)}, u32[]{:S(2)}) collective-permute-start(f32[3,8,256]{2,1,0:T(8,128)S(1)} %get-tuple-element.19), channel_id=1, source_target_pairs={{0,8},{1,9},{2,10},{32,40},{33,41},{34,42},{64,72},{65,73},{66,74}... | collective-permute-start | bytes 73736 | tf_op jit(solution)/shard_map/ppermute | solution.py:328
  35.1 2.3 %collective-permute-start.1 = (f32[3,8,256]{2,1,0:T(8,128)S(1)}, f32[3,8,256]{2,1,0:T(8,128)S(1)}, u32[]{:S(2)}, u32[]{:S(2)}) collective-permute-start(f32[3,8,256]{2,1,0:T(8,128)S(1)} %get-tuple-element.20), channel_id=1, source_target_pairs={{0,16},{1,17},{2,18},{32,48},{33,49},{34,50},{64,80},{65,81},{66,8... | collective-permute-start | bytes 73736 | tf_op jit(solution)/shard_map/ppermute | solution.py:328
  37.4 1.3 collective-permute-start.2
  38.7 0.0 collective-permute-done
  38.7 0.0 collective-permute-done.1
  38.7 0.9 collective-permute-done.2
  39.6 10.6 %collective-permute-start.3 = (f32[3,8,256]{2,1,0:T(8,128)S(1)}, f32[3,8,256]{2,1,0:T(8,128)S(1)}, u32[]{:S(2)}, u32[]{:S(2)}) collective-permute-start(f32[3,8,256]{2,1,0:T(8,128)S(1)} %fusion.5), channel_id=1, source_target_pairs={{0,4},{1,5},{2,6},{8,12},{9,13},{10,14},{16,20},{17,21},{18,22},{2... | collective-permute-start | bytes 73736 | tf_op jit(solution)/shard_map/ppermute | solution.py:331
  50.3 0.9 collective-permute-done.3
  51.2 1.9 %collective-permute-start.6 = (f32[3,8,256]{2,1,0:T(8,128)S(1)}, f32[3,8,256]{2,1,0:T(8,128)S(1)}, u32[]{:S(2)}, u32[]{:S(2)}) collective-permute-start(f32[3,8,256]{2,1,0:T(8,128)S(1)} %add.33), channel_id=1, source_target_pairs={{0,3},{1,0},{2,1},{4,7},{5,4},{6,5},{8,11},{9,8},{10,9},{12,15},{1... | collective-permute-start | bytes 73736 | tf_op jit(solution)/shard_map/ppermute | solution.py:337
  53.1 3.4 %collective-permute-start.5 = (f32[3,8,256]{2,1,0:T(8,128)S(1)}, f32[3,8,256]{2,1,0:T(8,128)S(1)}, u32[]{:S(2)}, u32[]{:S(2)}) collective-permute-start(f32[3,8,256]{2,1,0:T(8,128)S(1)} %add.33), channel_id=1, source_target_pairs={{0,1},{1,2},{2,3},{4,5},{5,6},{6,7},{8,9},{9,10},{10,11},{12,13},{... | collective-permute-start | bytes 73736 | tf_op jit(solution)/shard_map/ppermute | solution.py:337
  56.5 3.2 %collective-permute-start.4 = (f32[3,8,256]{2,1,0:T(8,128)S(1)}, f32[3,8,256]{2,1,0:T(8,128)S(1)}, u32[]{:S(2)}, u32[]{:S(2)}) collective-permute-start(f32[3,8,256]{2,1,0:T(8,128)S(1)} %add.33), channel_id=1, source_target_pairs={{0,2},{1,3},{2,0},{4,6},{5,7},{6,4},{8,10},{9,11},{10,8},{12,14},{... | collective-permute-start | bytes 73736 | tf_op jit(solution)/shard_map/ppermute | solution.py:337
  59.7 0.0 collective-permute-done.6
  59.7 0.0 collective-permute-done.5
  59.8 3.0 %collective-permute-done.4 = f32[3,8,256]{2,1,0:T(8,128)S(1)} collective-permute-done((f32[3,8,256]{2,1,0:T(8,128)S(1)}, f32[3,8,256]{2,1,0:T(8,128)S(1)}, u32[]{:S(2)}, u32[]{:S(2)}) %collective-permute-start.4) | collective-permute-done | bytes 24608 | tf_op jit(solution)/shard_map/ppermute | solution.py:337
  62.9 2.3 %collective-permute-start.9 = (f32[6,8,256]{2,1,0:T(8,128)S(1)}, f32[6,8,256]{2,1,0:T(8,128)S(1)}, u32[]{:S(2)}, u32[]{:S(2)}) collective-permute-start(f32[6,8,256]{2,1,0:T(8,128)S(1)} %slice_dynamic-update-slice_fusion), channel_id=1, source_target_pairs={{0,24},{1,25},{2,26},{3,27},{4,28},{5,29},{6,30},{7,31},{8,0},{9,1... | collective-permute-start | bytes 147464 | tf_op jit(solution)/shard_map/ppermute | solution.py:348
  65.1 0.4 collective-permute-start.8
  65.5 0.6 collective-permute-start.7
  66.2 10.4 %collective-permute-start.23 = (f32[3,32,512]{2,1,0:T(8,128)S(1)}, f32[3,32,512]{2,1,0:T(8,128)S(1)}, u32[]{:S(2)}, u32[]{:S(2)}) collective-permute-start(f32[3,32,512]{2,1,0:T(8,128)S(1)} %slice.64.refs_0_), channel_id=1, source_target_pairs={{0,224},{32,192},{64,32},{96,0},{128,96},{160,64},{192,160},{224,1... | collective-permute-start | bytes 589832 | tf_op jit(solution)/shard_map/ppermute | solution.py:362
  76.6 0.0 collective-permute-done.9
  76.6 0.0 collective-permute-done.8
  76.6 0.0 collective-permute-done.7
  76.6 0.1 collective-permute-start.12
  76.7 0.1 collective-permute-start.11
  76.8 1.4 collective-permute-start.10
  78.2 2.4 %collective-permute-start.22 = (f32[3,32,512]{2,1,0:T(8,128)S(1)}, f32[3,32,512]{2,1,0:T(8,128)S(1)}, u32[]{:S(2)}, u32[]{:S(2)}) collective-permute-start(f32[3,32,512]{2,1,0:T(8,128)S(1)} %slice.64.refs_0_), channel_id=1, source_target_pairs={{0,192},{32,224},{64,0},{96,32},{128,64},{160,96},{192,128},{224,1... | collective-permute-start | bytes 589832 | tf_op jit(solution)/shard_map/ppermute | solution.py:362
  80.6 0.0 collective-permute-done.23.refs_7_
  80.6 4.6 %collective-permute-start.13 = (f32[4,6,8,256]{3,2,1,0:T(8,128)S(1)}, f32[4,6,8,256]{3,2,1,0:T(8,128)S(1)}, u32[]{:S(2)}, u32[]{:S(2)}) collective-permute-start(f32[4,6,8,256]{3,2,1,0:T(8,128)S(1)} %pad_maximum_fusion.refs_0_), channel_id=1, source_target_pairs={{0,32},{32,0},{64,96},{96,64},{128,160},{160,128},{192,224},{224,1... | collective-permute-start | bytes 589832 | tf_op jit(solution)/shard_map/ppermute | solution.py:353
  85.2 0.0 collective-permute-done.12.refs_3_
  85.2 4.9 %collective-permute-start.16 = (f32[4,6,8,256]{3,2,1,0:T(8,128)S(1)}, f32[4,6,8,256]{3,2,1,0:T(8,128)S(1)}, u32[]{:S(2)}, u32[]{:S(2)}) collective-permute-start(f32[4,6,8,256]{3,2,1,0:T(8,128)S(1)} %collective-permute-done.12.refs_3_), channel_id=1, source_target_pairs={{0,32},{32,0},{64,96},{96,64},{128,160},{160,128},{192,224},{224,1... | collective-permute-start | bytes 589832 | tf_op jit(solution)/shard_map/ppermute | solution.py:353
  90.1 0.0 collective-permute-done.11.refs_2_
  90.1 0.0 collective-permute-start.15
  90.1 0.0 collective-permute-done.10.refs_1_
  90.1 0.8 collective-permute-start.14
  90.9 0.1 pad_add_fusion.place_ref
  91.0 0.5 collective-permute-done.22.refs_6_
  91.5 2.7 %collective-permute-start.21 = (f32[3,32,512]{2,1,0:T(8,128)S(1)}, f32[3,32,512]{2,1,0:T(8,128)S(1)}, u32[]{:S(2)}, u32[]{:S(2)}) collective-permute-start(f32[3,32,512]{2,1,0:T(8,128)S(1)} %slice.64.refs_0_), channel_id=1, source_target_pairs={{0,160},{32,128},{64,224},{96,192},{128,32},{160,0},{192,96},{224,... | collective-permute-start | bytes 589832 | tf_op jit(solution)/shard_map/ppermute | solution.py:362
  94.2 0.0 collective-permute-done.13.refs_4_
  94.2 1.1 collective-permute-start.20
  95.3 0.0 collective-permute-done.16.refs_7_
  95.3 1.1 collective-permute-start.19
  96.4 0.0 collective-permute-done.15.refs_6_
  96.4 0.1 collective-permute-start.18
  96.5 0.0 collective-permute-done.14.refs_5_
  96.5 1.1 collective-permute-start.17
  97.5 30.0 %factor_corner.1 = (f32[3,256,256]{2,1,0:T(8,128)S(1)}, f32[3,256,256]{2,1,0:T(8,128)S(1)}, f32[256,256]{1,0:T(8,128)S(1)}) custom-call(s32[2]{0:T(128)S(1)} %pad_add_fusion.place_ref, f32[4,6,8,256]{3,2,1,0:T(8,128)S(1)} %pad_maximum_fusion.refs_0_, f32[4,6,8,256]{3,2,1,0:T(8,128)S(1)} %collective-permute-done.10.refs_1_, ...), custom_call_target="tpu_custom_call" | custom-call | flops 30000001024 | bytes 10000000 | tf_op jit(solution)/shard_map/factor_corner/pallas_call | solution.py:169
  127.6 0.0 collective-permute-done.21.refs_5_
  127.6 0.0 collective-permute-done.20.refs_4_
  127.6 0.0 collective-permute-done.19.refs_3_
  127.6 0.0 collective-permute-done.18.refs_2_
  127.6 0.0 collective-permute-done.17.refs_1_
  127.6 4.5 %solve_columns.1 = (bf16[768,512]{1,0:T(8,128)(2,1)S(1)}, bf16[768,512]{1,0:T(8,128)(2,1)S(1)}) custom-call(s32[2]{0:T(128)S(1)} %pad_add_fusion.place_ref, f32[3,256,256]{2,1,0:T(8,128)S(1)} %get-tuple-element.11.v_ref, f32[3,256,256]{2,1,0:T(8,128)S(1)} %get-tuple-element.12.x_ref, f32[3,32,512]{2,1,0:T(8,128)S(1)} %slice.64.refs_0_, ...), custom_call_target="tpu_custom_call" | custom-call | flops 3000000000 | bytes 10000000 | tf_op jit(solution)/shard_map/solve_columns/pallas_call | solution.py:225
  132.1 1.5 all-gather.3.cloned.1.call-done
  133.6 8.9 %trailing_update.1 = f32[8,1024,128]{2,1,0:T(8,128)} custom-call(s32[2]{0:T(128)S(1)} %pad_add_fusion.place_ref, bf16[768,512]{1,0:T(8,128)(2,1)S(1)} %get-tuple-element.14.refs_0_, bf16[768,512]{1,0:T(8,128)(2,1)S(1)} %get-tuple-element.15.refs_1_, f32[256,256]{1,0:T(8,128)S(1)} %get-tuple-element.16.refs_2_, f32[8,1024,128]{2,1,0:T(8,128)} %bitcast.56, ...), custom_call_target="tpu_custom_call" | custom-call | flops 5000000000 | bytes 14000000 | tf_op jit(solution)/shard_map/trailing_update/pallas_call | solution.py:304
  (12 shorter events, 0.1 us)
Async XLA Ops:
  6.5 127.0 %all-gather.3.cloned.1.call-start = ((), (), s32[]{:S(2)}) async-start(), calls=%async_computation.1 | async-start | bytes 6488064 | tf_op jit(solution)/shard_map/all_gather | solution.py:376
  23.2 7.9 %collective-permute-start.24 = (f32[3,32,512]{2,1,0:T(8,128)S(1)}, f32[3,32,512]{2,1,0:T(8,128)S(1)}, u32[]{:S(2)}, u32[]{:S(2)}) collective-permute-start(f32[3,32,512]{2,1,0:T(8,128)S(1)} %slice.64.refs_0_), channel_id=1, source_target_pairs={{0,0},{1,32},{2,64},{3,96},{4,128},{5,160},{6,192},{7,224},{8,8},{... | collective-permute-start | bytes 589832 | tf_op jit(solution)/shard_map/ppermute | solution.py:371
  31.1 0.7 copy-start
  31.9 6.8 %collective-permute-start = (f32[3,8,256]{2,1,0:T(8,128)S(1)}, f32[3,8,256]{2,1,0:T(8,128)S(1)}, u32[]{:S(2)}, u32[]{:S(2)}) collective-permute-start(f32[3,8,256]{2,1,0:T(8,128)S(1)} %get-tuple-element.19), channel_id=1, source_target_pairs={{0,8},{1,9},{2,10},{32,40},{33,41},{34,42},{64,72},{65,73},{66,74}... | collective-permute-start | bytes 73736 | tf_op jit(solution)/shard_map/ppermute | solution.py:328
  35.1 3.6 %collective-permute-start.1 = (f32[3,8,256]{2,1,0:T(8,128)S(1)}, f32[3,8,256]{2,1,0:T(8,128)S(1)}, u32[]{:S(2)}, u32[]{:S(2)}) collective-permute-start(f32[3,8,256]{2,1,0:T(8,128)S(1)} %get-tuple-element.20), channel_id=1, source_target_pairs={{0,16},{1,17},{2,18},{32,48},{33,49},{34,50},{64,80},{65,81},{66,8... | collective-permute-start | bytes 73736 | tf_op jit(solution)/shard_map/ppermute | solution.py:328
  37.4 2.2 %collective-permute-start.2 = (f32[3,8,256]{2,1,0:T(8,128)S(1)}, f32[3,8,256]{2,1,0:T(8,128)S(1)}, u32[]{:S(2)}, u32[]{:S(2)}) collective-permute-start(f32[3,8,256]{2,1,0:T(8,128)S(1)} %get-tuple-element.21), channel_id=1, source_target_pairs={{0,24},{1,25},{2,26},{32,56},{33,57},{34,58},{64,88},{65,89},{66,9... | collective-permute-start | bytes 73736 | tf_op jit(solution)/shard_map/ppermute | solution.py:328
  39.6 11.6 %collective-permute-start.3 = (f32[3,8,256]{2,1,0:T(8,128)S(1)}, f32[3,8,256]{2,1,0:T(8,128)S(1)}, u32[]{:S(2)}, u32[]{:S(2)}) collective-permute-start(f32[3,8,256]{2,1,0:T(8,128)S(1)} %fusion.5), channel_id=1, source_target_pairs={{0,4},{1,5},{2,6},{8,12},{9,13},{10,14},{16,20},{17,21},{18,22},{2... | collective-permute-start | bytes 73736 | tf_op jit(solution)/shard_map/ppermute | solution.py:331
  51.2 8.5 %collective-permute-start.6 = (f32[3,8,256]{2,1,0:T(8,128)S(1)}, f32[3,8,256]{2,1,0:T(8,128)S(1)}, u32[]{:S(2)}, u32[]{:S(2)}) collective-permute-start(f32[3,8,256]{2,1,0:T(8,128)S(1)} %add.33), channel_id=1, source_target_pairs={{0,3},{1,0},{2,1},{4,7},{5,4},{6,5},{8,11},{9,8},{10,9},{12,15},{1... | collective-permute-start | bytes 73736 | tf_op jit(solution)/shard_map/ppermute | solution.py:337
  53.1 6.6 %collective-permute-start.5 = (f32[3,8,256]{2,1,0:T(8,128)S(1)}, f32[3,8,256]{2,1,0:T(8,128)S(1)}, u32[]{:S(2)}, u32[]{:S(2)}) collective-permute-start(f32[3,8,256]{2,1,0:T(8,128)S(1)} %add.33), channel_id=1, source_target_pairs={{0,1},{1,2},{2,3},{4,5},{5,6},{6,7},{8,9},{9,10},{10,11},{12,13},{... | collective-permute-start | bytes 73736 | tf_op jit(solution)/shard_map/ppermute | solution.py:337
  56.5 6.3 %collective-permute-start.4 = (f32[3,8,256]{2,1,0:T(8,128)S(1)}, f32[3,8,256]{2,1,0:T(8,128)S(1)}, u32[]{:S(2)}, u32[]{:S(2)}) collective-permute-start(f32[3,8,256]{2,1,0:T(8,128)S(1)} %add.33), channel_id=1, source_target_pairs={{0,2},{1,3},{2,0},{4,6},{5,7},{6,4},{8,10},{9,11},{10,8},{12,14},{... | collective-permute-start | bytes 73736 | tf_op jit(solution)/shard_map/ppermute | solution.py:337
  62.9 13.7 %collective-permute-start.9 = (f32[6,8,256]{2,1,0:T(8,128)S(1)}, f32[6,8,256]{2,1,0:T(8,128)S(1)}, u32[]{:S(2)}, u32[]{:S(2)}) collective-permute-start(f32[6,8,256]{2,1,0:T(8,128)S(1)} %slice_dynamic-update-slice_fusion), channel_id=1, source_target_pairs={{0,24},{1,25},{2,26},{3,27},{4,28},{5,29},{6,30},{7,31},{8,0},{9,1... | collective-permute-start | bytes 147464 | tf_op jit(solution)/shard_map/ppermute | solution.py:348
  65.1 11.4 %collective-permute-start.8 = (f32[6,8,256]{2,1,0:T(8,128)S(1)}, f32[6,8,256]{2,1,0:T(8,128)S(1)}, u32[]{:S(2)}, u32[]{:S(2)}) collective-permute-start(f32[6,8,256]{2,1,0:T(8,128)S(1)} %slice_dynamic-update-slice_fusion), channel_id=1, source_target_pairs={{0,16},{1,17},{2,18},{3,19},{4,20},{5,21},{6,22},{7,23},{8,24},{9,... | collective-permute-start | bytes 147464 | tf_op jit(solution)/shard_map/ppermute | solution.py:348
  65.5 11.1 %collective-permute-start.7 = (f32[6,8,256]{2,1,0:T(8,128)S(1)}, f32[6,8,256]{2,1,0:T(8,128)S(1)}, u32[]{:S(2)}, u32[]{:S(2)}) collective-permute-start(f32[6,8,256]{2,1,0:T(8,128)S(1)} %slice_dynamic-update-slice_fusion), channel_id=1, source_target_pairs={{0,8},{1,9},{2,10},{3,11},{4,12},{5,13},{6,14},{7,15},{8,16},{9,17... | collective-permute-start | bytes 147464 | tf_op jit(solution)/shard_map/ppermute | solution.py:348
  66.2 14.4 %collective-permute-start.23 = (f32[3,32,512]{2,1,0:T(8,128)S(1)}, f32[3,32,512]{2,1,0:T(8,128)S(1)}, u32[]{:S(2)}, u32[]{:S(2)}) collective-permute-start(f32[3,32,512]{2,1,0:T(8,128)S(1)} %slice.64.refs_0_), channel_id=1, source_target_pairs={{0,224},{32,192},{64,32},{96,0},{128,96},{160,64},{192,160},{224,1... | collective-permute-start | bytes 589832 | tf_op jit(solution)/shard_map/ppermute | solution.py:362
  76.6 8.6 %collective-permute-start.12 = (f32[4,6,8,256]{3,2,1,0:T(8,128)S(1)}, f32[4,6,8,256]{3,2,1,0:T(8,128)S(1)}, u32[]{:S(2)}, u32[]{:S(2)}) collective-permute-start(f32[4,6,8,256]{3,2,1,0:T(8,128)S(1)} %pad_maximum_fusion.refs_0_), channel_id=1, source_target_pairs={{0,192},{32,224},{64,0},{96,32},{128,64},{160,96},{192,128},{224,1... | collective-permute-start | bytes 589832 | tf_op jit(solution)/shard_map/ppermute | solution.py:352
  76.7 13.4 %collective-permute-start.11 = (f32[4,6,8,256]{3,2,1,0:T(8,128)S(1)}, f32[4,6,8,256]{3,2,1,0:T(8,128)S(1)}, u32[]{:S(2)}, u32[]{:S(2)}) collective-permute-start(f32[4,6,8,256]{3,2,1,0:T(8,128)S(1)} %pad_maximum_fusion.refs_0_), channel_id=1, source_target_pairs={{0,128},{32,160},{64,192},{96,224},{128,0},{160,32},{192,64},{224,... | collective-permute-start | bytes 589832 | tf_op jit(solution)/shard_map/ppermute | solution.py:352
  76.8 13.3 %collective-permute-start.10 = (f32[4,6,8,256]{3,2,1,0:T(8,128)S(1)}, f32[4,6,8,256]{3,2,1,0:T(8,128)S(1)}, u32[]{:S(2)}, u32[]{:S(2)}) collective-permute-start(f32[4,6,8,256]{3,2,1,0:T(8,128)S(1)} %pad_maximum_fusion.refs_0_), channel_id=1, source_target_pairs={{0,64},{32,96},{64,128},{96,160},{128,192},{160,224},{192,0},{224,... | collective-permute-start | bytes 589832 | tf_op jit(solution)/shard_map/ppermute | solution.py:352
  78.2 13.3 %collective-permute-start.22 = (f32[3,32,512]{2,1,0:T(8,128)S(1)}, f32[3,32,512]{2,1,0:T(8,128)S(1)}, u32[]{:S(2)}, u32[]{:S(2)}) collective-permute-start(f32[3,32,512]{2,1,0:T(8,128)S(1)} %slice.64.refs_0_), channel_id=1, source_target_pairs={{0,192},{32,224},{64,0},{96,32},{128,64},{160,96},{192,128},{224,1... | collective-permute-start | bytes 589832 | tf_op jit(solution)/shard_map/ppermute | solution.py:362
  80.6 13.6 %collective-permute-start.13 = (f32[4,6,8,256]{3,2,1,0:T(8,128)S(1)}, f32[4,6,8,256]{3,2,1,0:T(8,128)S(1)}, u32[]{:S(2)}, u32[]{:S(2)}) collective-permute-start(f32[4,6,8,256]{3,2,1,0:T(8,128)S(1)} %pad_maximum_fusion.refs_0_), channel_id=1, source_target_pairs={{0,32},{32,0},{64,96},{96,64},{128,160},{160,128},{192,224},{224,1... | collective-permute-start | bytes 589832 | tf_op jit(solution)/shard_map/ppermute | solution.py:353
  85.2 10.2 %collective-permute-start.16 = (f32[4,6,8,256]{3,2,1,0:T(8,128)S(1)}, f32[4,6,8,256]{3,2,1,0:T(8,128)S(1)}, u32[]{:S(2)}, u32[]{:S(2)}) collective-permute-start(f32[4,6,8,256]{3,2,1,0:T(8,128)S(1)} %collective-permute-done.12.refs_3_), channel_id=1, source_target_pairs={{0,32},{32,0},{64,96},{96,64},{128,160},{160,128},{192,224},{224,1... | collective-permute-start | bytes 589832 | tf_op jit(solution)/shard_map/ppermute | solution.py:353
  90.1 6.3 %collective-permute-start.15 = (f32[4,6,8,256]{3,2,1,0:T(8,128)S(1)}, f32[4,6,8,256]{3,2,1,0:T(8,128)S(1)}, u32[]{:S(2)}, u32[]{:S(2)}) collective-permute-start(f32[4,6,8,256]{3,2,1,0:T(8,128)S(1)} %collective-permute-done.11.refs_2_), channel_id=1, source_target_pairs={{0,32},{32,0},{64,96},{96,64},{128,160},{160,128},{192,224},{224,1... | collective-permute-start | bytes 589832 | tf_op jit(solution)/shard_map/ppermute | solution.py:353
  90.1 6.3 %collective-permute-start.14 = (f32[4,6,8,256]{3,2,1,0:T(8,128)S(1)}, f32[4,6,8,256]{3,2,1,0:T(8,128)S(1)}, u32[]{:S(2)}, u32[]{:S(2)}) collective-permute-start(f32[4,6,8,256]{3,2,1,0:T(8,128)S(1)} %collective-permute-done.10.refs_1_), channel_id=1, source_target_pairs={{0,32},{32,0},{64,96},{96,64},{128,160},{160,128},{192,224},{224,1... | collective-permute-start | bytes 589832 | tf_op jit(solution)/shard_map/ppermute | solution.py:353
  91.5 36.1 %collective-permute-start.21 = (f32[3,32,512]{2,1,0:T(8,128)S(1)}, f32[3,32,512]{2,1,0:T(8,128)S(1)}, u32[]{:S(2)}, u32[]{:S(2)}) collective-permute-start(f32[3,32,512]{2,1,0:T(8,128)S(1)} %slice.64.refs_0_), channel_id=1, source_target_pairs={{0,160},{32,128},{64,224},{96,192},{128,32},{160,0},{192,96},{224,... | collective-permute-start | bytes 589832 | tf_op jit(solution)/shard_map/ppermute | solution.py:362
  94.2 33.4 %collective-permute-start.20 = (f32[3,32,512]{2,1,0:T(8,128)S(1)}, f32[3,32,512]{2,1,0:T(8,128)S(1)}, u32[]{:S(2)}, u32[]{:S(2)}) collective-permute-start(f32[3,32,512]{2,1,0:T(8,128)S(1)} %slice.64.refs_0_), channel_id=1, source_target_pairs={{0,128},{32,160},{64,192},{96,224},{128,0},{160,32},{192,64},{224,... | collective-permute-start | bytes 589832 | tf_op jit(solution)/shard_map/ppermute | solution.py:362
  95.3 32.2 %collective-permute-start.19 = (f32[3,32,512]{2,1,0:T(8,128)S(1)}, f32[3,32,512]{2,1,0:T(8,128)S(1)}, u32[]{:S(2)}, u32[]{:S(2)}) collective-permute-start(f32[3,32,512]{2,1,0:T(8,128)S(1)} %slice.64.refs_0_), channel_id=1, source_target_pairs={{0,96},{32,64},{64,160},{96,128},{128,224},{160,192},{192,32},{224... | collective-permute-start | bytes 589832 | tf_op jit(solution)/shard_map/ppermute | solution.py:362
  96.4 31.2 %collective-permute-start.18 = (f32[3,32,512]{2,1,0:T(8,128)S(1)}, f32[3,32,512]{2,1,0:T(8,128)S(1)}, u32[]{:S(2)}, u32[]{:S(2)}) collective-permute-start(f32[3,32,512]{2,1,0:T(8,128)S(1)} %slice.64.refs_0_), channel_id=1, source_target_pairs={{0,64},{32,96},{64,128},{96,160},{128,192},{160,224},{192,0},{224,... | collective-permute-start | bytes 589832 | tf_op jit(solution)/shard_map/ppermute | solution.py:362
  96.5 31.1 %collective-permute-start.17 = (f32[3,32,512]{2,1,0:T(8,128)S(1)}, f32[3,32,512]{2,1,0:T(8,128)S(1)}, u32[]{:S(2)}, u32[]{:S(2)}) collective-permute-start(f32[3,32,512]{2,1,0:T(8,128)S(1)} %slice.64.refs_0_), channel_id=1, source_target_pairs={{0,32},{32,0},{64,96},{96,64},{128,160},{160,128},{192,224},{224,1... | collective-permute-start | bytes 589832 | tf_op jit(solution)/shard_map/ppermute | solution.py:362
Sparse Core Ops, SparseCore 0:
  32.0 101.5 all-gather.2

commit v4 on v3

--- a/solution.py
+++ b/solution.py
@@ -11,6 +11,7 @@
 BAND = 32
 PIV = 8
 PAIRS = tuple((k, j) for k in range(3) for j in range(k, 3))
+SHIFT = (0, 4, 1, 7, 2, 6, 3, 5)
 HIGHEST = lax.Precision.HIGHEST
 F32 = jnp.float32
 BF16 = jnp.bfloat16
@@ -217,7 +218,8 @@
         done[k] = split(product(vt[k], split(rest)))
         for ref, part in ((zhi_ref, done[k][0]), (zlo_ref, done[k][1])):
             for p in range(8):
-                ref[p * 96 + k * 32 : p * 96 + k * 32 + 32, :] = part[p * 32 : p * 32 + 32]
+                to = pl.multiple_of((my_row + SHIFT[p]) % 8 * 96 + k * 32, 32)
+                ref[pl.ds(to, 32), :] = part[p * 32 : p * 32 + 32]
 
 
 def solve(place, v, x, pieces):
@@ -368,10 +370,9 @@
     place = jnp.stack([my_row, my_col]).astype(jnp.int32)
     top = covariance[0].reshape(8, 32, 2 * B)
     mine = lax.all_to_all(top, "row", 0, 0, tiled=True)[:3]
+    places = [(r, y, z) for r in range(8) for y in range(4) for z in range(8)]
     turned = lax.ppermute(
-        mine,
-        ("row", "col"),
-        [(r * 32 + y * 8 + z, z * 32 + y * 8 + r) for r in range(8) for y in range(4) for z in range(8)],
+        mine, ("row", "col"), [(r * 32 + y * 8 + z, z * 32 + y * 8 + (z + SHIFT[r]) % 8) for r, y, z in places]
     )
     rows = lax.all_gather(turned, "col")
     own, other, first = spread_corner(mine[:, :, :B], my_col)

time: 150 us -> 145 us (0.967)
  starting transfers between devices: 64.4 us -> 54.7 us
  waiting for transfers between devices: 10.3 us -> 15.4 us
    ppermute x7, starting transfers between devices: 18.9 us -> 11.6 us  [spread_columns(): pieces.append(mine if n == 0 else lax.ppermute(mine, 'row', pairs))]
    ppermute x1, starting transfers between devices: 10.6 us -> 4.14 us  [spread_corner(): lax.ppermute(got, 'col', [(h * 8 + j, h * 8 + j + 4) for h in range(4) fo...]
    ppermute x1, starting transfers between devices: 4.43 us -> 9.7 us  [on_device(): lax.ppermute(mine, ('row', 'col'), [(r * 32 + y * 8 + z, z * 32 + y * 8 +...]
    ppermute x7, waiting for transfers between devices: 0.47 us -> 2.43 us  [spread_columns(): pieces.append(mine if n == 0 else lax.ppermute(mine, 'row', pairs))]
    ppermute x4, starting transfers between devices: 10.4 us -> 8.64 us  [spread_corner(): lax.ppermute(b, 'row', [(r, r ^ 1) for r in range(8)])]
  transfers between devices with their start and end apart: 26 -> 26, of which waited for: 6 -> 7; matrix products, arithmetic and copies ran while one was open for 0% -> 0% of each run, Pallas kernels for 23% -> 24%
where the time goes in v4:
time: 145 us
  starting transfers between devices  54.7 us (38%)
  Pallas kernels  43.4 us (30%)
  waiting for transfers between devices  15.4 us (11%)
  blocking collectives  15 us (10%)
  between operations  13.8 us (10%)
  local copies, waits for them, and re-layouts  2.36 us (2%)
    pallas_call x1, Pallas kernels, factor(): pl.pallas_call(factor_kernel, out_shape=(jax.ShapeDtypeStruct((3, B, B),...  30 us
    all_to_all x1, blocking collectives, on_device(): mine = lax.all_to_all(top, 'row', 0, 0, tiled=True)[:3]  15 us
    ppermute x7, starting transfers between devices, spread_columns(): pieces.append(mine if n == 0 else lax.ppermute(mine, 'row', pairs))  11.6 us
    ppermute x1, starting transfers between devices, on_device(): lax.ppermute(mine, ('row', 'col'), [(r * 32 + y * 8 + z, z * 32 + y * 8 +...  9.7 us
    pallas_call x1, Pallas kernels, update(): pl.pallas_call(update_kernel, out_shape=jax.ShapeDtypeStruct(flat.shape,...  8.91 us
    ppermute x4, starting transfers between devices, spread_corner(): lax.ppermute(b, 'row', [(r, r ^ 1) for r in range(8)])  8.64 us
    ppermute x3, starting transfers between devices, spread_corner(): stack.append(lax.ppermute(got, 'col', pairs))  7.19 us
    ppermute x3, starting transfers between devices, spread_corner(): lax.ppermute(quarter[:, d], 'col', [(j, d * 8 + j) for j in range(3)])  6.77 us
  transfers between devices with their start and end apart: 26, of which 7 were waited for; matrix products, arithmetic and copies ran while one was open for 0% of the time, Pallas kernels for 24%

profile of v4, /device:TPU:1, one launch (start us, length us, event | category | flops | bytes accessed | tf_op | source)
XLA Modules:
  0.0 144.8 jit_solution(17877545963502918705)
XLA Ops:
  6.5 0.0 all-gather.3.cloned.1.call-start
  6.5 1.2 slice.39
  7.8 0.4 reshape_squeeze.3
  8.2 15.0 %all_to_all.5 = f32[8,32,512]{2,1,0:T(8,128)S(1)} all-to-all(f32[8,32,512]{2,1,0:T(8,128)S(1)} %reshape_squeeze.3), channel_id=1, replica_groups=mesh['row'=8,'col'=32] {'row'}, dimensions={0} | all-to-all | bytes 1048576 | tf_op jit(solution)/shard_map/all_to_all | solution.py:372
  23.2 9.7 %collective-permute-start.24 = (f32[3,32,512]{2,1,0:T(8,128)S(1)}, f32[3,32,512]{2,1,0:T(8,128)S(1)}, u32[]{:S(2)}, u32[]{:S(2)}) collective-permute-start(f32[3,32,512]{2,1,0:T(8,128)S(1)} %slice.64.refs_0_), channel_id=1, source_target_pairs={{0,0},{1,33},{2,66},{3,99},{4,132},{5,165},{6,198},{7,231},{8,8},{... | collective-permute-start | bytes 589832 | tf_op jit(solution)/shard_map/ppermute | solution.py:374
  32.9 4.7 %collective-permute-done.24 = f32[3,32,512]{2,1,0:T(8,128)S(1)} collective-permute-done((f32[3,32,512]{2,1,0:T(8,128)S(1)}, f32[3,32,512]{2,1,0:T(8,128)S(1)}, u32[]{:S(2)}, u32[]{:S(2)}) %collective-permute-start.24) | collective-permute-done | bytes 196640 | tf_op jit(solution)/shard_map/ppermute | solution.py:374
  37.6 0.0 copy-start
  37.6 0.7 copy-done
  38.3 0.0 all-gather.3.cloned.1.call-update
  38.3 3.2 %collective-permute-start = (f32[3,8,256]{2,1,0:T(8,128)S(1)}, f32[3,8,256]{2,1,0:T(8,128)S(1)}, u32[]{:S(2)}, u32[]{:S(2)}) collective-permute-start(f32[3,8,256]{2,1,0:T(8,128)S(1)} %get-tuple-element.19), channel_id=1, source_target_pairs={{0,8},{1,9},{2,10},{32,40},{33,41},{34,42},{64,72},{65,73},{66,74}... | collective-permute-start | bytes 73736 | tf_op jit(solution)/shard_map/ppermute | solution.py:330
  41.5 2.3 %collective-permute-start.1 = (f32[3,8,256]{2,1,0:T(8,128)S(1)}, f32[3,8,256]{2,1,0:T(8,128)S(1)}, u32[]{:S(2)}, u32[]{:S(2)}) collective-permute-start(f32[3,8,256]{2,1,0:T(8,128)S(1)} %get-tuple-element.20), channel_id=1, source_target_pairs={{0,16},{1,17},{2,18},{32,48},{33,49},{34,50},{64,80},{65,81},{66,8... | collective-permute-start | bytes 73736 | tf_op jit(solution)/shard_map/ppermute | solution.py:330
  43.8 1.3 collective-permute-start.2
  45.1 0.0 collective-permute-done
  45.2 0.0 collective-permute-done.1
  45.2 0.9 collective-permute-done.2
  46.1 4.1 %collective-permute-start.3 = (f32[3,8,256]{2,1,0:T(8,128)S(1)}, f32[3,8,256]{2,1,0:T(8,128)S(1)}, u32[]{:S(2)}, u32[]{:S(2)}) collective-permute-start(f32[3,8,256]{2,1,0:T(8,128)S(1)} %fusion.5), channel_id=1, source_target_pairs={{0,4},{1,5},{2,6},{8,12},{9,13},{10,14},{16,20},{17,21},{18,22},{2... | collective-permute-start | bytes 73736 | tf_op jit(solution)/shard_map/ppermute | solution.py:333
  50.2 0.9 collective-permute-done.3
  51.1 1.9 %collective-permute-start.6 = (f32[3,8,256]{2,1,0:T(8,128)S(1)}, f32[3,8,256]{2,1,0:T(8,128)S(1)}, u32[]{:S(2)}, u32[]{:S(2)}) collective-permute-start(f32[3,8,256]{2,1,0:T(8,128)S(1)} %add.33), channel_id=1, source_target_pairs={{0,3},{1,0},{2,1},{4,7},{5,4},{6,5},{8,11},{9,8},{10,9},{12,15},{1... | collective-permute-start | bytes 73736 | tf_op jit(solution)/shard_map/ppermute | solution.py:339
  53.1 3.4 %collective-permute-start.5 = (f32[3,8,256]{2,1,0:T(8,128)S(1)}, f32[3,8,256]{2,1,0:T(8,128)S(1)}, u32[]{:S(2)}, u32[]{:S(2)}) collective-permute-start(f32[3,8,256]{2,1,0:T(8,128)S(1)} %add.33), channel_id=1, source_target_pairs={{0,1},{1,2},{2,3},{4,5},{5,6},{6,7},{8,9},{9,10},{10,11},{12,13},{... | collective-permute-start | bytes 73736 | tf_op jit(solution)/shard_map/ppermute | solution.py:339
  56.4 1.9 %collective-permute-start.4 = (f32[3,8,256]{2,1,0:T(8,128)S(1)}, f32[3,8,256]{2,1,0:T(8,128)S(1)}, u32[]{:S(2)}, u32[]{:S(2)}) collective-permute-start(f32[3,8,256]{2,1,0:T(8,128)S(1)} %add.33), channel_id=1, source_target_pairs={{0,2},{1,3},{2,0},{4,6},{5,7},{6,4},{8,10},{9,11},{10,8},{12,14},{... | collective-permute-start | bytes 73736 | tf_op jit(solution)/shard_map/ppermute | solution.py:339
  58.4 0.0 collective-permute-done.6
  58.4 0.0 collective-permute-done.5
  58.4 3.5 %collective-permute-done.4 = f32[3,8,256]{2,1,0:T(8,128)S(1)} collective-permute-done((f32[3,8,256]{2,1,0:T(8,128)S(1)}, f32[3,8,256]{2,1,0:T(8,128)S(1)}, u32[]{:S(2)}, u32[]{:S(2)}) %collective-permute-start.4) | collective-permute-done | bytes 24608 | tf_op jit(solution)/shard_map/ppermute | solution.py:339
  62.1 3.1 %collective-permute-start.9 = (f32[6,8,256]{2,1,0:T(8,128)S(1)}, f32[6,8,256]{2,1,0:T(8,128)S(1)}, u32[]{:S(2)}, u32[]{:S(2)}) collective-permute-start(f32[6,8,256]{2,1,0:T(8,128)S(1)} %slice_dynamic-update-slice_fusion), channel_id=1, source_target_pairs={{0,24},{1,25},{2,26},{3,27},{4,28},{5,29},{6,30},{7,31},{8,0},{9,1... | collective-permute-start | bytes 147464 | tf_op jit(solution)/shard_map/ppermute | solution.py:350
  65.2 0.3 collective-permute-start.8
  65.5 0.7 collective-permute-start.7
  66.2 3.6 %collective-permute-start.23 = (f32[3,32,512]{2,1,0:T(8,128)S(1)}, f32[3,32,512]{2,1,0:T(8,128)S(1)}, u32[]{:S(2)}, u32[]{:S(2)}) collective-permute-start(f32[3,32,512]{2,1,0:T(8,128)S(1)} %slice.64.refs_0_), channel_id=1, source_target_pairs={{0,224},{32,192},{64,32},{96,0},{128,96},{160,64},{192,160},{224,1... | collective-permute-start | bytes 589832 | tf_op jit(solution)/shard_map/ppermute | solution.py:364
  69.8 0.0 collective-permute-done.9
  69.8 0.0 collective-permute-done.8
  69.8 0.9 collective-permute-done.7
  70.7 0.4 collective-permute-start.12
  71.1 2.0 %collective-permute-start.11 = (f32[4,6,8,256]{3,2,1,0:T(8,128)S(1)}, f32[4,6,8,256]{3,2,1,0:T(8,128)S(1)}, u32[]{:S(2)}, u32[]{:S(2)}) collective-permute-start(f32[4,6,8,256]{3,2,1,0:T(8,128)S(1)} %pad_maximum_fusion.refs_0_), channel_id=1, source_target_pairs={{0,128},{32,160},{64,192},{96,224},{128,0},{160,32},{192,64},{224,... | collective-permute-start | bytes 589832 | tf_op jit(solution)/shard_map/ppermute | solution.py:354
  73.1 0.0 collective-permute-start.10
  73.2 2.7 %collective-permute-start.22 = (f32[3,32,512]{2,1,0:T(8,128)S(1)}, f32[3,32,512]{2,1,0:T(8,128)S(1)}, u32[]{:S(2)}, u32[]{:S(2)}) collective-permute-start(f32[3,32,512]{2,1,0:T(8,128)S(1)} %slice.64.refs_0_), channel_id=1, source_target_pairs={{0,192},{32,224},{64,0},{96,32},{128,64},{160,96},{192,128},{224,1... | collective-permute-start | bytes 589832 | tf_op jit(solution)/shard_map/ppermute | solution.py:364
  75.8 0.0 collective-permute-done.23.refs_7_
  75.8 4.8 %collective-permute-start.13 = (f32[4,6,8,256]{3,2,1,0:T(8,128)S(1)}, f32[4,6,8,256]{3,2,1,0:T(8,128)S(1)}, u32[]{:S(2)}, u32[]{:S(2)}) collective-permute-start(f32[4,6,8,256]{3,2,1,0:T(8,128)S(1)} %pad_maximum_fusion.refs_0_), channel_id=1, source_target_pairs={{0,32},{32,0},{64,96},{96,64},{128,160},{160,128},{192,224},{224,1... | collective-permute-start | bytes 589832 | tf_op jit(solution)/shard_map/ppermute | solution.py:355
  80.6 0.0 collective-permute-done.12.refs_3_
  80.6 2.9 %collective-permute-start.16 = (f32[4,6,8,256]{3,2,1,0:T(8,128)S(1)}, f32[4,6,8,256]{3,2,1,0:T(8,128)S(1)}, u32[]{:S(2)}, u32[]{:S(2)}) collective-permute-start(f32[4,6,8,256]{3,2,1,0:T(8,128)S(1)} %collective-permute-done.12.refs_3_), channel_id=1, source_target_pairs={{0,32},{32,0},{64,96},{96,64},{128,160},{160,128},{192,224},{224,1... | collective-permute-start | bytes 589832 | tf_op jit(solution)/shard_map/ppermute | solution.py:355
  83.6 0.0 collective-permute-done.11.refs_2_
  83.6 0.0 collective-permute-start.15
  83.6 0.0 collective-permute-done.10.refs_1_
  83.6 0.9 collective-permute-start.14
  84.5 0.1 pad_add_fusion.place_ref
  84.6 2.4 %collective-permute-done.22.refs_6_ = f32[3,32,512]{2,1,0:T(8,128)S(1)} collective-permute-done((f32[3,32,512]{2,1,0:T(8,128)S(1)}, f32[3,32,512]{2,1,0:T(8,128)S(1)}, u32[]{:S(2)}, u32[]{:S(2)}) %collective-permute-start.22) | collective-permute-done | bytes 196640 | tf_op jit(solution)/shard_map/ppermute | solution.py:364
  87.0 0.9 collective-permute-start.21
  87.9 0.0 collective-permute-done.13.refs_4_
  87.9 4.0 %collective-permute-start.20 = (f32[3,32,512]{2,1,0:T(8,128)S(1)}, f32[3,32,512]{2,1,0:T(8,128)S(1)}, u32[]{:S(2)}, u32[]{:S(2)}) collective-permute-start(f32[3,32,512]{2,1,0:T(8,128)S(1)} %slice.64.refs_0_), channel_id=1, source_target_pairs={{0,128},{32,160},{64,192},{96,224},{128,0},{160,32},{192,64},{224,... | collective-permute-start | bytes 589832 | tf_op jit(solution)/shard_map/ppermute | solution.py:364
  91.9 0.0 collective-permute-done.16.refs_7_
  91.9 0.0 collective-permute-start.19
  91.9 0.0 collective-permute-done.15.refs_6_
  91.9 0.3 collective-permute-start.18
  92.2 0.0 collective-permute-done.14.refs_5_
  92.2 0.2 collective-permute-start.17
  92.4 30.0 %factor_corner.1 = (f32[3,256,256]{2,1,0:T(8,128)S(1)}, f32[3,256,256]{2,1,0:T(8,128)S(1)}, f32[256,256]{1,0:T(8,128)S(1)}) custom-call(s32[2]{0:T(128)S(1)} %pad_add_fusion.place_ref, f32[4,6,8,256]{3,2,1,0:T(8,128)S(1)} %pad_maximum_fusion.refs_0_, f32[4,6,8,256]{3,2,1,0:T(8,128)S(1)} %collective-permute-done.10.refs_1_, ...), custom_call_target="tpu_custom_call" | custom-call | flops 30000001024 | bytes 10000000 | tf_op jit(solution)/shard_map/factor_corner/pallas_call | solution.py:170
  122.4 0.0 collective-permute-done.21.refs_5_
  122.4 0.0 collective-permute-done.20.refs_4_
  122.5 0.0 collective-permute-done.19.refs_3_
  122.5 0.0 collective-permute-done.18.refs_2_
  122.5 0.0 collective-permute-done.17.refs_1_
  122.5 4.5 %solve_columns.1 = (bf16[768,512]{1,0:T(8,128)(2,1)S(1)}, bf16[768,512]{1,0:T(8,128)(2,1)S(1)}) custom-call(s32[2]{0:T(128)S(1)} %pad_add_fusion.place_ref, f32[3,256,256]{2,1,0:T(8,128)S(1)} %get-tuple-element.11.v_ref, f32[3,256,256]{2,1,0:T(8,128)S(1)} %get-tuple-element.12.x_ref, f32[3,32,512]{2,1,0:T(8,128)S(1)} %slice.64.refs_0_, ...), custom_call_target="tpu_custom_call" | custom-call | flops 3000000000 | bytes 10000000 | tf_op jit(solution)/shard_map/solve_columns/pallas_call | solution.py:227
  127.0 2.0 %all-gather.3.cloned.1.call-done = f32[96,32,512]{2,1,0:T(8,128)} async-done(((f32[3,32,512]{2,1,0:T(8,128)}), f32[96,32,512]{2,1,0:T(8,128)}) %all-gather.3.cloned.1.call-update) | async-done | bytes 6291472 | tf_op jit(solution)/shard_map/all_gather | solution.py:377
  129.0 8.9 %trailing_update.1 = f32[8,1024,128]{2,1,0:T(8,128)} custom-call(s32[2]{0:T(128)S(1)} %pad_add_fusion.place_ref, bf16[768,512]{1,0:T(8,128)(2,1)S(1)} %get-tuple-element.14.refs_0_, bf16[768,512]{1,0:T(8,128)(2,1)S(1)} %get-tuple-element.15.refs_1_, f32[256,256]{1,0:T(8,128)S(1)} %get-tuple-element.16.refs_2_, f32[8,1024,128]{2,1,0:T(8,128)} %bitcast.56, ...), custom_call_target="tpu_custom_call" | custom-call | flops 5000000000 | bytes 14000000 | tf_op jit(solution)/shard_map/trailing_update/pallas_call | solution.py:306
  (12 shorter events, 0.1 us)
Async XLA Ops:
  6.5 122.4 %all-gather.3.cloned.1.call-start = ((), (), s32[]{:S(2)}) async-start(), calls=%async_computation.1 | async-start | bytes 6488064 | tf_op jit(solution)/shard_map/all_gather | solution.py:377
  23.2 14.4 %collective-permute-start.24 = (f32[3,32,512]{2,1,0:T(8,128)S(1)}, f32[3,32,512]{2,1,0:T(8,128)S(1)}, u32[]{:S(2)}, u32[]{:S(2)}) collective-permute-start(f32[3,32,512]{2,1,0:T(8,128)S(1)} %slice.64.refs_0_), channel_id=1, source_target_pairs={{0,0},{1,33},{2,66},{3,99},{4,132},{5,165},{6,198},{7,231},{8,8},{... | collective-permute-start | bytes 589832 | tf_op jit(solution)/shard_map/ppermute | solution.py:374
  37.6 0.7 copy-start
  38.3 6.8 %collective-permute-start = (f32[3,8,256]{2,1,0:T(8,128)S(1)}, f32[3,8,256]{2,1,0:T(8,128)S(1)}, u32[]{:S(2)}, u32[]{:S(2)}) collective-permute-start(f32[3,8,256]{2,1,0:T(8,128)S(1)} %get-tuple-element.19), channel_id=1, source_target_pairs={{0,8},{1,9},{2,10},{32,40},{33,41},{34,42},{64,72},{65,73},{66,74}... | collective-permute-start | bytes 73736 | tf_op jit(solution)/shard_map/ppermute | solution.py:330
  41.5 3.6 %collective-permute-start.1 = (f32[3,8,256]{2,1,0:T(8,128)S(1)}, f32[3,8,256]{2,1,0:T(8,128)S(1)}, u32[]{:S(2)}, u32[]{:S(2)}) collective-permute-start(f32[3,8,256]{2,1,0:T(8,128)S(1)} %get-tuple-element.20), channel_id=1, source_target_pairs={{0,16},{1,17},{2,18},{32,48},{33,49},{34,50},{64,80},{65,81},{66,8... | collective-permute-start | bytes 73736 | tf_op jit(solution)/shard_map/ppermute | solution.py:330
  43.8 2.2 %collective-permute-start.2 = (f32[3,8,256]{2,1,0:T(8,128)S(1)}, f32[3,8,256]{2,1,0:T(8,128)S(1)}, u32[]{:S(2)}, u32[]{:S(2)}) collective-permute-start(f32[3,8,256]{2,1,0:T(8,128)S(1)} %get-tuple-element.21), channel_id=1, source_target_pairs={{0,24},{1,25},{2,26},{32,56},{33,57},{34,58},{64,88},{65,89},{66,9... | collective-permute-start | bytes 73736 | tf_op jit(solution)/shard_map/ppermute | solution.py:330
  46.1 5.1 %collective-permute-start.3 = (f32[3,8,256]{2,1,0:T(8,128)S(1)}, f32[3,8,256]{2,1,0:T(8,128)S(1)}, u32[]{:S(2)}, u32[]{:S(2)}) collective-permute-start(f32[3,8,256]{2,1,0:T(8,128)S(1)} %fusion.5), channel_id=1, source_target_pairs={{0,4},{1,5},{2,6},{8,12},{9,13},{10,14},{16,20},{17,21},{18,22},{2... | collective-permute-start | bytes 73736 | tf_op jit(solution)/shard_map/ppermute | solution.py:333
  51.1 7.3 %collective-permute-start.6 = (f32[3,8,256]{2,1,0:T(8,128)S(1)}, f32[3,8,256]{2,1,0:T(8,128)S(1)}, u32[]{:S(2)}, u32[]{:S(2)}) collective-permute-start(f32[3,8,256]{2,1,0:T(8,128)S(1)} %add.33), channel_id=1, source_target_pairs={{0,3},{1,0},{2,1},{4,7},{5,4},{6,5},{8,11},{9,8},{10,9},{12,15},{1... | collective-permute-start | bytes 73736 | tf_op jit(solution)/shard_map/ppermute | solution.py:339
  53.1 5.4 %collective-permute-start.5 = (f32[3,8,256]{2,1,0:T(8,128)S(1)}, f32[3,8,256]{2,1,0:T(8,128)S(1)}, u32[]{:S(2)}, u32[]{:S(2)}) collective-permute-start(f32[3,8,256]{2,1,0:T(8,128)S(1)} %add.33), channel_id=1, source_target_pairs={{0,1},{1,2},{2,3},{4,5},{5,6},{6,7},{8,9},{9,10},{10,11},{12,13},{... | collective-permute-start | bytes 73736 | tf_op jit(solution)/shard_map/ppermute | solution.py:339
  56.4 5.6 %collective-permute-start.4 = (f32[3,8,256]{2,1,0:T(8,128)S(1)}, f32[3,8,256]{2,1,0:T(8,128)S(1)}, u32[]{:S(2)}, u32[]{:S(2)}) collective-permute-start(f32[3,8,256]{2,1,0:T(8,128)S(1)} %add.33), channel_id=1, source_target_pairs={{0,2},{1,3},{2,0},{4,6},{5,7},{6,4},{8,10},{9,11},{10,8},{12,14},{... | collective-permute-start | bytes 73736 | tf_op jit(solution)/shard_map/ppermute | solution.py:339
  62.1 7.7 %collective-permute-start.9 = (f32[6,8,256]{2,1,0:T(8,128)S(1)}, f32[6,8,256]{2,1,0:T(8,128)S(1)}, u32[]{:S(2)}, u32[]{:S(2)}) collective-permute-start(f32[6,8,256]{2,1,0:T(8,128)S(1)} %slice_dynamic-update-slice_fusion), channel_id=1, source_target_pairs={{0,24},{1,25},{2,26},{3,27},{4,28},{5,29},{6,30},{7,31},{8,0},{9,1... | collective-permute-start | bytes 147464 | tf_op jit(solution)/shard_map/ppermute | solution.py:350
  65.2 4.6 %collective-permute-start.8 = (f32[6,8,256]{2,1,0:T(8,128)S(1)}, f32[6,8,256]{2,1,0:T(8,128)S(1)}, u32[]{:S(2)}, u32[]{:S(2)}) collective-permute-start(f32[6,8,256]{2,1,0:T(8,128)S(1)} %slice_dynamic-update-slice_fusion), channel_id=1, source_target_pairs={{0,16},{1,17},{2,18},{3,19},{4,20},{5,21},{6,22},{7,23},{8,24},{9,... | collective-permute-start | bytes 147464 | tf_op jit(solution)/shard_map/ppermute | solution.py:350
  65.5 5.2 %collective-permute-start.7 = (f32[6,8,256]{2,1,0:T(8,128)S(1)}, f32[6,8,256]{2,1,0:T(8,128)S(1)}, u32[]{:S(2)}, u32[]{:S(2)}) collective-permute-start(f32[6,8,256]{2,1,0:T(8,128)S(1)} %slice_dynamic-update-slice_fusion), channel_id=1, source_target_pairs={{0,8},{1,9},{2,10},{3,11},{4,12},{5,13},{6,14},{7,15},{8,16},{9,17... | collective-permute-start | bytes 147464 | tf_op jit(solution)/shard_map/ppermute | solution.py:350
  66.2 9.6 %collective-permute-start.23 = (f32[3,32,512]{2,1,0:T(8,128)S(1)}, f32[3,32,512]{2,1,0:T(8,128)S(1)}, u32[]{:S(2)}, u32[]{:S(2)}) collective-permute-start(f32[3,32,512]{2,1,0:T(8,128)S(1)} %slice.64.refs_0_), channel_id=1, source_target_pairs={{0,224},{32,192},{64,32},{96,0},{128,96},{160,64},{192,160},{224,1... | collective-permute-start | bytes 589832 | tf_op jit(solution)/shard_map/ppermute | solution.py:364
  70.7 10.0 %collective-permute-start.12 = (f32[4,6,8,256]{3,2,1,0:T(8,128)S(1)}, f32[4,6,8,256]{3,2,1,0:T(8,128)S(1)}, u32[]{:S(2)}, u32[]{:S(2)}) collective-permute-start(f32[4,6,8,256]{3,2,1,0:T(8,128)S(1)} %pad_maximum_fusion.refs_0_), channel_id=1, source_target_pairs={{0,192},{32,224},{64,0},{96,32},{128,64},{160,96},{192,128},{224,1... | collective-permute-start | bytes 589832 | tf_op jit(solution)/shard_map/ppermute | solution.py:354
  71.1 12.4 %collective-permute-start.11 = (f32[4,6,8,256]{3,2,1,0:T(8,128)S(1)}, f32[4,6,8,256]{3,2,1,0:T(8,128)S(1)}, u32[]{:S(2)}, u32[]{:S(2)}) collective-permute-start(f32[4,6,8,256]{3,2,1,0:T(8,128)S(1)} %pad_maximum_fusion.refs_0_), channel_id=1, source_target_pairs={{0,128},{32,160},{64,192},{96,224},{128,0},{160,32},{192,64},{224,... | collective-permute-start | bytes 589832 | tf_op jit(solution)/shard_map/ppermute | solution.py:354
  73.1 10.4 %collective-permute-start.10 = (f32[4,6,8,256]{3,2,1,0:T(8,128)S(1)}, f32[4,6,8,256]{3,2,1,0:T(8,128)S(1)}, u32[]{:S(2)}, u32[]{:S(2)}) collective-permute-start(f32[4,6,8,256]{3,2,1,0:T(8,128)S(1)} %pad_maximum_fusion.refs_0_), channel_id=1, source_target_pairs={{0,64},{32,96},{64,128},{96,160},{128,192},{160,224},{192,0},{224,... | collective-permute-start | bytes 589832 | tf_op jit(solution)/shard_map/ppermute | solution.py:354
  73.2 13.8 %collective-permute-start.22 = (f32[3,32,512]{2,1,0:T(8,128)S(1)}, f32[3,32,512]{2,1,0:T(8,128)S(1)}, u32[]{:S(2)}, u32[]{:S(2)}) collective-permute-start(f32[3,32,512]{2,1,0:T(8,128)S(1)} %slice.64.refs_0_), channel_id=1, source_target_pairs={{0,192},{32,224},{64,0},{96,32},{128,64},{160,96},{192,128},{224,1... | collective-permute-start | bytes 589832 | tf_op jit(solution)/shard_map/ppermute | solution.py:364
  75.8 12.0 %collective-permute-start.13 = (f32[4,6,8,256]{3,2,1,0:T(8,128)S(1)}, f32[4,6,8,256]{3,2,1,0:T(8,128)S(1)}, u32[]{:S(2)}, u32[]{:S(2)}) collective-permute-start(f32[4,6,8,256]{3,2,1,0:T(8,128)S(1)} %pad_maximum_fusion.refs_0_), channel_id=1, source_target_pairs={{0,32},{32,0},{64,96},{96,64},{128,160},{160,128},{192,224},{224,1... | collective-permute-start | bytes 589832 | tf_op jit(solution)/shard_map/ppermute | solution.py:355
  80.6 11.3 %collective-permute-start.16 = (f32[4,6,8,256]{3,2,1,0:T(8,128)S(1)}, f32[4,6,8,256]{3,2,1,0:T(8,128)S(1)}, u32[]{:S(2)}, u32[]{:S(2)}) collective-permute-start(f32[4,6,8,256]{3,2,1,0:T(8,128)S(1)} %collective-permute-done.12.refs_3_), channel_id=1, source_target_pairs={{0,32},{32,0},{64,96},{96,64},{128,160},{160,128},{192,224},{224,1... | collective-permute-start | bytes 589832 | tf_op jit(solution)/shard_map/ppermute | solution.py:355
  83.6 8.4 %collective-permute-start.15 = (f32[4,6,8,256]{3,2,1,0:T(8,128)S(1)}, f32[4,6,8,256]{3,2,1,0:T(8,128)S(1)}, u32[]{:S(2)}, u32[]{:S(2)}) collective-permute-start(f32[4,6,8,256]{3,2,1,0:T(8,128)S(1)} %collective-permute-done.11.refs_2_), channel_id=1, source_target_pairs={{0,32},{32,0},{64,96},{96,64},{128,160},{160,128},{192,224},{224,1... | collective-permute-start | bytes 589832 | tf_op jit(solution)/shard_map/ppermute | solution.py:355
  83.6 8.6 %collective-permute-start.14 = (f32[4,6,8,256]{3,2,1,0:T(8,128)S(1)}, f32[4,6,8,256]{3,2,1,0:T(8,128)S(1)}, u32[]{:S(2)}, u32[]{:S(2)}) collective-permute-start(f32[4,6,8,256]{3,2,1,0:T(8,128)S(1)} %collective-permute-done.10.refs_1_), channel_id=1, source_target_pairs={{0,32},{32,0},{64,96},{96,64},{128,160},{160,128},{192,224},{224,1... | collective-permute-start | bytes 589832 | tf_op jit(solution)/shard_map/ppermute | solution.py:355
  87.0 35.5 %collective-permute-start.21 = (f32[3,32,512]{2,1,0:T(8,128)S(1)}, f32[3,32,512]{2,1,0:T(8,128)S(1)}, u32[]{:S(2)}, u32[]{:S(2)}) collective-permute-start(f32[3,32,512]{2,1,0:T(8,128)S(1)} %slice.64.refs_0_), channel_id=1, source_target_pairs={{0,160},{32,128},{64,224},{96,192},{128,32},{160,0},{192,96},{224,... | collective-permute-start | bytes 589832 | tf_op jit(solution)/shard_map/ppermute | solution.py:364
  87.9 34.6 %collective-permute-start.20 = (f32[3,32,512]{2,1,0:T(8,128)S(1)}, f32[3,32,512]{2,1,0:T(8,128)S(1)}, u32[]{:S(2)}, u32[]{:S(2)}) collective-permute-start(f32[3,32,512]{2,1,0:T(8,128)S(1)} %slice.64.refs_0_), channel_id=1, source_target_pairs={{0,128},{32,160},{64,192},{96,224},{128,0},{160,32},{192,64},{224,... | collective-permute-start | bytes 589832 | tf_op jit(solution)/shard_map/ppermute | solution.py:364
  91.9 30.5 %collective-permute-start.19 = (f32[3,32,512]{2,1,0:T(8,128)S(1)}, f32[3,32,512]{2,1,0:T(8,128)S(1)}, u32[]{:S(2)}, u32[]{:S(2)}) collective-permute-start(f32[3,32,512]{2,1,0:T(8,128)S(1)} %slice.64.refs_0_), channel_id=1, source_target_pairs={{0,96},{32,64},{64,160},{96,128},{128,224},{160,192},{192,32},{224... | collective-permute-start | bytes 589832 | tf_op jit(solution)/shard_map/ppermute | solution.py:364
  91.9 30.6 %collective-permute-start.18 = (f32[3,32,512]{2,1,0:T(8,128)S(1)}, f32[3,32,512]{2,1,0:T(8,128)S(1)}, u32[]{:S(2)}, u32[]{:S(2)}) collective-permute-start(f32[3,32,512]{2,1,0:T(8,128)S(1)} %slice.64.refs_0_), channel_id=1, source_target_pairs={{0,64},{32,96},{64,128},{96,160},{128,192},{160,224},{192,0},{224,... | collective-permute-start | bytes 589832 | tf_op jit(solution)/shard_map/ppermute | solution.py:364
  92.2 30.3 %collective-permute-start.17 = (f32[3,32,512]{2,1,0:T(8,128)S(1)}, f32[3,32,512]{2,1,0:T(8,128)S(1)}, u32[]{:S(2)}, u32[]{:S(2)}) collective-permute-start(f32[3,32,512]{2,1,0:T(8,128)S(1)} %slice.64.refs_0_), channel_id=1, source_target_pairs={{0,32},{32,0},{64,96},{96,64},{128,160},{160,128},{192,224},{224,1... | collective-permute-start | bytes 589832 | tf_op jit(solution)/shard_map/ppermute | solution.py:364
Sparse Core Ops, SparseCore 0:
  38.4 90.5 all-gather.2

commit v5 on v4

--- a/solution.py
+++ b/solution.py
@@ -111,6 +111,11 @@
                 g_ref[hi + BAND : B, left:right] -= dot(turned[hi + BAND : B], done)
 
 
+def product_tn(a, b):
+    mul = lambda p, q: lax.dot_general(p, q, (((0,), (0,)), ((), ())), preferred_element_type=F32)
+    return mul(a[0], b[0]) + (mul(a[0], b[1]) + mul(a[1], b[0]))
+
+
 def upper_mask():
     return lax.broadcasted_iota(jnp.int32, (B, B), 0) <= lax.broadcasted_iota(jnp.int32, (B, B), 1)
 
@@ -243,23 +248,26 @@
     zhi_ref, zlo_ref, diag_ref, a_hbm, u_hbm, o_hbm, a_ref, u_ref, a_sem, u_sem, o_sem = refs
     my_row, my_col = place_ref[0], place_ref[1]
     panel = my_col < 3
-    u_copies = [pltpu.make_async_copy(u_hbm.at[y], u_ref.at[y], u_sem.at[y]) for y in range(4)]
+    u_copies = []
+    for t in range(8):
+        part = (t % 4, slice(None), pl.ds(t // 4 * B, B))
+        u_copies.append(pltpu.make_async_copy(u_hbm.at[part], u_ref.at[part], u_sem.at[t]))
     a_copies = [pltpu.make_async_copy(a_hbm.at[t], a_ref.at[t], a_sem.at[t]) for t in range(8)]
     o_copies = [pltpu.make_async_copy(a_ref.at[t], o_hbm.at[t], o_sem.at[t]) for t in range(8)]
 
     def fetch(y):
-        u_copies[y].start()
-        a_copies[y].start()
-        a_copies[y + 4].start()
+        for t in (y, y + 4):
+            u_copies[t].start()
+            a_copies[t].start()
 
     fetch(0)
     fetch(1)
     for y in range(4):
-        u_copies[y].wait()
-        if y < 2:
-            fetch(y + 2)
         for t in (y, y + 4):
             i = t * 8 + my_row
+            u_copies[t].wait()
+            if t < 2:
+                fetch(t + 2)
             a_copies[t].wait()
 
             def write(u, change):
@@ -271,10 +279,10 @@
                     a_ref[t, at, :] = base - change[:, half * 128 : half * 128 + 128]
 
             def turned():
-                return split(u_ref[y, :, t // 4 * B : t // 4 * B + B].T)
+                return split(u_ref[y, :, t // 4 * B : t // 4 * B + B])
 
             def left():
-                write(0, product(turned(), (zhi_ref[:, :B], zlo_ref[:, :B])))
+                write(0, product_tn(turned(), (zhi_ref[:, :B], zlo_ref[:, :B])))
 
             if t < 4:
                 pl.when(i >= my_col)(left)
@@ -288,7 +296,7 @@
 
                 @pl.when(both)
                 def _():
-                    change = product(turned(), (zhi_ref[...], zlo_ref[...]))
+                    change = product_tn(turned(), (zhi_ref[...], zlo_ref[...]))
                     write(0, change[:, :B])
                     write(1, change[:, B:])
 
@@ -312,7 +320,7 @@
             pltpu.VMEM((8, 4 * B, 128), F32),
             pltpu.VMEM((4, 3 * B, 2 * B), F32),
             pltpu.SemaphoreType.DMA((8,)),
-            pltpu.SemaphoreType.DMA((4,)),
+            pltpu.SemaphoreType.DMA((8,)),
             pltpu.SemaphoreType.DMA((8,)),
         ],
         compiler_params=pltpu.CompilerParams(vmem_limit_bytes=49 * 2**20),

time: 145 us -> 145 us (level)
  no operation moved by 1% of the time
where the time goes in v5:
time: 145 us; the launch traced here: 144 us
  starting transfers between devices  54.7 us (38%)
  Pallas kernels  42.8 us (30%)
  waiting for transfers between devices  15.4 us (11%)
  blocking collectives  15 us (10%)
  between operations  13.8 us (10%)
  local copies, waits for them, and re-layouts  2.36 us (2%)
    pallas_call x1, Pallas kernels, factor(): pl.pallas_call(factor_kernel, out_shape=(jax.ShapeDtypeStruct((3, B, B),...  30 us
    all_to_all x1, blocking collectives, on_device(): mine = lax.all_to_all(top, 'row', 0, 0, tiled=True)[:3]  15 us
    ppermute x7, starting transfers between devices, spread_columns(): pieces.append(mine if n == 0 else lax.ppermute(mine, 'row', pairs))  11.6 us
    ppermute x1, starting transfers between devices, on_device(): lax.ppermute(mine, ('row', 'col'), [(r * 32 + y * 8 + z, z * 32 + y * 8 +...  9.7 us
    ppermute x4, starting transfers between devices, spread_corner(): lax.ppermute(b, 'row', [(r, r ^ 1) for r in range(8)])  8.64 us
    pallas_call x1, Pallas kernels, update(): pl.pallas_call(update_kernel, out_shape=jax.ShapeDtypeStruct(flat.shape,...  8.34 us
    ppermute x3, starting transfers between devices, spread_corner(): stack.append(lax.ppermute(got, 'col', pairs))  7.19 us
    ppermute x3, starting transfers between devices, spread_corner(): lax.ppermute(quarter[:, d], 'col', [(j, d * 8 + j) for j in range(3)])  6.77 us
  transfers between devices with their start and end apart: 26, of which 7 were waited for; matrix products, arithmetic and copies ran while one was open for 0% of the time, Pallas kernels for 24%

profile of v5, /device:TPU:1, one launch (start us, length us, event | category | flops | bytes accessed | tf_op | source)
XLA Modules:
  0.0 144.2 jit_solution(8953818388985688065)
XLA Ops:
  6.5 0.0 all-gather.3.cloned.1.call-start
  6.5 1.2 slice.39
  7.8 0.4 reshape_squeeze.3
  8.2 15.0 %all_to_all.5 = f32[8,32,512]{2,1,0:T(8,128)S(1)} all-to-all(f32[8,32,512]{2,1,0:T(8,128)S(1)} %reshape_squeeze.3), channel_id=1, replica_groups=mesh['row'=8,'col'=32] {'row'}, dimensions={0} | all-to-all | bytes 1048576 | tf_op jit(solution)/shard_map/all_to_all | solution.py:380
  23.2 9.7 %collective-permute-start.24 = (f32[3,32,512]{2,1,0:T(8,128)S(1)}, f32[3,32,512]{2,1,0:T(8,128)S(1)}, u32[]{:S(2)}, u32[]{:S(2)}) collective-permute-start(f32[3,32,512]{2,1,0:T(8,128)S(1)} %slice.64.refs_0_), channel_id=1, source_target_pairs={{0,0},{1,33},{2,66},{3,99},{4,132},{5,165},{6,198},{7,231},{8,8},{... | collective-permute-start | bytes 589832 | tf_op jit(solution)/shard_map/ppermute | solution.py:382
  32.9 4.7 %collective-permute-done.24 = f32[3,32,512]{2,1,0:T(8,128)S(1)} collective-permute-done((f32[3,32,512]{2,1,0:T(8,128)S(1)}, f32[3,32,512]{2,1,0:T(8,128)S(1)}, u32[]{:S(2)}, u32[]{:S(2)}) %collective-permute-start.24) | collective-permute-done | bytes 196640 | tf_op jit(solution)/shard_map/ppermute | solution.py:382
  37.6 0.0 copy-start
  37.6 0.7 copy-done
  38.3 0.0 all-gather.3.cloned.1.call-update
  38.3 3.2 %collective-permute-start = (f32[3,8,256]{2,1,0:T(8,128)S(1)}, f32[3,8,256]{2,1,0:T(8,128)S(1)}, u32[]{:S(2)}, u32[]{:S(2)}) collective-permute-start(f32[3,8,256]{2,1,0:T(8,128)S(1)} %get-tuple-element.19), channel_id=1, source_target_pairs={{0,8},{1,9},{2,10},{32,40},{33,41},{34,42},{64,72},{65,73},{66,74}... | collective-permute-start | bytes 73736 | tf_op jit(solution)/shard_map/ppermute | solution.py:338
  41.5 2.3 %collective-permute-start.1 = (f32[3,8,256]{2,1,0:T(8,128)S(1)}, f32[3,8,256]{2,1,0:T(8,128)S(1)}, u32[]{:S(2)}, u32[]{:S(2)}) collective-permute-start(f32[3,8,256]{2,1,0:T(8,128)S(1)} %get-tuple-element.20), channel_id=1, source_target_pairs={{0,16},{1,17},{2,18},{32,48},{33,49},{34,50},{64,80},{65,81},{66,8... | collective-permute-start | bytes 73736 | tf_op jit(solution)/shard_map/ppermute | solution.py:338
  43.8 1.3 collective-permute-start.2
  45.1 0.0 collective-permute-done
  45.2 0.0 collective-permute-done.1
  45.2 0.9 collective-permute-done.2
  46.1 4.1 %collective-permute-start.3 = (f32[3,8,256]{2,1,0:T(8,128)S(1)}, f32[3,8,256]{2,1,0:T(8,128)S(1)}, u32[]{:S(2)}, u32[]{:S(2)}) collective-permute-start(f32[3,8,256]{2,1,0:T(8,128)S(1)} %fusion.5), channel_id=1, source_target_pairs={{0,4},{1,5},{2,6},{8,12},{9,13},{10,14},{16,20},{17,21},{18,22},{2... | collective-permute-start | bytes 73736 | tf_op jit(solution)/shard_map/ppermute | solution.py:341
  50.2 0.9 collective-permute-done.3
  51.1 1.9 %collective-permute-start.6 = (f32[3,8,256]{2,1,0:T(8,128)S(1)}, f32[3,8,256]{2,1,0:T(8,128)S(1)}, u32[]{:S(2)}, u32[]{:S(2)}) collective-permute-start(f32[3,8,256]{2,1,0:T(8,128)S(1)} %add.33), channel_id=1, source_target_pairs={{0,3},{1,0},{2,1},{4,7},{5,4},{6,5},{8,11},{9,8},{10,9},{12,15},{1... | collective-permute-start | bytes 73736 | tf_op jit(solution)/shard_map/ppermute | solution.py:347
  53.1 3.4 %collective-permute-start.5 = (f32[3,8,256]{2,1,0:T(8,128)S(1)}, f32[3,8,256]{2,1,0:T(8,128)S(1)}, u32[]{:S(2)}, u32[]{:S(2)}) collective-permute-start(f32[3,8,256]{2,1,0:T(8,128)S(1)} %add.33), channel_id=1, source_target_pairs={{0,1},{1,2},{2,3},{4,5},{5,6},{6,7},{8,9},{9,10},{10,11},{12,13},{... | collective-permute-start | bytes 73736 | tf_op jit(solution)/shard_map/ppermute | solution.py:347
  56.4 1.9 %collective-permute-start.4 = (f32[3,8,256]{2,1,0:T(8,128)S(1)}, f32[3,8,256]{2,1,0:T(8,128)S(1)}, u32[]{:S(2)}, u32[]{:S(2)}) collective-permute-start(f32[3,8,256]{2,1,0:T(8,128)S(1)} %add.33), channel_id=1, source_target_pairs={{0,2},{1,3},{2,0},{4,6},{5,7},{6,4},{8,10},{9,11},{10,8},{12,14},{... | collective-permute-start | bytes 73736 | tf_op jit(solution)/shard_map/ppermute | solution.py:347
  58.4 0.0 collective-permute-done.6
  58.4 0.0 collective-permute-done.5
  58.4 3.5 %collective-permute-done.4 = f32[3,8,256]{2,1,0:T(8,128)S(1)} collective-permute-done((f32[3,8,256]{2,1,0:T(8,128)S(1)}, f32[3,8,256]{2,1,0:T(8,128)S(1)}, u32[]{:S(2)}, u32[]{:S(2)}) %collective-permute-start.4) | collective-permute-done | bytes 24608 | tf_op jit(solution)/shard_map/ppermute | solution.py:347
  62.1 3.1 %collective-permute-start.9 = (f32[6,8,256]{2,1,0:T(8,128)S(1)}, f32[6,8,256]{2,1,0:T(8,128)S(1)}, u32[]{:S(2)}, u32[]{:S(2)}) collective-permute-start(f32[6,8,256]{2,1,0:T(8,128)S(1)} %slice_dynamic-update-slice_fusion), channel_id=1, source_target_pairs={{0,24},{1,25},{2,26},{3,27},{4,28},{5,29},{6,30},{7,31},{8,0},{9,1... | collective-permute-start | bytes 147464 | tf_op jit(solution)/shard_map/ppermute | solution.py:358
  65.2 0.3 collective-permute-start.8
  65.5 0.7 collective-permute-start.7
  66.2 3.6 %collective-permute-start.23 = (f32[3,32,512]{2,1,0:T(8,128)S(1)}, f32[3,32,512]{2,1,0:T(8,128)S(1)}, u32[]{:S(2)}, u32[]{:S(2)}) collective-permute-start(f32[3,32,512]{2,1,0:T(8,128)S(1)} %slice.64.refs_0_), channel_id=1, source_target_pairs={{0,224},{32,192},{64,32},{96,0},{128,96},{160,64},{192,160},{224,1... | collective-permute-start | bytes 589832 | tf_op jit(solution)/shard_map/ppermute | solution.py:372
  69.8 0.0 collective-permute-done.9
  69.8 0.0 collective-permute-done.8
  69.8 0.9 collective-permute-done.7
  70.7 0.4 collective-permute-start.12
  71.1 2.0 %collective-permute-start.11 = (f32[4,6,8,256]{3,2,1,0:T(8,128)S(1)}, f32[4,6,8,256]{3,2,1,0:T(8,128)S(1)}, u32[]{:S(2)}, u32[]{:S(2)}) collective-permute-start(f32[4,6,8,256]{3,2,1,0:T(8,128)S(1)} %pad_maximum_fusion.refs_0_), channel_id=1, source_target_pairs={{0,128},{32,160},{64,192},{96,224},{128,0},{160,32},{192,64},{224,... | collective-permute-start | bytes 589832 | tf_op jit(solution)/shard_map/ppermute | solution.py:362
  73.1 0.0 collective-permute-start.10
  73.2 2.7 %collective-permute-start.22 = (f32[3,32,512]{2,1,0:T(8,128)S(1)}, f32[3,32,512]{2,1,0:T(8,128)S(1)}, u32[]{:S(2)}, u32[]{:S(2)}) collective-permute-start(f32[3,32,512]{2,1,0:T(8,128)S(1)} %slice.64.refs_0_), channel_id=1, source_target_pairs={{0,192},{32,224},{64,0},{96,32},{128,64},{160,96},{192,128},{224,1... | collective-permute-start | bytes 589832 | tf_op jit(solution)/shard_map/ppermute | solution.py:372
  75.8 0.0 collective-permute-done.23.refs_7_
  75.8 4.8 %collective-permute-start.13 = (f32[4,6,8,256]{3,2,1,0:T(8,128)S(1)}, f32[4,6,8,256]{3,2,1,0:T(8,128)S(1)}, u32[]{:S(2)}, u32[]{:S(2)}) collective-permute-start(f32[4,6,8,256]{3,2,1,0:T(8,128)S(1)} %pad_maximum_fusion.refs_0_), channel_id=1, source_target_pairs={{0,32},{32,0},{64,96},{96,64},{128,160},{160,128},{192,224},{224,1... | collective-permute-start | bytes 589832 | tf_op jit(solution)/shard_map/ppermute | solution.py:363
  80.6 0.0 collective-permute-done.12.refs_3_
  80.6 2.9 %collective-permute-start.16 = (f32[4,6,8,256]{3,2,1,0:T(8,128)S(1)}, f32[4,6,8,256]{3,2,1,0:T(8,128)S(1)}, u32[]{:S(2)}, u32[]{:S(2)}) collective-permute-start(f32[4,6,8,256]{3,2,1,0:T(8,128)S(1)} %collective-permute-done.12.refs_3_), channel_id=1, source_target_pairs={{0,32},{32,0},{64,96},{96,64},{128,160},{160,128},{192,224},{224,1... | collective-permute-start | bytes 589832 | tf_op jit(solution)/shard_map/ppermute | solution.py:363
  83.6 0.0 collective-permute-done.11.refs_2_
  83.6 0.0 collective-permute-start.15
  83.6 0.0 collective-permute-done.10.refs_1_
  83.6 0.9 collective-permute-start.14
  84.5 0.1 pad_add_fusion.place_ref
  84.6 2.4 %collective-permute-done.22.refs_6_ = f32[3,32,512]{2,1,0:T(8,128)S(1)} collective-permute-done((f32[3,32,512]{2,1,0:T(8,128)S(1)}, f32[3,32,512]{2,1,0:T(8,128)S(1)}, u32[]{:S(2)}, u32[]{:S(2)}) %collective-permute-start.22) | collective-permute-done | bytes 196640 | tf_op jit(solution)/shard_map/ppermute | solution.py:372
  87.0 0.9 collective-permute-start.21
  87.9 0.0 collective-permute-done.13.refs_4_
  87.9 4.0 %collective-permute-start.20 = (f32[3,32,512]{2,1,0:T(8,128)S(1)}, f32[3,32,512]{2,1,0:T(8,128)S(1)}, u32[]{:S(2)}, u32[]{:S(2)}) collective-permute-start(f32[3,32,512]{2,1,0:T(8,128)S(1)} %slice.64.refs_0_), channel_id=1, source_target_pairs={{0,128},{32,160},{64,192},{96,224},{128,0},{160,32},{192,64},{224,... | collective-permute-start | bytes 589832 | tf_op jit(solution)/shard_map/ppermute | solution.py:372
  91.9 0.0 collective-permute-done.16.refs_7_
  91.9 0.0 collective-permute-start.19
  91.9 0.0 collective-permute-done.15.refs_6_
  91.9 0.3 collective-permute-start.18
  92.2 0.0 collective-permute-done.14.refs_5_
  92.2 0.2 collective-permute-start.17
  92.4 30.0 %factor_corner.1 = (f32[3,256,256]{2,1,0:T(8,128)S(1)}, f32[3,256,256]{2,1,0:T(8,128)S(1)}, f32[256,256]{1,0:T(8,128)S(1)}) custom-call(s32[2]{0:T(128)S(1)} %pad_add_fusion.place_ref, f32[4,6,8,256]{3,2,1,0:T(8,128)S(1)} %pad_maximum_fusion.refs_0_, f32[4,6,8,256]{3,2,1,0:T(8,128)S(1)} %collective-permute-done.10.refs_1_, ...), custom_call_target="tpu_custom_call" | custom-call | flops 30000001024 | bytes 10000000 | tf_op jit(solution)/shard_map/factor_corner/pallas_call | solution.py:175
  122.4 0.0 collective-permute-done.21.refs_5_
  122.4 0.0 collective-permute-done.20.refs_4_
  122.5 0.0 collective-permute-done.19.refs_3_
  122.5 0.0 collective-permute-done.18.refs_2_
  122.5 0.0 collective-permute-done.17.refs_1_
  122.5 4.5 %solve_columns.1 = (bf16[768,512]{1,0:T(8,128)(2,1)S(1)}, bf16[768,512]{1,0:T(8,128)(2,1)S(1)}) custom-call(s32[2]{0:T(128)S(1)} %pad_add_fusion.place_ref, f32[3,256,256]{2,1,0:T(8,128)S(1)} %get-tuple-element.11.v_ref, f32[3,256,256]{2,1,0:T(8,128)S(1)} %get-tuple-element.12.x_ref, f32[3,32,512]{2,1,0:T(8,128)S(1)} %slice.64.refs_0_, ...), custom_call_target="tpu_custom_call" | custom-call | flops 3000000000 | bytes 10000000 | tf_op jit(solution)/shard_map/solve_columns/pallas_call | solution.py:232
  127.0 2.0 %all-gather.3.cloned.1.call-done = f32[96,32,512]{2,1,0:T(8,128)} async-done(((f32[3,32,512]{2,1,0:T(8,128)}), f32[96,32,512]{2,1,0:T(8,128)}) %all-gather.3.cloned.1.call-update) | async-done | bytes 6291472 | tf_op jit(solution)/shard_map/all_gather | solution.py:385
  129.0 8.3 %trailing_update.1 = f32[8,1024,128]{2,1,0:T(8,128)} custom-call(s32[2]{0:T(128)S(1)} %pad_add_fusion.place_ref, bf16[768,512]{1,0:T(8,128)(2,1)S(1)} %get-tuple-element.14.refs_0_, bf16[768,512]{1,0:T(8,128)(2,1)S(1)} %get-tuple-element.15.refs_1_, f32[256,256]{1,0:T(8,128)S(1)} %get-tuple-element.16.refs_2_, f32[8,1024,128]{2,1,0:T(8,128)} %bitcast.56, ...), custom_call_target="tpu_custom_call" | custom-call | flops 5000000000 | bytes 14000000 | tf_op jit(solution)/shard_map/trailing_update/pallas_call | solution.py:314
  (12 shorter events, 0.1 us)
Async XLA Ops:
  6.5 122.4 %all-gather.3.cloned.1.call-start = ((), (), s32[]{:S(2)}) async-start(), calls=%async_computation.1 | async-start | bytes 6488064 | tf_op jit(solution)/shard_map/all_gather | solution.py:385
  23.2 14.4 %collective-permute-start.24 = (f32[3,32,512]{2,1,0:T(8,128)S(1)}, f32[3,32,512]{2,1,0:T(8,128)S(1)}, u32[]{:S(2)}, u32[]{:S(2)}) collective-permute-start(f32[3,32,512]{2,1,0:T(8,128)S(1)} %slice.64.refs_0_), channel_id=1, source_target_pairs={{0,0},{1,33},{2,66},{3,99},{4,132},{5,165},{6,198},{7,231},{8,8},{... | collective-permute-start | bytes 589832 | tf_op jit(solution)/shard_map/ppermute | solution.py:382
  37.6 0.7 copy-start
  38.3 6.8 %collective-permute-start = (f32[3,8,256]{2,1,0:T(8,128)S(1)}, f32[3,8,256]{2,1,0:T(8,128)S(1)}, u32[]{:S(2)}, u32[]{:S(2)}) collective-permute-start(f32[3,8,256]{2,1,0:T(8,128)S(1)} %get-tuple-element.19), channel_id=1, source_target_pairs={{0,8},{1,9},{2,10},{32,40},{33,41},{34,42},{64,72},{65,73},{66,74}... | collective-permute-start | bytes 73736 | tf_op jit(solution)/shard_map/ppermute | solution.py:338
  41.5 3.6 %collective-permute-start.1 = (f32[3,8,256]{2,1,0:T(8,128)S(1)}, f32[3,8,256]{2,1,0:T(8,128)S(1)}, u32[]{:S(2)}, u32[]{:S(2)}) collective-permute-start(f32[3,8,256]{2,1,0:T(8,128)S(1)} %get-tuple-element.20), channel_id=1, source_target_pairs={{0,16},{1,17},{2,18},{32,48},{33,49},{34,50},{64,80},{65,81},{66,8... | collective-permute-start | bytes 73736 | tf_op jit(solution)/shard_map/ppermute | solution.py:338
  43.8 2.2 %collective-permute-start.2 = (f32[3,8,256]{2,1,0:T(8,128)S(1)}, f32[3,8,256]{2,1,0:T(8,128)S(1)}, u32[]{:S(2)}, u32[]{:S(2)}) collective-permute-start(f32[3,8,256]{2,1,0:T(8,128)S(1)} %get-tuple-element.21), channel_id=1, source_target_pairs={{0,24},{1,25},{2,26},{32,56},{33,57},{34,58},{64,88},{65,89},{66,9... | collective-permute-start | bytes 73736 | tf_op jit(solution)/shard_map/ppermute | solution.py:338
  46.1 5.1 %collective-permute-start.3 = (f32[3,8,256]{2,1,0:T(8,128)S(1)}, f32[3,8,256]{2,1,0:T(8,128)S(1)}, u32[]{:S(2)}, u32[]{:S(2)}) collective-permute-start(f32[3,8,256]{2,1,0:T(8,128)S(1)} %fusion.5), channel_id=1, source_target_pairs={{0,4},{1,5},{2,6},{8,12},{9,13},{10,14},{16,20},{17,21},{18,22},{2... | collective-permute-start | bytes 73736 | tf_op jit(solution)/shard_map/ppermute | solution.py:341
  51.1 7.3 %collective-permute-start.6 = (f32[3,8,256]{2,1,0:T(8,128)S(1)}, f32[3,8,256]{2,1,0:T(8,128)S(1)}, u32[]{:S(2)}, u32[]{:S(2)}) collective-permute-start(f32[3,8,256]{2,1,0:T(8,128)S(1)} %add.33), channel_id=1, source_target_pairs={{0,3},{1,0},{2,1},{4,7},{5,4},{6,5},{8,11},{9,8},{10,9},{12,15},{1... | collective-permute-start | bytes 73736 | tf_op jit(solution)/shard_map/ppermute | solution.py:347
  53.1 5.4 %collective-permute-start.5 = (f32[3,8,256]{2,1,0:T(8,128)S(1)}, f32[3,8,256]{2,1,0:T(8,128)S(1)}, u32[]{:S(2)}, u32[]{:S(2)}) collective-permute-start(f32[3,8,256]{2,1,0:T(8,128)S(1)} %add.33), channel_id=1, source_target_pairs={{0,1},{1,2},{2,3},{4,5},{5,6},{6,7},{8,9},{9,10},{10,11},{12,13},{... | collective-permute-start | bytes 73736 | tf_op jit(solution)/shard_map/ppermute | solution.py:347
  56.4 5.6 %collective-permute-start.4 = (f32[3,8,256]{2,1,0:T(8,128)S(1)}, f32[3,8,256]{2,1,0:T(8,128)S(1)}, u32[]{:S(2)}, u32[]{:S(2)}) collective-permute-start(f32[3,8,256]{2,1,0:T(8,128)S(1)} %add.33), channel_id=1, source_target_pairs={{0,2},{1,3},{2,0},{4,6},{5,7},{6,4},{8,10},{9,11},{10,8},{12,14},{... | collective-permute-start | bytes 73736 | tf_op jit(solution)/shard_map/ppermute | solution.py:347
  62.1 7.7 %collective-permute-start.9 = (f32[6,8,256]{2,1,0:T(8,128)S(1)}, f32[6,8,256]{2,1,0:T(8,128)S(1)}, u32[]{:S(2)}, u32[]{:S(2)}) collective-permute-start(f32[6,8,256]{2,1,0:T(8,128)S(1)} %slice_dynamic-update-slice_fusion), channel_id=1, source_target_pairs={{0,24},{1,25},{2,26},{3,27},{4,28},{5,29},{6,30},{7,31},{8,0},{9,1... | collective-permute-start | bytes 147464 | tf_op jit(solution)/shard_map/ppermute | solution.py:358
  65.2 4.6 %collective-permute-start.8 = (f32[6,8,256]{2,1,0:T(8,128)S(1)}, f32[6,8,256]{2,1,0:T(8,128)S(1)}, u32[]{:S(2)}, u32[]{:S(2)}) collective-permute-start(f32[6,8,256]{2,1,0:T(8,128)S(1)} %slice_dynamic-update-slice_fusion), channel_id=1, source_target_pairs={{0,16},{1,17},{2,18},{3,19},{4,20},{5,21},{6,22},{7,23},{8,24},{9,... | collective-permute-start | bytes 147464 | tf_op jit(solution)/shard_map/ppermute | solution.py:358
  65.5 5.2 %collective-permute-start.7 = (f32[6,8,256]{2,1,0:T(8,128)S(1)}, f32[6,8,256]{2,1,0:T(8,128)S(1)}, u32[]{:S(2)}, u32[]{:S(2)}) collective-permute-start(f32[6,8,256]{2,1,0:T(8,128)S(1)} %slice_dynamic-update-slice_fusion), channel_id=1, source_target_pairs={{0,8},{1,9},{2,10},{3,11},{4,12},{5,13},{6,14},{7,15},{8,16},{9,17... | collective-permute-start | bytes 147464 | tf_op jit(solution)/shard_map/ppermute | solution.py:358
  66.2 9.6 %collective-permute-start.23 = (f32[3,32,512]{2,1,0:T(8,128)S(1)}, f32[3,32,512]{2,1,0:T(8,128)S(1)}, u32[]{:S(2)}, u32[]{:S(2)}) collective-permute-start(f32[3,32,512]{2,1,0:T(8,128)S(1)} %slice.64.refs_0_), channel_id=1, source_target_pairs={{0,224},{32,192},{64,32},{96,0},{128,96},{160,64},{192,160},{224,1... | collective-permute-start | bytes 589832 | tf_op jit(solution)/shard_map/ppermute | solution.py:372
  70.7 10.0 %collective-permute-start.12 = (f32[4,6,8,256]{3,2,1,0:T(8,128)S(1)}, f32[4,6,8,256]{3,2,1,0:T(8,128)S(1)}, u32[]{:S(2)}, u32[]{:S(2)}) collective-permute-start(f32[4,6,8,256]{3,2,1,0:T(8,128)S(1)} %pad_maximum_fusion.refs_0_), channel_id=1, source_target_pairs={{0,192},{32,224},{64,0},{96,32},{128,64},{160,96},{192,128},{224,1... | collective-permute-start | bytes 589832 | tf_op jit(solution)/shard_map/ppermute | solution.py:362
  71.1 12.4 %collective-permute-start.11 = (f32[4,6,8,256]{3,2,1,0:T(8,128)S(1)}, f32[4,6,8,256]{3,2,1,0:T(8,128)S(1)}, u32[]{:S(2)}, u32[]{:S(2)}) collective-permute-start(f32[4,6,8,256]{3,2,1,0:T(8,128)S(1)} %pad_maximum_fusion.refs_0_), channel_id=1, source_target_pairs={{0,128},{32,160},{64,192},{96,224},{128,0},{160,32},{192,64},{224,... | collective-permute-start | bytes 589832 | tf_op jit(solution)/shard_map/ppermute | solution.py:362
  73.1 10.4 %collective-permute-start.10 = (f32[4,6,8,256]{3,2,1,0:T(8,128)S(1)}, f32[4,6,8,256]{3,2,1,0:T(8,128)S(1)}, u32[]{:S(2)}, u32[]{:S(2)}) collective-permute-start(f32[4,6,8,256]{3,2,1,0:T(8,128)S(1)} %pad_maximum_fusion.refs_0_), channel_id=1, source_target_pairs={{0,64},{32,96},{64,128},{96,160},{128,192},{160,224},{192,0},{224,... | collective-permute-start | bytes 589832 | tf_op jit(solution)/shard_map/ppermute | solution.py:362
  73.2 13.8 %collective-permute-start.22 = (f32[3,32,512]{2,1,0:T(8,128)S(1)}, f32[3,32,512]{2,1,0:T(8,128)S(1)}, u32[]{:S(2)}, u32[]{:S(2)}) collective-permute-start(f32[3,32,512]{2,1,0:T(8,128)S(1)} %slice.64.refs_0_), channel_id=1, source_target_pairs={{0,192},{32,224},{64,0},{96,32},{128,64},{160,96},{192,128},{224,1... | collective-permute-start | bytes 589832 | tf_op jit(solution)/shard_map/ppermute | solution.py:372
  75.8 12.0 %collective-permute-start.13 = (f32[4,6,8,256]{3,2,1,0:T(8,128)S(1)}, f32[4,6,8,256]{3,2,1,0:T(8,128)S(1)}, u32[]{:S(2)}, u32[]{:S(2)}) collective-permute-start(f32[4,6,8,256]{3,2,1,0:T(8,128)S(1)} %pad_maximum_fusion.refs_0_), channel_id=1, source_target_pairs={{0,32},{32,0},{64,96},{96,64},{128,160},{160,128},{192,224},{224,1... | collective-permute-start | bytes 589832 | tf_op jit(solution)/shard_map/ppermute | solution.py:363
  80.6 11.3 %collective-permute-start.16 = (f32[4,6,8,256]{3,2,1,0:T(8,128)S(1)}, f32[4,6,8,256]{3,2,1,0:T(8,128)S(1)}, u32[]{:S(2)}, u32[]{:S(2)}) collective-permute-start(f32[4,6,8,256]{3,2,1,0:T(8,128)S(1)} %collective-permute-done.12.refs_3_), channel_id=1, source_target_pairs={{0,32},{32,0},{64,96},{96,64},{128,160},{160,128},{192,224},{224,1... | collective-permute-start | bytes 589832 | tf_op jit(solution)/shard_map/ppermute | solution.py:363
  83.6 8.4 %collective-permute-start.15 = (f32[4,6,8,256]{3,2,1,0:T(8,128)S(1)}, f32[4,6,8,256]{3,2,1,0:T(8,128)S(1)}, u32[]{:S(2)}, u32[]{:S(2)}) collective-permute-start(f32[4,6,8,256]{3,2,1,0:T(8,128)S(1)} %collective-permute-done.11.refs_2_), channel_id=1, source_target_pairs={{0,32},{32,0},{64,96},{96,64},{128,160},{160,128},{192,224},{224,1... | collective-permute-start | bytes 589832 | tf_op jit(solution)/shard_map/ppermute | solution.py:363
  83.6 8.6 %collective-permute-start.14 = (f32[4,6,8,256]{3,2,1,0:T(8,128)S(1)}, f32[4,6,8,256]{3,2,1,0:T(8,128)S(1)}, u32[]{:S(2)}, u32[]{:S(2)}) collective-permute-start(f32[4,6,8,256]{3,2,1,0:T(8,128)S(1)} %collective-permute-done.10.refs_1_), channel_id=1, source_target_pairs={{0,32},{32,0},{64,96},{96,64},{128,160},{160,128},{192,224},{224,1... | collective-permute-start | bytes 589832 | tf_op jit(solution)/shard_map/ppermute | solution.py:363
  87.0 35.5 %collective-permute-start.21 = (f32[3,32,512]{2,1,0:T(8,128)S(1)}, f32[3,32,512]{2,1,0:T(8,128)S(1)}, u32[]{:S(2)}, u32[]{:S(2)}) collective-permute-start(f32[3,32,512]{2,1,0:T(8,128)S(1)} %slice.64.refs_0_), channel_id=1, source_target_pairs={{0,160},{32,128},{64,224},{96,192},{128,32},{160,0},{192,96},{224,... | collective-permute-start | bytes 589832 | tf_op jit(solution)/shard_map/ppermute | solution.py:372
  87.9 34.6 %collective-permute-start.20 = (f32[3,32,512]{2,1,0:T(8,128)S(1)}, f32[3,32,512]{2,1,0:T(8,128)S(1)}, u32[]{:S(2)}, u32[]{:S(2)}) collective-permute-start(f32[3,32,512]{2,1,0:T(8,128)S(1)} %slice.64.refs_0_), channel_id=1, source_target_pairs={{0,128},{32,160},{64,192},{96,224},{128,0},{160,32},{192,64},{224,... | collective-permute-start | bytes 589832 | tf_op jit(solution)/shard_map/ppermute | solution.py:372
  91.9 30.5 %collective-permute-start.19 = (f32[3,32,512]{2,1,0:T(8,128)S(1)}, f32[3,32,512]{2,1,0:T(8,128)S(1)}, u32[]{:S(2)}, u32[]{:S(2)}) collective-permute-start(f32[3,32,512]{2,1,0:T(8,128)S(1)} %slice.64.refs_0_), channel_id=1, source_target_pairs={{0,96},{32,64},{64,160},{96,128},{128,224},{160,192},{192,32},{224... | collective-permute-start | bytes 589832 | tf_op jit(solution)/shard_map/ppermute | solution.py:372
  91.9 30.6 %collective-permute-start.18 = (f32[3,32,512]{2,1,0:T(8,128)S(1)}, f32[3,32,512]{2,1,0:T(8,128)S(1)}, u32[]{:S(2)}, u32[]{:S(2)}) collective-permute-start(f32[3,32,512]{2,1,0:T(8,128)S(1)} %slice.64.refs_0_), channel_id=1, source_target_pairs={{0,64},{32,96},{64,128},{96,160},{128,192},{160,224},{192,0},{224,... | collective-permute-start | bytes 589832 | tf_op jit(solution)/shard_map/ppermute | solution.py:372
  92.2 30.3 %collective-permute-start.17 = (f32[3,32,512]{2,1,0:T(8,128)S(1)}, f32[3,32,512]{2,1,0:T(8,128)S(1)}, u32[]{:S(2)}, u32[]{:S(2)}) collective-permute-start(f32[3,32,512]{2,1,0:T(8,128)S(1)} %slice.64.refs_0_), channel_id=1, source_target_pairs={{0,32},{32,0},{64,96},{96,64},{128,160},{160,128},{192,224},{224,1... | collective-permute-start | bytes 589832 | tf_op jit(solution)/shard_map/ppermute | solution.py:372
Sparse Core Ops, SparseCore 0:
  38.4 90.5 all-gather.2
